TPU v7x, 32 devices: a whole 2x2x4 slice. The times are simulated.
32 devices in a mesh: dp: 8 (over y, x, core), tensor: 4 (over z).
Axes of the slice: x: 2, y: 2, z: 4, core: 2. Of those that a mesh axis runs over, the one named last changes fastest.
Arguments:
- tokens: bfloat16 [16384, 768], P('dp'), may hold values from -6 to 6
- segments: int32 [16384], P('dp'), may hold values from 0 to 3, as said below
- query_weight: bfloat16 [768, 768], P(None, 'tensor'), may hold values from -0.21875 to 0.21875
- key_weight: bfloat16 [768, 768], P(None, 'tensor'), may hold values from -0.21875 to 0.21875
- value_weight: bfloat16 [768, 768], P(None, 'tensor'), may hold values from -0.21875 to 0.21875
- query_bias: float32 [768], P('tensor'), may hold values from -3 to 3
- value_bias: float32 [768], P('tensor'), may hold values from -3 to 3
- output_weight: bfloat16 [768, 768], P('tensor'), may hold values from -3 to 3
- output_bias: float32 [768], replicated, may hold values from -3 to 3
- gain_one: float32 [768], replicated, may hold values from 0.25 to 1.75
- shift_one: float32 [768], replicated, may hold values from -3 to 3
- inner_weight: bfloat16 [768, 3072], P(None, 'tensor'), may hold values from -0.21875 to 0.21875
- inner_bias: float32 [3072], P('tensor'), may hold values from -3 to 3
- down_weight: bfloat16 [3072, 768], P('tensor'), may hold values from -0.109375 to 0.109375
- down_bias: float32 [768], replicated, may hold values from -3 to 3
- gain_two: float32 [768], replicated, may hold values from 0.25 to 1.75
- shift_two: float32 [768], replicated, may hold values from -3 to 3
- cotangent: bfloat16 [16384, 768], P('dp'), may hold values from -6 to 6
Outputs:
- layer_out: bfloat16 [16384, 768], P('dp')
- tokens_grad: float32 [16384, 768], P('dp')
- query_grad: float32 [768, 768], P(None, 'tensor')
- key_grad: float32 [768, 768], P(None, 'tensor')
- value_grad: float32 [768, 768], P(None, 'tensor')
- querybias_grad: float32 [768], P('tensor')
- valuebias_grad: float32 [768], P('tensor')
- output_grad: float32 [768, 768], P('tensor')
- outbias_grad: float32 [768], replicated
- gainone_grad: float32 [768], replicated
- shiftone_grad: float32 [768], replicated
- inner_grad: float32 [768, 3072], P(None, 'tensor')
- innerbias_grad: float32 [3072], P('tensor')
- down_grad: float32 [3072, 768], P('tensor')
- downbias_grad: float32 [768], replicated
- gaintwo_grad: float32 [768], replicated
- shifttwo_grad: float32 [768], replicated
Inputs may be any that keep to these rules, and one draw needn't show every extreme that they name: `segments`: each document is a run of 204 to 2048 tokens, the last cut off at the end, and may cross sequence borders; documents are labelled 0, 1, 2, 3, 0, 1, ... in order, so that the documents that touch one sequence carry distinct labels.
All inputs are finite; a program needn't handle non-finite values.
Results may differ from a plain program's by a relative error of at most 0.014.
Values sent between devices are 32-bit elements; how exact they have to be, the bound alone decides.
No kernel may reach another device: no remote copies, remote signals or barrier semaphores. Data moves between devices by JAX's collectives and lax.ppermute only.
A program may use at most 128 MiB of HBM per device.

v0:
```python
import jax
import jax.numpy as jnp
from jax import lax
from jax.sharding import PartitionSpec as P

HEAD_DIM = 64
SEQ_LEN = 512


EPS = 1e-06


def normalize(values, gain, shift):
    center = values - jnp.mean(values, axis=1, keepdims=True)
    spread = jnp.mean(center * center, axis=1, keepdims=True)
    return center * lax.rsqrt(spread + EPS) * gain + shift


def smooth(values):
    return jax.nn.gelu(values, approximate=False)


def matmul(left, right):
    return jnp.dot(left, right, preferred_element_type=jnp.float32)


def inner_first(left, right):
    return lax.dot_general(
        left, right, (((0,), (0,)), ((), ())), preferred_element_type=jnp.float32
    )


def inner_last(left, right):
    return lax.dot_general(
        left, right, (((1,), (1,)), ((), ())), preferred_element_type=jnp.float32
    )


def attend_scores(query_heads, key_heads, allowed, factor):
    scores = (
        jnp.einsum("sqhd,skhd->shqk", query_heads, key_heads, preferred_element_type=jnp.float32)
        * factor
    )
    return jnp.where(allowed, scores, -1000000000.0)


def per_device(
    tokens,
    segments,
    query_weight,
    key_weight,
    value_weight,
    query_bias,
    value_bias,
    output_weight,
    output_bias,
    gain_one,
    shift_one,
    inner_weight,
    inner_bias,
    down_weight,
    down_bias,
    gain_two,
    shift_two,
    cotangent,
):
    tok_rows = tokens.shape[0]
    seq_count = tok_rows // SEQ_LEN
    head_count = query_weight.shape[1] // HEAD_DIM
    factor = HEAD_DIM ** (-0.5)
    head_shape = (seq_count, SEQ_LEN, head_count, HEAD_DIM)
    query_rows = (matmul(tokens, query_weight) + query_bias).astype(jnp.bfloat16)
    key_rows = matmul(tokens, key_weight).astype(jnp.bfloat16)
    value_rows = (matmul(tokens, value_weight) + value_bias).astype(jnp.bfloat16)
    query_heads = query_rows.reshape(head_shape)
    key_heads = key_rows.reshape(head_shape)
    value_heads = value_rows.reshape(head_shape)
    segment_rows = segments.reshape(seq_count, SEQ_LEN)
    allowed = (segment_rows[:, :, None] == segment_rows[:, None, :])[:, None]
    scores = attend_scores(query_heads, key_heads, allowed, factor)
    highest = jnp.max(scores, axis=3, keepdims=True)
    log_total = highest + jnp.log(jnp.sum(jnp.exp(scores - highest), axis=3, keepdims=True))
    weights_low = jnp.exp(scores - log_total).astype(jnp.bfloat16)
    context = jnp.einsum(
        "shqk,skhd->sqhd", weights_low, value_heads, preferred_element_type=jnp.float32
    )
    context_low = context.reshape(tok_rows, head_count * HEAD_DIM).astype(jnp.bfloat16)
    attention = lax.psum(matmul(context_low, output_weight), "tensor")
    first_sum = tokens.astype(jnp.float32) + attention + output_bias
    normed, first_pull = jax.vjp(normalize, first_sum, gain_one, shift_one)
    normed_low = normed.astype(jnp.bfloat16)
    inner_rows = matmul(normed_low, inner_weight) + inner_bias
    activated, gelu_pull = jax.vjp(smooth, inner_rows)
    activated_low = activated.astype(jnp.bfloat16)
    mixed = lax.psum(matmul(activated_low, down_weight), "tensor")
    second_sum = normed + mixed + down_bias
    layer_norm_out, second_pull = jax.vjp(normalize, second_sum, gain_two, shift_two)
    upstream = cotangent.astype(jnp.float32)
    second_grad, gaintwo_part, shifttwo_part = second_pull(upstream)
    downbias_part = jnp.sum(second_grad, axis=0)
    mixed_grad = second_grad.astype(jnp.bfloat16)
    down_part = inner_first(activated_low, mixed_grad)
    activated_grad = inner_last(mixed_grad, down_weight)
    (inner_grad_rows,) = gelu_pull(activated_grad)
    inner_low = inner_grad_rows.astype(jnp.bfloat16)
    innerbias_part = jnp.sum(inner_low.astype(jnp.float32), axis=0)
    inner_part = inner_first(normed_low, inner_low)
    normed_grad = second_grad + lax.psum(inner_last(inner_low, inner_weight), "tensor")
    first_grad, gainone_part, shiftone_part = first_pull(normed_grad)
    outbias_part = jnp.sum(first_grad, axis=0)
    attention_grad = first_grad.astype(jnp.bfloat16)
    output_part = inner_first(context_low, attention_grad)
    context_grad = (
        inner_last(attention_grad, output_weight).astype(jnp.bfloat16).reshape(head_shape)
    )
    scores_again = attend_scores(query_heads, key_heads, allowed, factor)
    probs = jnp.exp(scores_again - log_total)
    probs_low = probs.astype(jnp.bfloat16)
    probs_grad = jnp.einsum(
        "sqhd,skhd->shqk", context_grad, value_heads, preferred_element_type=jnp.float32
    )
    value_grad_heads = jnp.einsum(
        "shqk,sqhd->skhd", probs_low, context_grad, preferred_element_type=jnp.float32
    )
    centering = jnp.sum(probs * probs_grad, axis=3, keepdims=True)
    scores_grad = (probs * (probs_grad - centering)).astype(jnp.bfloat16)
    query_grad_heads = (
        jnp.einsum("shqk,skhd->sqhd", scores_grad, key_heads, preferred_element_type=jnp.float32)
        * factor
    )
    key_grad_heads = (
        jnp.einsum("shqk,sqhd->skhd", scores_grad, query_heads, preferred_element_type=jnp.float32)
        * factor
    )
    local_width = head_count * HEAD_DIM
    query_low = query_grad_heads.reshape(tok_rows, local_width).astype(jnp.bfloat16)
    key_low = key_grad_heads.reshape(tok_rows, local_width).astype(jnp.bfloat16)
    value_low = value_grad_heads.reshape(tok_rows, local_width).astype(jnp.bfloat16)
    query_part = inner_first(tokens, query_low)
    key_part = inner_first(tokens, key_low)
    value_part = inner_first(tokens, value_low)
    querybias_part = jnp.sum(query_low.astype(jnp.float32), axis=0)
    valuebias_part = jnp.sum(value_low.astype(jnp.float32), axis=0)
    input_terms = (
        inner_last(query_low, query_weight)
        + inner_last(key_low, key_weight)
        + inner_last(value_low, value_weight)
    )
    tokens_grad = first_grad + lax.psum(input_terms, "tensor")
    summed = lax.psum(
        (
            query_part,
            key_part,
            value_part,
            querybias_part,
            valuebias_part,
            output_part,
            outbias_part,
            gainone_part,
            shiftone_part,
            inner_part,
            innerbias_part,
            down_part,
            downbias_part,
            gaintwo_part,
            shifttwo_part,
        ),
        "dp",
    )
    return (
        layer_norm_out.astype(jnp.bfloat16),
        tokens_grad,
        summed[0],
        summed[1],
        summed[2],
        summed[3],
        summed[4],
        summed[5],
        summed[6],
        summed[7],
        summed[8],
        summed[9],
        summed[10],
        summed[11],
        summed[12],
        summed[13],
        summed[14],
    )


def solution(mesh):
    in_specs = (
        P("dp", None),
        P("dp"),
        P(None, "tensor"),
        P(None, "tensor"),
        P(None, "tensor"),
        P("tensor"),
        P("tensor"),
        P("tensor", None),
        P(),
        P(),
        P(),
        P(None, "tensor"),
        P("tensor"),
        P("tensor", None),
        P(),
        P(),
        P(),
        P("dp", None),
    )
    out_specs = (
        P("dp", None),
        P("dp", None),
        P(None, "tensor"),
        P(None, "tensor"),
        P(None, "tensor"),
        P("tensor"),
        P("tensor"),
        P("tensor", None),
        P(),
        P(),
        P(),
        P(None, "tensor"),
        P("tensor"),
        P("tensor", None),
        P(),
        P(),
        P(),
    )
    return jax.shard_map(
        per_device, mesh=mesh, in_specs=in_specs, out_specs=out_specs, check_vma=False
    )
```

profile of v0, /device:TPU:0, one launch (start us, length us, event | category | flops | bytes accessed | tf_op | source)
XLA Modules:
  0.0 1195.2 jit_solution(60687093274911555)
XLA Ops:
  8.1 3.2 fusion.14
  11.8 3.1 fusion.13
  14.9 1.5 reshape.138
  16.4 3.1 convolution_convert_fusion.1
  19.4 1.5 reshape.140
  22.1 7.4 fusion
  29.5 7.4 exponential_reduce_fusion
  37.0 6.5 fusion.15
  45.2 3.7 fusion.39
  49.0 225.6 %all-reduce.8.cloned.1.call-done = f32[2048,768]{1,0:T(8,128)} async-done(((f32[2048,768]{1,0:T(8,128)}), f32[2048,768]{1,0:T(8,128)}) %all-reduce.8.cloned.1.call-update) | async-done | bytes 6291472 | tf_op jit(solution)/shard_map/psum | solution.py:88
  274.6 4.6 fusion.38
  281.8 18.3 %multiply_convert_fusion.1 = (bf16[2048,768]{1,0:T(8,128)(2,1)S(1)}, f32[2048,768]{1,0:T(8,128)}, f32[2048,768]{1,0:T(8,128)}) fusion(f32[768]{0:T(1024)S(1)} %copy-done.30, bf16[2048,768]{1,0:T(8,128)(2,1)S(1)} %fusion.12, bf16[768,768]{1,0:T(8,128)(2,1)S(1)} %copy-done), kind=kOutput, calls=%fused_computation.26 | convolution fusion | flops 2519728128 | bytes 20057088 | tf_op jit(solution)/shard_map/dot_general | solution.py:24
  300.2 1.7 copy-done.33
  301.8 4.5 fusion.40
  306.4 221.9 %all-reduce.10.cloned.1.call-done = f32[2048,768]{1,0:T(8,128)} async-done(((f32[2048,768]{1,0:T(8,128)}), f32[2048,768]{1,0:T(8,128)}) %all-reduce.10.cloned.1.call-update) | async-done | bytes 6291472 | tf_op jit(solution)/shard_map/psum | solution.py:95
  528.3 5.7 fusion.36
  536.0 2.6 fusion.6
  538.6 4.3 fusion.35
  542.9 9.3 convert_reduce_fusion.1
  552.3 1.6 copy-done.32
  553.9 4.5 fusion.41
  558.5 221.9 %all-reduce.12.cloned.1.call-done = f32[2048,768]{1,0:T(8,128)} async-done(((f32[2048,768]{1,0:T(8,128)}), f32[2048,768]{1,0:T(8,128)}) %all-reduce.12.cloned.1.call-update) | async-done | bytes 6291472 | tf_op jit(solution)/shard_map/psum | solution.py:108
  780.4 8.3 multiply_reduce_fusion.1
  788.7 4.2 fusion.34
  793.0 2.7 copy-done.3
  795.7 1.3 convolution_convert_fusion
  797.0 1.5 reshape.141
  798.5 8.6 convert_reduce_fusion.2
  807.1 11.0 multiply_reduce_fusion
  818.2 7.7 multiply_convert_fusion
  825.9 2.0 fusion.16
  833.7 3.8 add_add_fusion.2
  837.7 7.1 fusion.44
  844.8 7.2 fusion.29
  852.0 1.7 convolution_bitcast_fusion
  853.7 1.7 convolution_bitcast_fusion.1
  855.3 1.7 convolution_bitcast_fusion.2
  857.0 1.9 fusion.31
  859.1 200.4 %all-reduce.14.cloned.1.call-done = f32[2048,768]{1,0:T(8,128)} async-done(((f32[2048,768]{1,0:T(8,128)}), f32[2048,768]{1,0:T(8,128)}) %all-reduce.14.cloned.1.call-update) | async-done | bytes 6291472 | tf_op jit(solution)/shard_map/psum | solution.py:149
  1059.4 7.7 add_reduce_fusion
  1067.1 26.0 %all-reduce = (f32[192]{0:T(256)}, f32[192]{0:T(256)}, f32[768]{0:T(1024)}, f32[768]{0:T(1024)}, f32[768]{0:T(1024)}, /*index=5*/f32[768]{0:T(1024)}, f32[768]{0:T(1024)}, f32[768]{0:T(1024)}, f32[768]{0:T(1024)}) all-reduce(f32[192]{0:T(256)S(1)} %reduce_sum.218, ...), channel_id=1, replica_groups=mesh['dp'=8,'tensor'=4] {'dp'}, use_global_device_ids=true, to_apply=%region_19.20 | all-reduce | flops 5760 | bytes 46080 | tf_op jit(solution)/shard_map/psum | solution.py:150
  1093.1 84.6 %all-reduce.16.cloned.1.call-done = (f32[768,192]{0,1:T(8,128)}, f32[768,192]{0,1:T(8,128)}, f32[768,192]{0,1:T(8,128)}, f32[192,768]{1,0:T(8,128)}, f32[768,768]{1,0:T(8,128)}, /*index=5*/f32[768,768]{1,0:T(8,128)}) async-done(((f32[768,192]{0,1:T(8,128)}, f32[768,192]{0,1:T(8,128)}, f32[768,192]{0,1:T(8,128)}, f32[192,768]{1,0:T(8,128)}, f32[768,768]{1,0:T(8,128)}, /*index=5*/f32[768,768]{1,0:T(8,128)}), ...) | async-done | bytes 7077904 | tf_op jit(solution)/shard_map/psum | solution.py:150
  1177.7 2.1 copy.109
  1179.8 2.0 copy.110
  1181.8 1.9 copy.111
  1183.7 1.9 copy.112
  1185.6 1.4 copy.113
  1187.1 1.4 copy.114
  (122 shorter events, 15.2 us)
Async XLA Ops:
  7.2 274.6 %copy-start = (bf16[768,768]{1,0:T(8,128)(2,1)S(1)}, bf16[768,768]{1,0:T(8,128)(2,1)}, u32[]{:S(2)}) copy-start(bf16[768,768]{1,0:T(8,128)(2,1)} %param.29) | copy-start | bytes 3538948
  7.2 4.6 copy-start.31
  7.2 267.4 %all-reduce.8.cloned.1.call-start = ((), (), s32[]{:S(2)}) async-start(), calls=%async_computation | async-start | bytes 12582912 | tf_op jit(solution)/shard_map/psum | solution.py:88
  11.2 5.1 copy-start.18
  29.5 7.4 copy-start.11
  36.9 8.2 copy-start.16
  44.3 0.9 copy-start.7
  45.2 229.5 %copy-start.26 = (f32[768]{0:T(1024)S(1)}, f32[768]{0:T(1024)}, u32[]{:S(2)}) copy-start(f32[768]{0:T(1024)} %param.26) | copy-start | bytes 9220
  48.9 479.4 %all-reduce.10.cloned.1.call-start = ((), (), s32[]{:S(2)}) async-start(), calls=%async_computation.1 | async-start | bytes 12582912 | tf_op jit(solution)/shard_map/psum | solution.py:95
  279.2 2.6 copy-start.2
  279.2 0.9 copy-start.21
  279.3 0.9 copy-start.23
  280.1 1.7 copy-start.30
  281.8 18.3 %copy-start.10 = (bf16[2048,768]{1,0:T(8,128)(2,1)}, bf16[2048,768]{1,0:T(8,128)(2,1)S(1)}, u32[]{:S(2)}) copy-start(bf16[2048,768]{1,0:T(8,128)(2,1)S(1)} %fusion.12) | copy-start | bytes 9437188
  281.8 20.0 %copy-start.28 = (bf16[768,768]{1,0:T(8,128)(2,1)S(1)}, bf16[768,768]{1,0:T(8,128)(2,1)}, u32[]{:S(2)}) copy-start(bf16[768,768]{1,0:T(8,128)(2,1)} %param.31) | copy-start | bytes 3538948
  300.2 1.7 copy-start.33
  306.4 222.0 %copy-start.27 = (f32[768]{0:T(1024)S(1)}, f32[768]{0:T(1024)}, u32[]{:S(2)}) copy-start(f32[768]{0:T(1024)} %param.32) | copy-start | bytes 9220
  306.4 474.0 %all-reduce.12.cloned.1.call-start = ((), (), s32[]{:S(2)}) async-start(), calls=%async_computation.2 | async-start | bytes 12582912 | tf_op jit(solution)/shard_map/psum | solution.py:108
  534.1 1.9 copy-start.6
  534.1 1.9 copy-start.22
  534.9 3.6 copy-start.24
  536.0 6.9 slice-start.5
  538.6 4.3 copy-start.29
  538.6 4.3 slice-start.6
  542.9 9.4 copy-start.5
  552.3 1.6 copy-start.32
  558.4 501.0 %all-reduce.14.cloned.1.call-start = ((), (), s32[]{:S(2)}) async-start(), calls=%async_computation.3 | async-start | bytes 12582912 | tf_op jit(solution)/shard_map/psum | solution.py:149
  793.0 2.7 copy-start.3
  798.5 8.6 copy-start.12
  798.5 8.6 copy-start.13
  798.5 19.6 %slice-start = ((s8[12582912]{0:T(1024)(128)(4,1)}), s8[4194304]{0:T(1024)(128)(4,1)S(1)}, s32[]{:S(2)}) async-start(s8[12582912]{0:T(1024)(128)(4,1)} %bitcast.74), calls=%async_computation.5 | async-start | bytes 8388608
  798.5 19.7 %slice-start.1 = ((s8[12582912]{0:T(1024)(128)(4,1)}), s8[4194304]{0:T(1024)(128)(4,1)S(1)}, s32[]{:S(2)}) async-start(s8[12582912]{0:T(1024)(128)(4,1)} %bitcast.74), calls=%async_computation.6 | async-start | bytes 8388608
  807.1 11.1 slice-start.2
  825.8 2.0 copy-start.9
  829.1 2.4 copy-start.17
  831.3 1.3 copy-start.19
  832.6 1.1 copy-start.20
  837.5 340.3 %all-reduce.16.cloned.1.call-start = ((), (), s32[]{:S(2)}) async-start(), calls=%async_computation.4 | async-start | bytes 14155776 | tf_op jit(solution)/shard_map/psum | solution.py:150
  837.7 7.1 copy-start.34
  844.8 7.2 copy-start.4
  852.0 5.0 slice-start.3
  852.0 5.0 copy-start.8
  853.7 3.3 slice-start.4
  859.1 208.0 %copy-start.25 = (f32[768]{0:T(1024)S(1)}, f32[768]{0:T(1024)}, u32[]{:S(2)}) copy-start(f32[768]{0:T(1024)} %get-tuple-element.62) | copy-start | bytes 9220
  1177.7 7.9 copy-start.15
  1177.7 9.3 copy-start.14
  1177.7 10.7 copy-start.1
Sparse Core Ops, SparseCore 0:
  49.1 225.5 all-reduce.7
  306.5 221.7 all-reduce.9
  558.6 221.7 all-reduce.11
  837.6 221.7 all-reduce.13
  1064.5 113.1 all-reduce.15
where the time goes:
time: 1200 us
  waiting for transfers between devices  955 us (80%)
  matrix products  115 us (10%)
  other arithmetic  56.8 us (5%)
  local copies, waits for them, and re-layouts  28.1 us (2%)
  blocking collectives  26 us (2%)
  between operations  14.6 us (1%)
    psum x1, waiting for transfers between devices, per_device(): attention = lax.psum(matmul(context_low, output_weight), 'tensor')  226 us
    psum x1, waiting for transfers between devices, per_device(): mixed = lax.psum(matmul(activated_low, down_weight), 'tensor')  222 us
    psum x1, waiting for transfers between devices, per_device(): lax.psum(inner_last(inner_low, inner_weight), 'tensor')  222 us
    psum x1, waiting for transfers between devices, per_device(): tokens_grad = first_grad + lax.psum(input_terms, 'tensor')  200 us
    psum x1, waiting for transfers between devices, per_device(): lax.psum((query_part, key_part, value_part, querybias_part, valuebias_par...  84.6 us
    dot_general x6, matrix products, matmul(): return jnp.dot(left, right, preferred_element_type=jnp.float32)  35.9 us
    psum x1, blocking collectives, per_device(): lax.psum((query_part, key_part, value_part, querybias_part, valuebias_par...  26 us
  transfers between devices with their start and end apart: 5, of which 5 were waited for; matrix products, arithmetic and copies ran while one was open for 2% of the time, Pallas kernels for 0%

commit v1 on v0

v1 whole, which is shorter than its diff:
```python
import functools
import math

import jax
import jax.numpy as jnp
from jax import lax
from jax.experimental import pallas as pl
from jax.experimental.pallas import tpu as pltpu
from jax.sharding import PartitionSpec as P

HEAD_DIM = 64
SEQ_LEN = 512
EPS = 1e-06
MASKED = -1000000000.0
LANES = 8
LOW = jnp.bfloat16
WIDE = jnp.float32
VMEM_LIMIT = 56 * 1024 * 1024

NN = (((1,), (0,)), ((), ()))
NT = (((1,), (1,)), ((), ()))


def dot(left, right, dims):
    return lax.dot_general(left, right, dims, preferred_element_type=WIDE)


def params(**kw):
    return pltpu.CompilerParams(vmem_limit_bytes=VMEM_LIMIT, **kw)


def whole(shape):
    zeros = (0,) * len(shape)
    return pl.BlockSpec(shape, lambda i: zeros)


def rows(block, width):
    return pl.BlockSpec((block, width), lambda i: (i, 0))


def head_mask(width, head):
    lane = lax.broadcasted_iota(jnp.int32, (1, width), 1)
    return (lane >= head * HEAD_DIM) & (lane < (head + 1) * HEAD_DIM)


def same_document(seg_col, seg_row):
    return jnp.where(seg_col == seg_row, jnp.float32(3e38), jnp.float32(MASKED))


def attend_forward(remote, width, x_ref, scol_ref, srow_ref, bias_ref, acc_ref, *rest):
    if remote:
        place_ref, slices, rest = rest[0], rest[1 : 1 + LANES], rest[1 + LANES :]
        qkv_ref, c_ref, l_ref, out_ref, w_ref, wide_ref = rest
        part = width // LANES

        @pl.when(pl.program_id(0) == 0)
        def _():
            here = place_ref[0]
            for m in range(LANES):
                spot = here ^ m
                for t in range(4):
                    at = pl.multiple_of(t * width + spot * part, 8)
                    wide_ref[pl.ds(at, part), :] = slices[m][t * part : (t + 1) * part, :]
            w_ref[...] = wide_ref[...].astype(LOW)
    else:
        w_ref, qkv_ref, c_ref, l_ref, out_ref = rest
    heads = width // HEAD_DIM
    x = x_ref[...]
    qkv = dot(x, w_ref[: 3 * width, :], NT) + bias_ref[...]
    qkv = qkv.astype(LOW)
    qkv_ref[...] = qkv
    queries = qkv[:, :width] * LOW(HEAD_DIM**-0.5)
    keys = qkv[:, width : 2 * width]
    values_t = qkv[:, 2 * width :].T
    limit = same_document(scol_ref[...], srow_ref[0])
    parts = []
    for h in range(heads):
        key_h = jnp.where(head_mask(width, h), keys, LOW(0))
        scores = jnp.minimum(dot(key_h, queries, NT), limit)
        top = jnp.max(scores, axis=0, keepdims=True)
        weights = jnp.exp(scores - top)
        total = jnp.sum(weights, axis=0, keepdims=True)
        l_ref[0, h : h + 1, :] = top + jnp.log(total)
        value_h = values_t[h * HEAD_DIM : (h + 1) * HEAD_DIM, :]
        parts.append(dot(value_h, weights.astype(LOW), NN) / total)
    context = jnp.concatenate(parts, axis=0).T.astype(LOW)
    c_ref[...] = context
    add = dot(context, w_ref[3 * width :, :], NN)
    out_ref[...] = acc_ref[...] + add


def attend_backward(width, own, qkv_ref, c_ref, l_ref, scol_ref, srow_ref, da_ref, w_ref, acc_ref, *rest):
    out_ref = rest[0]
    heads = width // HEAD_DIM
    qkv = qkv_ref[...]
    queries = qkv[:, :width] * LOW(HEAD_DIM**-0.5)
    keys = qkv[:, width : 2 * width]
    values = qkv[:, 2 * width :]
    keys_t = keys.T
    dc = dot(da_ref[...], w_ref[3 * width :, :], NT).astype(LOW)
    prod_t = (dc.astype(WIDE) * c_ref[...].astype(WIDE)).T
    limit = same_document(scol_ref[...], srow_ref[0])
    dq_parts = []
    dk = jnp.zeros((SEQ_LEN, width), WIDE)
    dv = jnp.zeros((SEQ_LEN, width), WIDE)
    for h in range(heads):
        mask = head_mask(width, h)
        key_h = jnp.where(mask, keys, LOW(0))
        query_h = jnp.where(mask, queries, LOW(0))
        value_h = jnp.where(mask, values, LOW(0))
        dc_h = jnp.where(mask, dc, LOW(0))
        scores = jnp.minimum(dot(key_h, queries, NT), limit)
        probs = jnp.exp(scores - l_ref[0, h : h + 1, :])
        dprobs = dot(value_h, dc, NT)
        delta = jnp.sum(prod_t[h * HEAD_DIM : (h + 1) * HEAD_DIM, :], axis=0, keepdims=True)
        dscores = (probs * (dprobs - delta)).astype(LOW)
        dv = dv + dot(probs.astype(LOW), dc_h, NN)
        dk = dk + dot(dscores, query_h, NN)
        dq_parts.append(dot(keys_t[h * HEAD_DIM : (h + 1) * HEAD_DIM, :], dscores, NN))
    dq = jnp.concatenate(dq_parts, axis=0).T * (HEAD_DIM**-0.5)
    dqkv = jnp.concatenate([dq, dk, dv], axis=1).astype(LOW)
    if own:
        rest[1][...] = dqkv
        row_sum = jnp.sum(dqkv.astype(WIDE), axis=0, keepdims=True)
        sum_ref = rest[2]

        @pl.when(pl.program_id(0) == 0)
        def _():
            sum_ref[...] = jnp.zeros_like(sum_ref)

        sum_ref[0:1, :] += row_sum
    out_ref[...] = acc_ref[...] + dot(dqkv, w_ref[: 3 * width, :], NN)


def call_attend_forward(tokens, scol, srow, bias, acc, weight, place, slices):
    count, model = tokens.shape
    width = bias.shape[1] // 3
    seqs = count // SEQ_LEN
    remote = slices is not None
    in_specs = [
        rows(SEQ_LEN, model),
        rows(SEQ_LEN, 1),
        pl.BlockSpec((1, 1, SEQ_LEN), lambda i: (i, 0, 0)),
        whole((1, 3 * width)),
        rows(SEQ_LEN, model),
    ]
    out_specs = [
        rows(SEQ_LEN, 3 * width),
        rows(SEQ_LEN, width),
        pl.BlockSpec((1, 8, SEQ_LEN), lambda i: (i, 0, 0)),
        rows(SEQ_LEN, model),
    ]
    out_shape = [
        jax.ShapeDtypeStruct((count, 3 * width), LOW),
        jax.ShapeDtypeStruct((count, width), LOW),
        jax.ShapeDtypeStruct((seqs, 8, SEQ_LEN), WIDE),
        jax.ShapeDtypeStruct((count, model), WIDE),
    ]
    scratch = []
    if remote:
        in_specs += [pl.BlockSpec(memory_space=pltpu.SMEM)]
        in_specs += [whole(slices[0].shape)] * LANES
        out_specs += [whole((4 * width, model))]
        out_shape += [jax.ShapeDtypeStruct((4 * width, model), LOW)]
        scratch = [pltpu.VMEM((4 * width, model), WIDE)]
        extra = (place, *slices)
    else:
        in_specs += [whole((4 * width, model))]
        extra = (weight,)
    flops = 2 * count * model * width * 4 + 4 * count * SEQ_LEN * width * 4
    return pl.pallas_call(
        functools.partial(attend_forward, remote, width),
        grid=(seqs,),
        in_specs=in_specs,
        out_specs=out_specs,
        out_shape=out_shape,
        scratch_shapes=scratch,
        compiler_params=params(),
        cost_estimate=pl.CostEstimate(
            flops=flops, bytes_accessed=count * model * 12, transcendentals=count * SEQ_LEN * width // HEAD_DIM
        ),
    )(tokens, scol, srow, bias, acc, *extra)


def call_attend_backward(own, qkv, context, logs, scol, srow, da, weight, acc):
    count, model = acc.shape
    width = context.shape[1]
    seqs = count // SEQ_LEN
    in_specs = [
        rows(SEQ_LEN, 3 * width),
        rows(SEQ_LEN, width),
        pl.BlockSpec((1, 8, SEQ_LEN), lambda i: (i, 0, 0)),
        rows(SEQ_LEN, 1),
        pl.BlockSpec((1, 1, SEQ_LEN), lambda i: (i, 0, 0)),
        rows(SEQ_LEN, model),
        whole((4 * width, model)),
        rows(SEQ_LEN, model),
    ]
    out_specs = [rows(SEQ_LEN, model)]
    out_shape = [jax.ShapeDtypeStruct((count, model), WIDE)]
    if own:
        out_specs += [rows(SEQ_LEN, 3 * width), whole((8, 3 * width))]
        out_shape += [
            jax.ShapeDtypeStruct((count, 3 * width), LOW),
            jax.ShapeDtypeStruct((8, 3 * width), WIDE),
        ]
    flops = 2 * count * model * width * 4 + 10 * count * SEQ_LEN * width * 4
    return pl.pallas_call(
        functools.partial(attend_backward, width, own),
        grid=(seqs,),
        in_specs=in_specs,
        out_specs=out_specs,
        out_shape=out_shape,
        compiler_params=params(),
        cost_estimate=pl.CostEstimate(
            flops=flops, bytes_accessed=count * model * 12, transcendentals=count * SEQ_LEN * width // HEAD_DIM
        ),
    )(qkv, context, logs, scol, srow, da, weight, acc)


def gelu_pair(u):
    tail = jnp.exp(u * u * -0.5)
    t = 1.0 / (1.0 + jnp.abs(u) * (0.3275911 * math.sqrt(0.5)))
    poly = 0.5 * 1.061405429
    for c in (-1.453152027, 1.421413741, -0.284496736, 0.254829592):
        poly = poly * t + 0.5 * c
    half = poly * t * tail
    phi = jnp.where(u < 0.0, half, 1.0 - half)
    return u * phi, phi + u * tail * (1.0 / math.sqrt(2.0 * math.pi))


def stats(values):
    mean = jnp.mean(values, axis=1, keepdims=True)
    center = values - mean
    scale = lax.rsqrt(jnp.mean(center * center, axis=1, keepdims=True) + EPS)
    return center * scale, scale


def feed_forward(remote, x_ref, acc_ref, bias_ref, *rest):
    if remote:
        place_ref, slices, rest = rest[0], rest[1 : 1 + LANES], rest[1 + LANES :]
        slope_ref, out_ref, wi_ref, wd_ref = rest
        part = slices[0].shape[0] // 2

        @pl.when(pl.program_id(0) == 0)
        def _():
            here = place_ref[0]
            for m in range(LANES):
                at = pl.multiple_of((here ^ m) * part, part)
                wi_ref[pl.ds(at, part), :] = slices[m][:part, :].astype(LOW)
                wd_ref[pl.ds(at, part), :] = slices[m][part:, :].astype(LOW)

        normed_low = x_ref[...]
    else:
        (obias_ref, gain_ref, shift_ref, wi_ref, wd_ref) = rest[:5]
        slope_ref, out_ref, h1_ref, n1_ref, act_ref = rest[5:]
        h1 = x_ref[...].astype(WIDE) + acc_ref[...] + obias_ref[...]
        h1_ref[...] = h1
        hat, _ = stats(h1)
        normed_low = (hat * gain_ref[...] + shift_ref[...]).astype(LOW)
        n1_ref[...] = normed_low
    hidden = wi_ref.shape[0]
    chunk = 256
    total = None
    for c in range(0, hidden, chunk):
        cols = slice(c, c + chunk)
        u = dot(normed_low, wi_ref[cols, :], NT) + bias_ref[:, cols]
        act, slope = gelu_pair(u)
        act = act.astype(LOW)
        slope_ref[:, cols] = slope.astype(LOW)
        if not remote:
            act_ref[:, cols] = act
        add = dot(act, wd_ref[cols, :], NN)
        total = add if total is None else total + add
    out_ref[...] = total if not remote else acc_ref[...] + total


def call_feed_forward(x, acc, bias, remote, extra, block=512):
    count, model = acc.shape
    hidden = bias.shape[1]
    in_specs = [rows(block, model), rows(block, model), whole((1, hidden))]
    out_specs = [rows(block, hidden), rows(block, model)]
    out_shape = [
        jax.ShapeDtypeStruct((count, hidden), LOW),
        jax.ShapeDtypeStruct((count, model), WIDE),
    ]
    if remote:
        in_specs += [pl.BlockSpec(memory_space=pltpu.SMEM)]
        in_specs += [whole(extra[1].shape)] * LANES
        out_specs += [whole((hidden, model))] * 2
        out_shape += [jax.ShapeDtypeStruct((hidden, model), LOW)] * 2
    else:
        in_specs += [whole((1, model))] * 3 + [whole((hidden, model))] * 2
        out_specs += [rows(block, model), rows(block, model), rows(block, hidden)]
        out_shape += [
            jax.ShapeDtypeStruct((count, model), WIDE),
            jax.ShapeDtypeStruct((count, model), LOW),
            jax.ShapeDtypeStruct((count, hidden), LOW),
        ]
    return pl.pallas_call(
        functools.partial(feed_forward, remote),
        grid=(count // block,),
        in_specs=in_specs,
        out_specs=out_specs,
        out_shape=out_shape,
        compiler_params=params(),
        cost_estimate=pl.CostEstimate(
            flops=4 * count * model * hidden, bytes_accessed=count * model * 14, transcendentals=count * hidden * 2
        ),
    )(x, acc, bias, *extra)


def norm_back(grad, hat, scale, gain):
    d = grad * gain
    first = jnp.mean(d, axis=1, keepdims=True)
    second = jnp.mean(d * hat, axis=1, keepdims=True)
    return scale * (d - first - hat * second)


def column_sum(values):
    return jnp.sum(values, axis=0, keepdims=True)


def middle(groups, h1_ref, m_ref, cot_ref, g1_ref, b1_ref, db_ref, g2_ref, b2_ref, *rest):
    slopes, wis, wds = rest[:groups], rest[groups : 2 * groups], rest[2 * groups : 3 * groups]
    layer_ref, dm_ref, du_ref, dh1_ref, da_ref, sums_ref = rest[3 * groups :]

    @pl.when(pl.program_id(0) == 0)
    def _():
        sums_ref[...] = jnp.zeros_like(sums_ref)

    hat1, scale1 = stats(h1_ref[...])
    normed = hat1 * g1_ref[...] + b1_ref[...]
    hat2, scale2 = stats(normed + m_ref[...] + db_ref[...])
    layer_ref[...] = (hat2 * g2_ref[...] + b2_ref[...]).astype(LOW)
    up = cot_ref[...].astype(WIDE)
    sums_ref[0:1, :] += column_sum(up * hat2)
    sums_ref[1:2, :] += column_sum(up)
    dh2 = norm_back(up, hat2, scale2, g2_ref[...])
    sums_ref[2:3, :] += column_sum(dh2)
    dm = dh2.astype(LOW)
    dm_ref[...] = dm
    dn1 = dh2
    hidden = wis[0].shape[0]
    chunk = 256
    for g in range(groups):
        for c in range(0, hidden, chunk):
            cols = slice(c, c + chunk)
            dact = dot(dm, wds[g][cols, :], NT)
            du = (dact * slopes[g][:, cols].astype(WIDE)).astype(LOW)
            if g == 0:
                du_ref[:, cols] = du
                sums_ref[6:7, cols] += column_sum(du.astype(WIDE))
            dn1 = dn1 + dot(du, wis[g][cols, :], NN)
    sums_ref[3:4, :] += column_sum(dn1 * hat1)
    sums_ref[4:5, :] += column_sum(dn1)
    dh1 = norm_back(dn1, hat1, scale1, g1_ref[...])
    sums_ref[5:6, :] += column_sum(dh1)
    dh1_ref[...] = dh1
    da_ref[...] = dh1.astype(LOW)


def call_middle(h1, mixed, cot, vectors, slopes, wis, wds, block=256):
    count, model = h1.shape
    groups = len(slopes)
    hidden = wis[0].shape[0]
    once = pl.BlockSpec((hidden, model), lambda i: (0, 0), pipeline_mode=pl.Buffered(1))
    in_specs = [rows(block, model)] * 3 + [whole((1, model))] * 5
    in_specs += [rows(block, hidden)] * groups + [once] * (2 * groups)
    out_specs = [
        rows(block, model),
        rows(block, model),
        rows(block, hidden),
        rows(block, model),
        rows(block, model),
        whole((8, model)),
    ]
    out_shape = [
        jax.ShapeDtypeStruct((count, model), LOW),
        jax.ShapeDtypeStruct((count, model), LOW),
        jax.ShapeDtypeStruct((count, hidden), LOW),
        jax.ShapeDtypeStruct((count, model), WIDE),
        jax.ShapeDtypeStruct((count, model), LOW),
        jax.ShapeDtypeStruct((8, model), WIDE),
    ]
    return pl.pallas_call(
        functools.partial(middle, groups),
        grid=(count // block,),
        in_specs=in_specs,
        out_specs=out_specs,
        out_shape=out_shape,
        compiler_params=params(),
        cost_estimate=pl.CostEstimate(
            flops=4 * count * model * hidden * groups, bytes_accessed=count * model * 30, transcendentals=0
        ),
    )(h1, mixed, cot, *vectors, *slopes, *wis, *wds)


def inner_first(left, right):
    return lax.dot_general(left, right, (((0,), (0,)), ((), ())), preferred_element_type=WIDE)


def swap(value, mask, size):
    return lax.ppermute(value, "dp", [(i, i ^ mask) for i in range(size)])


def spread(piece, shift, order, groups, size):
    mine = lax.ppermute(piece, "tensor", [((i + shift) % groups, i) for i in range(groups)])
    first, second = order
    got = {0: mine}
    got[first] = swap(mine, first, size)
    got[second] = swap(mine, second, size)
    got[first ^ second] = swap(got[first], second, size)
    for m in (0, 2, 4, 6):
        got[m ^ 1] = swap(got[m], 1, size)
    return [got[m] for m in range(LANES)]


def per_device(
    groups,
    size,
    tokens,
    segments,
    query_weight,
    key_weight,
    value_weight,
    query_bias,
    value_bias,
    output_weight,
    output_bias,
    gain_one,
    shift_one,
    inner_weight,
    inner_bias,
    down_weight,
    down_bias,
    gain_two,
    shift_two,
    cotangent,
):
    count, model = tokens.shape
    width = query_weight.shape[1]
    hidden = inner_weight.shape[1]
    place = (lax.axis_index("dp") % LANES).astype(jnp.int32)
    place_arg = place.reshape(1)

    qkvo = jnp.concatenate([query_weight.T, key_weight.T, value_weight.T, output_weight], axis=0)
    inner_t = inner_weight.T
    narrow, deep = width // LANES, hidden // LANES
    head_piece = lax.dynamic_slice(
        qkvo.reshape(4, width, model), (0, place * narrow, 0), (4, narrow, model)
    ).reshape(4 * narrow, model).astype(WIDE)
    deep_piece = jnp.concatenate(
        [
            lax.dynamic_slice(inner_t, (place * deep, 0), (deep, model)),
            lax.dynamic_slice(down_weight, (place * deep, 0), (deep, model)),
        ],
        axis=0,
    ).astype(WIDE)
    biases = jnp.concatenate([query_bias, jnp.zeros_like(query_bias), value_bias, inner_bias]).reshape(1, -1)
    bias_of = [biases] + [
        lax.ppermute(biases, "tensor", [((i + j) % groups, i) for i in range(groups)]) for j in range(1, groups)
    ]
    orders = ((2, 4), (4, 2))
    head_slices = [None] + [spread(head_piece, j, orders[j % 2], groups, size) for j in range(1, groups)]
    deep_slices = [None] + [spread(deep_piece, j, orders[(j + 1) % 2], groups, size) for j in range(1, groups)]

    scol = segments.reshape(count, 1)
    srow = segments.reshape(count // SEQ_LEN, 1, SEQ_LEN)
    acc = jnp.zeros((count, model), WIDE)
    saved = []
    for j in range(groups):
        out = call_attend_forward(
            tokens, scol, srow, bias_of[j][:, : 3 * width], acc, qkvo if j == 0 else None, place_arg, head_slices[j]
        )
        qkv, context, logs, acc = out[:4]
        saved.append((qkv, context, logs, qkvo if j == 0 else out[4]))

    row = lambda v: v.reshape(1, -1)
    wis, wds, slopes = [inner_t], [down_weight], []
    slope, mixed, h1, n1, act = call_feed_forward(
        tokens,
        acc,
        biases[:, 3 * width :],
        False,
        (row(output_bias), row(gain_one), row(shift_one), inner_t, down_weight),
    )
    slopes.append(slope)
    for j in range(1, groups):
        slope, mixed, wi, wd = call_feed_forward(
            n1, mixed, bias_of[j][:, 3 * width :], True, (place_arg, *deep_slices[j])
        )
        slopes.append(slope)
        wis.append(wi)
        wds.append(wd)

    vectors = (row(gain_one), row(shift_one), row(down_bias), row(gain_two), row(shift_two))
    layer_out, dm, du, dh1, da, sums = call_middle(h1, mixed, cotangent, vectors, slopes, wis, wds)

    down_part = lax.psum(inner_first(act, dm), "dp")
    inner_part = lax.psum(inner_first(n1, du), "dp")

    acc = dh1
    for j in range(groups):
        qkv, context, logs, weight = saved[j]
        out = call_attend_backward(j == 0, qkv, context, logs, scol, srow, da, weight, acc)
        acc = out[0]
        if j == 0:
            dqkv, qkv_sums = out[1:]
    tokens_grad = acc
    rest = lax.psum(
        (
            inner_first(dqkv, tokens),
            inner_first(saved[0][1], da),
            sums,
            qkv_sums,
        ),
        "dp",
    )
    qkv_grad, output_grad, sums, qkv_sums = rest
    return (
        layer_out,
        tokens_grad,
        qkv_grad[:width].T,
        qkv_grad[width : 2 * width].T,
        qkv_grad[2 * width :].T,
        qkv_sums[0, :width],
        qkv_sums[0, 2 * width :],
        output_grad,
        sums[5],
        sums[3],
        sums[4],
        inner_part,
        sums[6, :hidden],
        down_part,
        sums[2],
        sums[0],
        sums[1],
    )


def solution(mesh):
    whole_rows, columns, lines, split = P("dp", None), P(None, "tensor"), P("tensor", None), P("tensor")
    in_specs = (
        whole_rows, P("dp"), columns, columns, columns, split, split, lines, P(), P(), P(),
        columns, split, lines, P(), P(), P(), whole_rows,
    )
    out_specs = (
        whole_rows, whole_rows, columns, columns, columns, split, split, lines, P(), P(), P(),
        columns, split, lines, P(), P(), P(),
    )
    body = functools.partial(per_device, mesh.shape["tensor"], mesh.shape["dp"])
    return jax.shard_map(body, mesh=mesh, in_specs=in_specs, out_specs=out_specs, check_vma=False)
```

time: 1200 us -> 491 us (0.41)
  waiting for transfers between devices: 955 us -> 122 us
  Pallas kernels: 0 us -> 237 us
  matrix products: 115 us -> 17.1 us
  other arithmetic: 56.8 us -> 2.37 us
  starting transfers between devices: 0.38 us -> 39.3 us
    psum x5 -> x1, waiting for transfers between devices: 954 us -> 41.3 us  [per_device(): lax.psum((inner_first(dqkv, tokens), inner_first(saved[0][1], da), sums,...]
    pallas_call x0 -> x13, Pallas kernels: none -> 237 us  [the longest x4 74.9 us: call_attend_backward(): pl.pallas_call(functools.partial(attend_backward, width, own), grid=(seqs...]
    dot_general x18 -> x0, matrix products: 93.7 us -> none  [the longest x6 35.9 us: matmul(): return jnp.dot(left, right, preferred_element_type=jnp.float32)]
    ppermute x0 -> x51, waiting for transfers between devices: none -> 80.2 us  [the longest x6 33.9 us: spread(): lax.ppermute(piece, 'tensor', [((i + shift) % groups, i) for i in range(g...]
    reduce_sum x10 -> x0, other arithmetic: 46.5 us -> none  [the longest x4 18.8 us: normalize(): center = values - jnp.mean(values, axis=1, keepdims=True)]
    ppermute x0 -> x51, starting transfers between devices: none -> 39.3 us  [the longest x42 23.4 us: swap(): return lax.ppermute(value, 'dp', [(i, i ^ mask) for i in range(size)])]
  transfers between devices with their start and end apart: 5 -> 52, of which waited for: 5 -> 13; matrix products, arithmetic and copies ran while one was open for 2% -> 4% of each run, Pallas kernels for 0% -> 34%
where the time goes in v1:
time: 491 us; the launch traced here: 486 us
  Pallas kernels  237 us (48%)
  waiting for transfers between devices  122 us (25%)
  starting transfers between devices  39.3 us (8%)
  local copies, waits for them, and re-layouts  27.6 us (6%)
  blocking collectives  25.8 us (5%)
  matrix products  17.1 us (3%)
  between operations  15.2 us (3%)
    pallas_call x4, Pallas kernels, call_attend_backward(): pl.pallas_call(functools.partial(attend_backward, width, own), grid=(seqs...  74.9 us
    pallas_call x4, Pallas kernels, call_feed_forward(): pl.pallas_call(functools.partial(feed_forward, remote), grid=(count // bl...  63.5 us
    pallas_call x4, Pallas kernels, call_attend_forward(): pl.pallas_call(functools.partial(attend_forward, remote, width), grid=(se...  59.5 us
    psum x1, waiting for transfers between devices, per_device(): lax.psum((inner_first(dqkv, tokens), inner_first(saved[0][1], da), sums,...  41.3 us
    pallas_call x1, Pallas kernels, call_middle(): pl.pallas_call(functools.partial(middle, groups), grid=(count // block,),...  39.7 us
    ppermute x6, waiting for transfers between devices, spread(): lax.ppermute(piece, 'tensor', [((i + shift) % groups, i) for i in range(g...  33.9 us
    ppermute x42, waiting for transfers between devices, swap(): return lax.ppermute(value, 'dp', [(i, i ^ mask) for i in range(size)])  28.7 us
    psum x1, blocking collectives, per_device(): lax.psum((inner_first(dqkv, tokens), inner_first(saved[0][1], da), sums,...  25.8 us
  transfers between devices with their start and end apart: 52, of which 13 were waited for; matrix products, arithmetic and copies ran while one was open for 4% of the time, Pallas kernels for 34%

profile of v1, /device:TPU:0, one launch (start us, length us, event | category | flops | bytes accessed | tf_op | source)
XLA Modules:
  0.0 486.4 jit_solution(10370206242545575763)
XLA Ops:
  7.3 1.4 pad_maximum_fusion.rest_0_.w_ref
  8.8 3.1 collective-permute-start.19
  11.9 2.6 collective-permute-start.11
  15.8 6.2 %collective-permute-done.19.rest_1_ = f32[96,768]{1,0:T(8,128)} collective-permute-done((f32[96,768]{1,0:T(8,128)S(1)}, f32[96,768]{1,0:T(8,128)}, u32[]{:S(2)}, u32[]{:S(2)}) %collective-permute-start.19) | collective-permute-done | bytes 294944 | tf_op jit(solution)/shard_map/ppermute | solution.py:408
  22.0 1.8 collective-permute-start.23
  23.7 1.5 collective-permute-start.21
  26.3 12.1 %collective-permute-done.2 = f32[1,1344]{1,0:T(1,128)S(1)} collective-permute-done((f32[1,1344]{1,0:T(1,128)S(1)}, f32[1,1344]{1,0:T(1,128)S(1)}, u32[]{:S(2)}, u32[]{:S(2)}) %collective-permute-start.2) | collective-permute-done | bytes 5408 | tf_op jit(solution)/shard_map/ppermute | solution.py:462
  38.4 4.0 collective-permute-start.1
  42.4 1.6 collective-permute-done.1
  44.0 1.5 collective-permute-start
  45.5 4.0 collective-permute-done
  50.6 1.6 constant_dynamic-slice_fusion
  52.9 1.6 collective-permute-start.7
  55.8 3.8 collective-permute-done.15.rest_5_
  62.8 2.6 collective-permute-done.7.rest_5_
  65.4 4.0 collective-permute-done.5.rest_3_
  70.6 3.0 collective-permute-done.43.rest_1_
  73.7 24.6 %collective-permute-done.35.rest_1_ = f32[192,768]{1,0:T(8,128)} collective-permute-done((f32[192,768]{1,0:T(8,128)S(1)}, f32[192,768]{1,0:T(8,128)}, u32[]{:S(2)}, u32[]{:S(2)}) %collective-permute-start.35) | collective-permute-done | bytes 589856 | tf_op jit(solution)/shard_map/ppermute | solution.py:408
  99.0 1.5 collective-permute-start.9
  101.1 6.9 %collective-permute-done.17.rest_7_ = f32[96,768]{1,0:T(8,128)S(1)} collective-permute-done((f32[96,768]{1,0:T(8,128)}, f32[96,768]{1,0:T(8,128)S(1)}, u32[]{:S(2)}, u32[]{:S(2)}) %collective-permute-start.17) | collective-permute-done | bytes 294944 | tf_op jit(solution)/shard_map/ppermute | solution.py:404
  108.4 1.5 collective-permute-start.45
  111.6 1.5 collective-permute-start.39
  113.8 10.4 %collective-permute-done.47.rest_5_ = f32[192,768]{1,0:T(8,128)S(1)} collective-permute-done((f32[192,768]{1,0:T(8,128)S(1)}, f32[192,768]{1,0:T(8,128)S(1)}, u32[]{:S(2)}, u32[]{:S(2)}) %collective-permute-start.47) | collective-permute-done | bytes 589856 | tf_op jit(solution)/shard_map/ppermute | solution.py:404
  124.3 1.6 collective-permute-start.29
  128.3 3.1 broadcast_in_dim.7.acc_ref
  131.5 14.4 %shard_map.305 = (bf16[2048,576]{1,0:T(8,128)(2,1)}, bf16[2048,192]{1,0:T(8,128)(2,1)}, f32[4,8,512]{2,1,0:T(8,128)}, f32[2048,768]{1,0:T(8,128)}) custom-call(bf16[2048,768]{1,0:T(8,128)(2,1)} %x_ref.9, s32[2048,1]{1,0:T(8,128)} %copy.40.scol_ref, s32[4,1,512]{2,1,0:T(1,128)} %bitcast.35, f32[1,576]{1,0:T(1,128)} %slice.83.bias_ref, ...), custom_call_target="tpu_custom_call" | custom-call | flops 5637144576 | bytes 18874368 | tf_op jit(solution)/shard_map/pallas_call | solution.py:171
  153.8 1.6 collective-permute-start.49
  156.4 15.0 %shard_map.306 = (bf16[2048,576]{1,0:T(8,128)(2,1)}, bf16[2048,192]{1,0:T(8,128)(2,1)}, f32[4,8,512]{2,1,0:T(8,128)}, f32[2048,768]{1,0:T(8,128)}, bf16[768,768]{1,0:T(8,128)(2,1)}) custom-call(bf16[2048,768]{1,0:T(8,128)(2,1)} %x_ref.9, s32[2048,1]{1,0:T(8,128)} %copy.40.scol_ref, s32[4,1,512]{2,1,0:T(1,128)} %bitcast.36, f32[1,576]{1,0:T(1,128)} %slice.82.bias_ref, ...), custom_call_target="tpu_custom_call" | custom-call | flops 5637144576 | bytes 18874368 | tf_op jit(solution)/shard_map/pallas_call | solution.py:171
  171.5 15.1 %shard_map.307 = (bf16[2048,576]{1,0:T(8,128)(2,1)}, bf16[2048,192]{1,0:T(8,128)(2,1)}, f32[4,8,512]{2,1,0:T(8,128)}, f32[2048,768]{1,0:T(8,128)}, bf16[768,768]{1,0:T(8,128)(2,1)}) custom-call(bf16[2048,768]{1,0:T(8,128)(2,1)} %x_ref.9, s32[2048,1]{1,0:T(8,128)} %copy.40.scol_ref, s32[4,1,512]{2,1,0:T(1,128)} %bitcast.37, f32[1,576]{1,0:T(1,128)} %slice.81.bias_ref, ...), custom_call_target="tpu_custom_call" | custom-call | flops 5637144576 | bytes 18874368 | tf_op jit(solution)/shard_map/pallas_call | solution.py:171
  187.8 15.0 %shard_map.308 = (bf16[2048,576]{1,0:T(8,128)(2,1)}, bf16[2048,192]{1,0:T(8,128)(2,1)}, f32[4,8,512]{2,1,0:T(8,128)}, f32[2048,768]{1,0:T(8,128)}, bf16[768,768]{1,0:T(8,128)(2,1)}) custom-call(bf16[2048,768]{1,0:T(8,128)(2,1)} %x_ref.9, s32[2048,1]{1,0:T(8,128)} %copy.40.scol_ref, s32[4,1,512]{2,1,0:T(1,128)} %bitcast.38, f32[1,576]{1,0:T(1,128)} %slice.80.bias_ref, ...), custom_call_target="tpu_custom_call" | custom-call | flops 5637144576 | bytes 18874368 | tf_op jit(solution)/shard_map/pallas_call | solution.py:171
  203.3 16.8 %shard_map.309 = (bf16[2048,768]{1,0:T(8,128)(2,1)}, f32[2048,768]{1,0:T(8,128)}, f32[2048,768]{1,0:T(8,128)}, bf16[2048,768]{1,0:T(8,128)(2,1)}, bf16[2048,768]{1,0:T(8,128)(2,1)}) custom-call(bf16[2048,768]{1,0:T(8,128)(2,1)} %x_ref.9, f32[2048,768]{1,0:T(8,128)} %get-tuple-element.65.acc_ref, f32[1,768]{1,0:T(1,128)} %slice.84.bias_ref, ...), custom_call_target="tpu_custom_call" | custom-call | flops 4831838208 | bytes 22020096 | tf_op jit(solution)/shard_map/pallas_call | solution.py:300
  221.7 15.6 %shard_map.310 = (bf16[2048,768]{1,0:T(8,128)(2,1)}, f32[2048,768]{1,0:T(8,128)}, bf16[768,768]{1,0:T(8,128)(2,1)}, bf16[768,768]{1,0:T(8,128)(2,1)}) custom-call(bf16[2048,768]{1,0:T(8,128)(2,1)} %get-tuple-element.67.x_ref, f32[2048,768]{1,0:T(8,128)} %get-tuple-element.68.acc_ref, f32[1,768]{1,0:T(1,128)} %slice.85.bias_ref, s32[1]{0:T(128)} %bitcast.5.rest_0_, ...), custom_call_target="tpu_custom_call" | custom-call | flops 4831838208 | bytes 22020096 | tf_op jit(solution)/shard_map/pallas_call | solution.py:300
  238.2 15.6 %shard_map.311 = (bf16[2048,768]{1,0:T(8,128)(2,1)}, f32[2048,768]{1,0:T(8,128)}, bf16[768,768]{1,0:T(8,128)(2,1)}, bf16[768,768]{1,0:T(8,128)(2,1)}) custom-call(bf16[2048,768]{1,0:T(8,128)(2,1)} %get-tuple-element.67.x_ref, f32[2048,768]{1,0:T(8,128)} %get-tuple-element.69.acc_ref, f32[1,768]{1,0:T(1,128)} %slice.86.bias_ref, s32[1]{0:T(128)} %bitcast.5.rest_0_, ...), custom_call_target="tpu_custom_call" | custom-call | flops 4831838208 | bytes 22020096 | tf_op jit(solution)/shard_map/pallas_call | solution.py:300
  255.1 15.6 %shard_map.312 = (bf16[2048,768]{1,0:T(8,128)(2,1)}, f32[2048,768]{1,0:T(8,128)}, bf16[768,768]{1,0:T(8,128)(2,1)}, bf16[768,768]{1,0:T(8,128)(2,1)}) custom-call(bf16[2048,768]{1,0:T(8,128)(2,1)} %get-tuple-element.67.x_ref, f32[2048,768]{1,0:T(8,128)} %get-tuple-element.70.acc_ref, f32[1,768]{1,0:T(1,128)} %slice.87.bias_ref, s32[1]{0:T(128)} %bitcast.5.rest_0_, ...), custom_call_target="tpu_custom_call" | custom-call | flops 4831838208 | bytes 22020096 | tf_op jit(solution)/shard_map/pallas_call | solution.py:300
  270.7 39.7 %shard_map.313 = (bf16[2048,768]{1,0:T(8,128)(2,1)}, bf16[2048,768]{1,0:T(8,128)(2,1)}, bf16[2048,768]{1,0:T(8,128)(2,1)}, f32[2048,768]{1,0:T(8,128)}, bf16[2048,768]{1,0:T(8,128)(2,1)}, /*index=5*/f32[8,768]{1,0:T(8,128)}) custom-call(f32[2048,768]{1,0:T(8,128)} %get-tuple-element.66.h1_ref, f32[2048,768]{1,0:T(8,128)} %get-tuple-element.71.m_ref, ...), custom_call_target="tpu_custom_call" | custom-call | flops 19327352832 | bytes 47185920 | tf_op jit(solution)/shard_map/pallas_call | solution.py:386
  310.4 6.1 %fusion.3 = f32[768,768]{1,0:T(8,128)} fusion(bf16[2048,768]{1,0:T(8,128)(2,1)S(1)} %copy-done.61, bf16[2048,768]{1,0:T(8,128)(2,1)} %get-tuple-element.104), kind=kOutput, calls=%fused_computation.19 | convolution fusion | flops 2415919104 | bytes 8650752 | tf_op jit(solution)/shard_map/dot_general | solution.py:400
  316.5 1.6 fusion.2
  318.2 19.0 %shard_map.314 = (f32[2048,768]{1,0:T(8,128)}, bf16[2048,576]{1,0:T(8,128)(2,1)}, f32[8,576]{1,0:T(8,128)}) custom-call(bf16[2048,576]{1,0:T(8,128)(2,1)} %get-tuple-element.96.qkv_ref, bf16[2048,192]{1,0:T(8,128)(2,1)} %get-tuple-element.97.c_ref, f32[4,8,512]{2,1,0:T(8,128)} %get-tuple-element.98.l_ref, s32[2048,1]{1,0:T(8,128)} %copy.40.scol_ref, ...), custom_call_target="tpu_custom_call" | custom-call | flops 10468982784 | bytes 18874368 | tf_op jit(solution)/shard_map/pallas_call | solution.py:208
  337.3 5.2 %fusion.1 = f32[576,768]{1,0:T(8,128)} fusion(bf16[2048,576]{1,0:T(8,128)(2,1)} %get-tuple-element.101, bf16[2048,768]{1,0:T(8,128)(2,1)S(1)} %copy-done.24), kind=kOutput, calls=%fused_computation.17 | convolution fusion | flops 1811939328 | bytes 7274496 | tf_op jit(solution)/shard_map/dot_general | solution.py:400
  342.5 4.2 fusion.4
  347.4 25.8 %all-reduce = (f32[8,576]{1,0:T(8,128)S(1)}, f32[8,768]{1,0:T(8,128)S(1)}) all-reduce(f32[8,576]{1,0:T(8,128)S(1)} %copy-done.7, f32[8,768]{1,0:T(8,128)S(1)} %copy-done.6), channel_id=1, replica_groups=mesh['dp'=8,'tensor'=4] {'dp'}, use_global_device_ids=true, to_apply=%region_1.2 | all-reduce | flops 10752 | bytes 86016 | tf_op jit(solution)/shard_map/psum | solution.py:511
  374.4 18.6 %shard_map.315.acc_ref = f32[2048,768]{1,0:T(8,128)} custom-call(bf16[2048,576]{1,0:T(8,128)(2,1)} %get-tuple-element.92.qkv_ref, bf16[2048,192]{1,0:T(8,128)(2,1)} %get-tuple-element.93.c_ref, f32[4,8,512]{2,1,0:T(8,128)} %get-tuple-element.94.l_ref, s32[2048,1]{1,0:T(8,128)} %copy.40.scol_ref, s32[4,1,512]{2,1,0:T(1,128)} %bitcast.40, ...), custom_call_target="tpu_custom_call" | custom-call | flops 10468982784 | bytes 18874368 | tf_op jit(solution)/shard_map/pallas_call | solution.py:208
  393.1 18.6 %shard_map.316.acc_ref = f32[2048,768]{1,0:T(8,128)} custom-call(bf16[2048,576]{1,0:T(8,128)(2,1)} %get-tuple-element.88.qkv_ref, bf16[2048,192]{1,0:T(8,128)(2,1)} %get-tuple-element.89.c_ref, f32[4,8,512]{2,1,0:T(8,128)} %get-tuple-element.90.l_ref, s32[2048,1]{1,0:T(8,128)} %copy.40.scol_ref, s32[4,1,512]{2,1,0:T(1,128)} %bitcast.41, ...), custom_call_target="tpu_custom_call" | custom-call | flops 10468982784 | bytes 18874368 | tf_op jit(solution)/shard_map/pallas_call | solution.py:208
  411.7 18.5 %shard_map.317 = f32[2048,768]{1,0:T(8,128)} custom-call(bf16[2048,576]{1,0:T(8,128)(2,1)} %get-tuple-element.83.qkv_ref, bf16[2048,192]{1,0:T(8,128)(2,1)} %get-tuple-element.84.c_ref, f32[4,8,512]{2,1,0:T(8,128)} %get-tuple-element.85.l_ref, s32[2048,1]{1,0:T(8,128)} %copy.40.scol_ref, s32[4,1,512]{2,1,0:T(1,128)} %bitcast.42, ...), custom_call_target="tpu_custom_call" | custom-call | flops 10468982784 | bytes 18874368 | tf_op jit(solution)/shard_map/pallas_call | solution.py:208
  430.2 41.3 %all-reduce.4.cloned.1.call-done = (f32[576,768]{1,0:T(8,128)}, f32[192,768]{1,0:T(8,128)}, f32[768,768]{1,0:T(8,128)}, f32[768,768]{1,0:T(8,128)}) async-done(((f32[576,768]{1,0:T(8,128)}, f32[192,768]{1,0:T(8,128)}, f32[768,768]{1,0:T(8,128)}, f32[768,768]{1,0:T(8,128)}), (f32[576,768]{1,0:T(8,128)}, f32[192,768]{1,0:T(8,128)}, f32[768,768]{1,0:T(8,128)}, ...) | async-done | bytes 7077904 | tf_op jit(solution)/shard_map/psum | solution.py:511
  471.5 2.8 slice_bitcast_fusion
  475.2 1.4 copy.52
  477.7 1.4 copy.53
  (233 shorter events, 35.0 us)
Async XLA Ops:
  7.2 464.3 %all-reduce.4.cloned.1.call-start = ((), (), s32[]{:S(2)}) async-start(), calls=%async_computation | async-start | bytes 14155776 | tf_op jit(solution)/shard_map/psum | solution.py:511
  8.8 13.2 %collective-permute-start.19 = (f32[96,768]{1,0:T(8,128)S(1)}, f32[96,768]{1,0:T(8,128)}, u32[]{:S(2)}, u32[]{:S(2)}) collective-permute-start(f32[96,768]{1,0:T(8,128)S(1)} %bitcast_convert_fusion), channel_id=1, source_target_pairs={{3,0},{0,1},{1,2},{2,3},{7,4},{4,5},{5,6},{6,7},{11,8},{8,9},{9,10... | collective-permute-start | bytes 884744 | tf_op jit(solution)/shard_map/ppermute | solution.py:408
  11.9 37.6 %collective-permute-start.11 = (f32[96,768]{1,0:T(8,128)S(1)}, f32[96,768]{1,0:T(8,128)}, u32[]{:S(2)}, u32[]{:S(2)}) collective-permute-start(f32[96,768]{1,0:T(8,128)S(1)} %bitcast_convert_fusion), channel_id=1, source_target_pairs={{2,0},{3,1},{0,2},{1,3},{6,4},{7,5},{4,6},{5,7},{10,8},{11,9},{8,1... | collective-permute-start | bytes 884744 | tf_op jit(solution)/shard_map/ppermute | solution.py:408
  14.4 35.6 %collective-permute-start.3 = (f32[96,768]{1,0:T(8,128)S(1)}, f32[96,768]{1,0:T(8,128)}, u32[]{:S(2)}, u32[]{:S(2)}) collective-permute-start(f32[96,768]{1,0:T(8,128)S(1)} %bitcast_convert_fusion), channel_id=1, source_target_pairs={{1,0},{2,1},{3,2},{0,3},{5,4},{6,5},{7,6},{4,7},{9,8},{10,9},{11,1... | collective-permute-start | bytes 884744 | tf_op jit(solution)/shard_map/ppermute | solution.py:408
  22.0 30.8 %collective-permute-start.23 = (f32[96,768]{1,0:T(8,128)}, f32[96,768]{1,0:T(8,128)}, u32[]{:S(2)}, u32[]{:S(2)}) collective-permute-start(f32[96,768]{1,0:T(8,128)} %collective-permute-done.19.rest_1_), channel_id=1, source_target_pairs={{0,16},{4,20},{8,24},{12,28},{16,0},{20,4},{24,8},{28,12},{1,17},{... | collective-permute-start | bytes 884744 | tf_op jit(solution)/shard_map/ppermute | solution.py:404
  23.7 29.2 %collective-permute-start.21 = (f32[96,768]{1,0:T(8,128)}, f32[96,768]{1,0:T(8,128)}, u32[]{:S(2)}, u32[]{:S(2)}) collective-permute-start(f32[96,768]{1,0:T(8,128)} %collective-permute-done.19.rest_1_), channel_id=1, source_target_pairs={{0,8},{4,12},{8,0},{12,4},{16,24},{20,28},{24,16},{28,20},{1,9},{5... | collective-permute-start | bytes 884744 | tf_op jit(solution)/shard_map/ppermute | solution.py:404
  25.3 13.0 %collective-permute-start.2 = (f32[1,1344]{1,0:T(1,128)S(1)}, f32[1,1344]{1,0:T(1,128)S(1)}, u32[]{:S(2)}, u32[]{:S(2)}) collective-permute-start(f32[1,1344]{1,0:T(1,128)S(1)} %reshape.74), channel_id=1, source_target_pairs={{1,0},{2,1},{3,2},{0,3},{5,4},{6,5},{7,6},{4,7},{9,8},{10,9},{11,1... | collective-permute-start | bytes 16136 | tf_op jit(solution)/shard_map/ppermute | solution.py:462
  38.4 5.6 %collective-permute-start.1 = (f32[1,1344]{1,0:T(1,128)S(1)}, f32[1,1344]{1,0:T(1,128)S(1)}, u32[]{:S(2)}, u32[]{:S(2)}) collective-permute-start(f32[1,1344]{1,0:T(1,128)S(1)} %reshape.74), channel_id=1, source_target_pairs={{2,0},{3,1},{0,2},{1,3},{6,4},{7,5},{4,6},{5,7},{10,8},{11,9},{8,1... | collective-permute-start | bytes 16136 | tf_op jit(solution)/shard_map/ppermute | solution.py:462
  44.0 5.4 %collective-permute-start = (f32[1,1344]{1,0:T(1,128)S(1)}, f32[1,1344]{1,0:T(1,128)S(1)}, u32[]{:S(2)}, u32[]{:S(2)}) collective-permute-start(f32[1,1344]{1,0:T(1,128)S(1)} %reshape.74), channel_id=1, source_target_pairs={{3,0},{0,1},{1,2},{2,3},{7,4},{4,5},{5,6},{6,7},{11,8},{8,9},{9,10... | collective-permute-start | bytes 16136 | tf_op jit(solution)/shard_map/ppermute | solution.py:462
  49.4 6.0 %collective-permute-start.20 = (f32[96,768]{1,0:T(8,128)}, f32[96,768]{1,0:T(8,128)}, u32[]{:S(2)}, u32[]{:S(2)}) collective-permute-start(f32[96,768]{1,0:T(8,128)} %collective-permute-done.19.rest_1_), channel_id=1, source_target_pairs={{0,4},{4,0},{8,12},{12,8},{16,20},{20,16},{24,28},{28,24},{1,5},{5... | collective-permute-start | bytes 884744 | tf_op jit(solution)/shard_map/ppermute | solution.py:404
  49.5 10.2 %collective-permute-start.15 = (f32[96,768]{1,0:T(8,128)}, f32[96,768]{1,0:T(8,128)}, u32[]{:S(2)}, u32[]{:S(2)}) collective-permute-start(f32[96,768]{1,0:T(8,128)} %collective-permute-done.11.rest_1_), channel_id=1, source_target_pairs={{0,16},{4,20},{8,24},{12,28},{16,0},{20,4},{24,8},{28,12},{1,17},{... | collective-permute-start | bytes 884744 | tf_op jit(solution)/shard_map/ppermute | solution.py:404
  50.0 10.7 %collective-permute-start.13 = (f32[96,768]{1,0:T(8,128)}, f32[96,768]{1,0:T(8,128)}, u32[]{:S(2)}, u32[]{:S(2)}) collective-permute-start(f32[96,768]{1,0:T(8,128)} %collective-permute-done.11.rest_1_), channel_id=1, source_target_pairs={{0,8},{4,12},{8,0},{12,4},{16,24},{20,28},{24,16},{28,20},{1,9},{5... | collective-permute-start | bytes 884744 | tf_op jit(solution)/shard_map/ppermute | solution.py:404
  52.8 8.9 %collective-permute-start.12 = (f32[96,768]{1,0:T(8,128)}, f32[96,768]{1,0:T(8,128)S(1)}, u32[]{:S(2)}, u32[]{:S(2)}) collective-permute-start(f32[96,768]{1,0:T(8,128)} %collective-permute-done.11.rest_1_), channel_id=1, source_target_pairs={{0,4},{4,0},{8,12},{12,8},{16,20},{20,16},{24,28},{28,24},{1,5},{5... | collective-permute-start | bytes 884744 | tf_op jit(solution)/shard_map/ppermute | solution.py:404
  52.9 12.5 %collective-permute-start.7 = (f32[96,768]{1,0:T(8,128)}, f32[96,768]{1,0:T(8,128)S(1)}, u32[]{:S(2)}, u32[]{:S(2)}) collective-permute-start(f32[96,768]{1,0:T(8,128)} %collective-permute-done.3.rest_1_), channel_id=1, source_target_pairs={{0,16},{4,20},{8,24},{12,28},{16,0},{20,4},{24,8},{28,12},{1,17},{... | collective-permute-start | bytes 884744 | tf_op jit(solution)/shard_map/ppermute | solution.py:404
  55.5 18.2 %collective-permute-start.43 = (f32[192,768]{1,0:T(8,128)S(1)}, f32[192,768]{1,0:T(8,128)S(1)}, u32[]{:S(2)}, u32[]{:S(2)}) collective-permute-start(f32[192,768]{1,0:T(8,128)S(1)} %maximum_convert_fusion), channel_id=1, source_target_pairs={{3,0},{0,1},{1,2},{2,3},{7,4},{4,5},{5,6},{6,7},{11,8},{8,9},{9,10... | collective-permute-start | bytes 1769480 | tf_op jit(solution)/shard_map/ppermute | solution.py:408
  59.6 38.6 %collective-permute-start.35 = (f32[192,768]{1,0:T(8,128)S(1)}, f32[192,768]{1,0:T(8,128)}, u32[]{:S(2)}, u32[]{:S(2)}) collective-permute-start(f32[192,768]{1,0:T(8,128)S(1)} %maximum_convert_fusion), channel_id=1, source_target_pairs={{2,0},{3,1},{0,2},{1,3},{6,4},{7,5},{4,6},{5,7},{10,8},{11,9},{8,1... | collective-permute-start | bytes 1769480 | tf_op jit(solution)/shard_map/ppermute | solution.py:408
  60.8 37.5 %collective-permute-start.27 = (f32[192,768]{1,0:T(8,128)S(1)}, f32[192,768]{1,0:T(8,128)}, u32[]{:S(2)}, u32[]{:S(2)}) collective-permute-start(f32[192,768]{1,0:T(8,128)S(1)} %maximum_convert_fusion), channel_id=1, source_target_pairs={{1,0},{2,1},{3,2},{0,3},{5,4},{6,5},{7,6},{4,7},{9,8},{10,9},{11,1... | collective-permute-start | bytes 1769480 | tf_op jit(solution)/shard_map/ppermute | solution.py:408
  61.7 7.8 %collective-permute-start.5 = (f32[96,768]{1,0:T(8,128)}, f32[96,768]{1,0:T(8,128)S(1)}, u32[]{:S(2)}, u32[]{:S(2)}) collective-permute-start(f32[96,768]{1,0:T(8,128)} %collective-permute-done.3.rest_1_), channel_id=1, source_target_pairs={{0,8},{4,12},{8,0},{12,4},{16,24},{20,28},{24,16},{28,20},{1,9},{5... | collective-permute-start | bytes 884744 | tf_op jit(solution)/shard_map/ppermute | solution.py:404
  65.4 5.2 %collective-permute-start.4 = (f32[96,768]{1,0:T(8,128)}, f32[96,768]{1,0:T(8,128)}, u32[]{:S(2)}, u32[]{:S(2)}) collective-permute-start(f32[96,768]{1,0:T(8,128)} %collective-permute-done.3.rest_1_), channel_id=1, source_target_pairs={{0,4},{4,0},{8,12},{12,8},{16,20},{20,16},{24,28},{28,24},{1,5},{5... | collective-permute-start | bytes 884744 | tf_op jit(solution)/shard_map/ppermute | solution.py:404
  69.4 29.4 %collective-permute-start.25 = (f32[96,768]{1,0:T(8,128)}, f32[96,768]{1,0:T(8,128)S(1)}, u32[]{:S(2)}, u32[]{:S(2)}) collective-permute-start(f32[96,768]{1,0:T(8,128)} %collective-permute-done.23.rest_5_), channel_id=1, source_target_pairs={{0,8},{4,12},{8,0},{12,4},{16,24},{20,28},{24,16},{28,20},{1,9},{5... | collective-permute-start | bytes 884744 | tf_op jit(solution)/shard_map/ppermute | solution.py:404
  70.6 28.4 %collective-permute-start.24 = (f32[96,768]{1,0:T(8,128)}, f32[96,768]{1,0:T(8,128)S(1)}, u32[]{:S(2)}, u32[]{:S(2)}) collective-permute-start(f32[96,768]{1,0:T(8,128)} %collective-permute-done.23.rest_5_), channel_id=1, source_target_pairs={{0,4},{4,0},{8,12},{12,8},{16,20},{20,16},{24,28},{28,24},{1,5},{5... | collective-permute-start | bytes 884744 | tf_op jit(solution)/shard_map/ppermute | solution.py:404
  73.6 26.9 %collective-permute-start.22 = (f32[96,768]{1,0:T(8,128)}, f32[96,768]{1,0:T(8,128)S(1)}, u32[]{:S(2)}, u32[]{:S(2)}) collective-permute-start(f32[96,768]{1,0:T(8,128)} %collective-permute-done.21.rest_3_), channel_id=1, source_target_pairs={{0,4},{4,0},{8,12},{12,8},{16,20},{20,16},{24,28},{28,24},{1,5},{5... | collective-permute-start | bytes 884744 | tf_op jit(solution)/shard_map/ppermute | solution.py:404
  98.3 9.6 %collective-permute-start.17 = (f32[96,768]{1,0:T(8,128)}, f32[96,768]{1,0:T(8,128)S(1)}, u32[]{:S(2)}, u32[]{:S(2)}) collective-permute-start(f32[96,768]{1,0:T(8,128)} %collective-permute-done.13.rest_3_), channel_id=1, source_target_pairs={{0,16},{4,20},{8,24},{12,28},{16,0},{20,4},{24,8},{28,12},{1,17},{... | collective-permute-start | bytes 884744 | tf_op jit(solution)/shard_map/ppermute | solution.py:404
  98.8 9.6 %collective-permute-start.14 = (f32[96,768]{1,0:T(8,128)}, f32[96,768]{1,0:T(8,128)S(1)}, u32[]{:S(2)}, u32[]{:S(2)}) collective-permute-start(f32[96,768]{1,0:T(8,128)} %collective-permute-done.13.rest_3_), channel_id=1, source_target_pairs={{0,4},{4,0},{8,12},{12,8},{16,20},{20,16},{24,28},{28,24},{1,5},{5... | collective-permute-start | bytes 884744 | tf_op jit(solution)/shard_map/ppermute | solution.py:404
  99.0 10.9 %collective-permute-start.9 = (f32[96,768]{1,0:T(8,128)S(1)}, f32[96,768]{1,0:T(8,128)S(1)}, u32[]{:S(2)}, u32[]{:S(2)}) collective-permute-start(f32[96,768]{1,0:T(8,128)S(1)} %collective-permute-done.7.rest_5_), channel_id=1, source_target_pairs={{0,8},{4,12},{8,0},{12,4},{16,24},{20,28},{24,16},{28,20},{1,9},{5... | collective-permute-start | bytes 884744 | tf_op jit(solution)/shard_map/ppermute | solution.py:404
  100.5 9.5 %collective-permute-start.8 = (f32[96,768]{1,0:T(8,128)S(1)}, f32[96,768]{1,0:T(8,128)S(1)}, u32[]{:S(2)}, u32[]{:S(2)}) collective-permute-start(f32[96,768]{1,0:T(8,128)S(1)} %collective-permute-done.7.rest_5_), channel_id=1, source_target_pairs={{0,4},{4,0},{8,12},{12,8},{16,20},{20,16},{24,28},{28,24},{1,5},{5... | collective-permute-start | bytes 884744 | tf_op jit(solution)/shard_map/ppermute | solution.py:404
  100.6 10.0 %collective-permute-start.6 = (f32[96,768]{1,0:T(8,128)S(1)}, f32[96,768]{1,0:T(8,128)S(1)}, u32[]{:S(2)}, u32[]{:S(2)}) collective-permute-start(f32[96,768]{1,0:T(8,128)S(1)} %collective-permute-done.5.rest_3_), channel_id=1, source_target_pairs={{0,4},{4,0},{8,12},{12,8},{16,20},{20,16},{24,28},{28,24},{1,5},{5... | collective-permute-start | bytes 884744 | tf_op jit(solution)/shard_map/ppermute | solution.py:404
  107.9 16.2 %collective-permute-start.47 = (f32[192,768]{1,0:T(8,128)S(1)}, f32[192,768]{1,0:T(8,128)S(1)}, u32[]{:S(2)}, u32[]{:S(2)}) collective-permute-start(f32[192,768]{1,0:T(8,128)S(1)} %collective-permute-done.43.rest_1_), channel_id=1, source_target_pairs={{0,16},{4,20},{8,24},{12,28},{16,0},{20,4},{24,8},{28,12},{1,17},{... | collective-permute-start | bytes 1769480 | tf_op jit(solution)/shard_map/ppermute | solution.py:404
  108.4 19.4 %collective-permute-start.45 = (f32[192,768]{1,0:T(8,128)S(1)}, f32[192,768]{1,0:T(8,128)}, u32[]{:S(2)}, u32[]{:S(2)}) collective-permute-start(f32[192,768]{1,0:T(8,128)S(1)} %collective-permute-done.43.rest_1_), channel_id=1, source_target_pairs={{0,8},{4,12},{8,0},{12,4},{16,24},{20,28},{24,16},{28,20},{1,9},{5... | collective-permute-start | bytes 1769480 | tf_op jit(solution)/shard_map/ppermute | solution.py:404
  111.6 42.2 %collective-permute-start.39 = (f32[192,768]{1,0:T(8,128)}, f32[192,768]{1,0:T(8,128)}, u32[]{:S(2)}, u32[]{:S(2)}) collective-permute-start(f32[192,768]{1,0:T(8,128)} %collective-permute-done.35.rest_1_), channel_id=1, source_target_pairs={{0,16},{4,20},{8,24},{12,28},{16,0},{20,4},{24,8},{28,12},{1,17},{... | collective-permute-start | bytes 1769480 | tf_op jit(solution)/shard_map/ppermute | solution.py:404
  113.1 40.7 %collective-permute-start.37 = (f32[192,768]{1,0:T(8,128)}, f32[192,768]{1,0:T(8,128)}, u32[]{:S(2)}, u32[]{:S(2)}) collective-permute-start(f32[192,768]{1,0:T(8,128)} %collective-permute-done.35.rest_1_), channel_id=1, source_target_pairs={{0,8},{4,12},{8,0},{12,4},{16,24},{20,28},{24,16},{28,20},{1,9},{5... | collective-permute-start | bytes 1769480 | tf_op jit(solution)/shard_map/ppermute | solution.py:404
  113.8 41.6 %collective-permute-start.36 = (f32[192,768]{1,0:T(8,128)}, f32[192,768]{1,0:T(8,128)}, u32[]{:S(2)}, u32[]{:S(2)}) collective-permute-start(f32[192,768]{1,0:T(8,128)} %collective-permute-done.35.rest_1_), channel_id=1, source_target_pairs={{0,4},{4,0},{8,12},{12,8},{16,20},{20,16},{24,28},{28,24},{1,5},{5... | collective-permute-start | bytes 1769480 | tf_op jit(solution)/shard_map/ppermute | solution.py:404
  124.3 31.7 %collective-permute-start.29 = (f32[192,768]{1,0:T(8,128)}, f32[192,768]{1,0:T(8,128)}, u32[]{:S(2)}, u32[]{:S(2)}) collective-permute-start(f32[192,768]{1,0:T(8,128)} %collective-permute-done.27.rest_1_), channel_id=1, source_target_pairs={{0,8},{4,12},{8,0},{12,4},{16,24},{20,28},{24,16},{28,20},{1,9},{5... | collective-permute-start | bytes 1769480 | tf_op jit(solution)/shard_map/ppermute | solution.py:404
  127.8 43.6 %collective-permute-start.31 = (f32[192,768]{1,0:T(8,128)}, f32[192,768]{1,0:T(8,128)S(1)}, u32[]{:S(2)}, u32[]{:S(2)}) collective-permute-start(f32[192,768]{1,0:T(8,128)} %collective-permute-done.27.rest_1_), channel_id=1, source_target_pairs={{0,16},{4,20},{8,24},{12,28},{16,0},{20,4},{24,8},{28,12},{1,17},{... | collective-permute-start | bytes 1769480 | tf_op jit(solution)/shard_map/ppermute | solution.py:404
  153.8 32.8 %collective-permute-start.28 = (f32[192,768]{1,0:T(8,128)}, f32[192,768]{1,0:T(8,128)S(1)}, u32[]{:S(2)}, u32[]{:S(2)}) collective-permute-start(f32[192,768]{1,0:T(8,128)} %collective-permute-done.27.rest_1_), channel_id=1, source_target_pairs={{0,4},{4,0},{8,12},{12,8},{16,20},{20,16},{24,28},{28,24},{1,5},{5... | collective-permute-start | bytes 1769480 | tf_op jit(solution)/shard_map/ppermute | solution.py:404
  153.8 33.3 %collective-permute-start.49 = (f32[192,768]{1,0:T(8,128)}, f32[192,768]{1,0:T(8,128)S(1)}, u32[]{:S(2)}, u32[]{:S(2)}) collective-permute-start(f32[192,768]{1,0:T(8,128)} %collective-permute-done.45.rest_3_), channel_id=1, source_target_pairs={{0,16},{4,20},{8,24},{12,28},{16,0},{20,4},{24,8},{28,12},{1,17},{... | collective-permute-start | bytes 1769480 | tf_op jit(solution)/shard_map/ppermute | solution.py:404
  155.4 31.8 %collective-permute-start.41 = (f32[192,768]{1,0:T(8,128)}, f32[192,768]{1,0:T(8,128)S(1)}, u32[]{:S(2)}, u32[]{:S(2)}) collective-permute-start(f32[192,768]{1,0:T(8,128)} %collective-permute-done.39.rest_5_), channel_id=1, source_target_pairs={{0,8},{4,12},{8,0},{12,4},{16,24},{20,28},{24,16},{28,20},{1,9},{5... | collective-permute-start | bytes 1769480 | tf_op jit(solution)/shard_map/ppermute | solution.py:404
  155.9 31.7 %collective-permute-start.33 = (f32[192,768]{1,0:T(8,128)}, f32[192,768]{1,0:T(8,128)S(1)}, u32[]{:S(2)}, u32[]{:S(2)}) collective-permute-start(f32[192,768]{1,0:T(8,128)} %collective-permute-done.29.rest_3_), channel_id=1, source_target_pairs={{0,16},{4,20},{8,24},{12,28},{16,0},{20,4},{24,8},{28,12},{1,17},{... | collective-permute-start | bytes 1769480 | tf_op jit(solution)/shard_map/ppermute | solution.py:404
  171.4 31.4 %collective-permute-start.40 = (f32[192,768]{1,0:T(8,128)}, f32[192,768]{1,0:T(8,128)S(1)}, u32[]{:S(2)}, u32[]{:S(2)}) collective-permute-start(f32[192,768]{1,0:T(8,128)} %collective-permute-done.39.rest_5_), channel_id=1, source_target_pairs={{0,4},{4,0},{8,12},{12,8},{16,20},{20,16},{24,28},{28,24},{1,5},{5... | collective-permute-start | bytes 1769480 | tf_op jit(solution)/shard_map/ppermute | solution.py:404
  186.6 34.0 %collective-permute-start.30 = (f32[192,768]{1,0:T(8,128)}, f32[192,768]{1,0:T(8,128)S(1)}, u32[]{:S(2)}, u32[]{:S(2)}) collective-permute-start(f32[192,768]{1,0:T(8,128)} %collective-permute-done.29.rest_3_), channel_id=1, source_target_pairs={{0,4},{4,0},{8,12},{12,8},{16,20},{20,16},{24,28},{28,24},{1,5},{5... | collective-permute-start | bytes 1769480 | tf_op jit(solution)/shard_map/ppermute | solution.py:404
  187.1 33.0 %collective-permute-start.38 = (f32[192,768]{1,0:T(8,128)}, f32[192,768]{1,0:T(8,128)S(1)}, u32[]{:S(2)}, u32[]{:S(2)}) collective-permute-start(f32[192,768]{1,0:T(8,128)} %collective-permute-done.37.rest_3_), channel_id=1, source_target_pairs={{0,4},{4,0},{8,12},{12,8},{16,20},{20,16},{24,28},{28,24},{1,5},{5... | collective-permute-start | bytes 1769480 | tf_op jit(solution)/shard_map/ppermute | solution.py:404
  187.2 33.1 %collective-permute-start.32 = (f32[192,768]{1,0:T(8,128)S(1)}, f32[192,768]{1,0:T(8,128)S(1)}, u32[]{:S(2)}, u32[]{:S(2)}) collective-permute-start(f32[192,768]{1,0:T(8,128)S(1)} %collective-permute-done.31.rest_5_), channel_id=1, source_target_pairs={{0,4},{4,0},{8,12},{12,8},{16,20},{20,16},{24,28},{28,24},{1,5},{5... | collective-permute-start | bytes 1769480 | tf_op jit(solution)/shard_map/ppermute | solution.py:404
  187.7 33.2 %collective-permute-start.34 = (f32[192,768]{1,0:T(8,128)S(1)}, f32[192,768]{1,0:T(8,128)S(1)}, u32[]{:S(2)}, u32[]{:S(2)}) collective-permute-start(f32[192,768]{1,0:T(8,128)S(1)} %collective-permute-done.33.rest_7_), channel_id=1, source_target_pairs={{0,4},{4,0},{8,12},{12,8},{16,20},{20,16},{24,28},{28,24},{1,5},{5... | collective-permute-start | bytes 1769480 | tf_op jit(solution)/shard_map/ppermute | solution.py:404
  202.9 34.5 %collective-permute-start.42 = (f32[192,768]{1,0:T(8,128)S(1)}, f32[192,768]{1,0:T(8,128)S(1)}, u32[]{:S(2)}, u32[]{:S(2)}) collective-permute-start(f32[192,768]{1,0:T(8,128)S(1)} %collective-permute-done.41.rest_7_), channel_id=1, source_target_pairs={{0,4},{4,0},{8,12},{12,8},{16,20},{20,16},{24,28},{28,24},{1,5},{5... | collective-permute-start | bytes 1769480 | tf_op jit(solution)/shard_map/ppermute | solution.py:404
  220.1 33.6 %collective-permute-start.44 = (f32[192,768]{1,0:T(8,128)S(1)}, f32[192,768]{1,0:T(8,128)S(1)}, u32[]{:S(2)}, u32[]{:S(2)}) collective-permute-start(f32[192,768]{1,0:T(8,128)S(1)} %collective-permute-done.43.rest_1_), channel_id=1, source_target_pairs={{0,4},{4,0},{8,12},{12,8},{16,20},{20,16},{24,28},{28,24},{1,5},{5... | collective-permute-start | bytes 1769480 | tf_op jit(solution)/shard_map/ppermute | solution.py:404
  220.3 33.4 %collective-permute-start.46 = (f32[192,768]{1,0:T(8,128)}, f32[192,768]{1,0:T(8,128)S(1)}, u32[]{:S(2)}, u32[]{:S(2)}) collective-permute-start(f32[192,768]{1,0:T(8,128)} %collective-permute-done.45.rest_3_), channel_id=1, source_target_pairs={{0,4},{4,0},{8,12},{12,8},{16,20},{20,16},{24,28},{28,24},{1,5},{5... | collective-permute-start | bytes 1769480 | tf_op jit(solution)/shard_map/ppermute | solution.py:404
  220.7 33.1 %collective-permute-start.48 = (f32[192,768]{1,0:T(8,128)S(1)}, f32[192,768]{1,0:T(8,128)S(1)}, u32[]{:S(2)}, u32[]{:S(2)}) collective-permute-start(f32[192,768]{1,0:T(8,128)S(1)} %copy-done.27), channel_id=1, source_target_pairs={{0,4},{4,0},{8,12},{12,8},{16,20},{20,16},{24,28},{28,24},{1,5},{5... | collective-permute-start | bytes 1769480 | tf_op jit(solution)/shard_map/ppermute | solution.py:404
  220.9 32.9 %collective-permute-start.50 = (f32[192,768]{1,0:T(8,128)S(1)}, f32[192,768]{1,0:T(8,128)S(1)}, u32[]{:S(2)}, u32[]{:S(2)}) collective-permute-start(f32[192,768]{1,0:T(8,128)S(1)} %collective-permute-done.49.rest_7_), channel_id=1, source_target_pairs={{0,4},{4,0},{8,12},{12,8},{16,20},{20,16},{24,28},{28,24},{1,5},{5... | collective-permute-start | bytes 1769480 | tf_op jit(solution)/shard_map/ppermute | solution.py:404
  (67 other events, 1371.6 us)
Sparse Core Ops, SparseCore 0:
  346.8 124.7 all-reduce.3

commit v2 on v1

v2 whole, which is shorter than its diff:
```python
import functools
import math

import jax
import jax.numpy as jnp
from jax import lax
from jax.experimental import pallas as pl
from jax.experimental.pallas import tpu as pltpu
from jax.sharding import PartitionSpec as P

HEAD_DIM = 64
SEQ_LEN = 512
EPS = 1e-06
MASKED = -1000000000.0
LANES = 8
LOW = jnp.bfloat16
WIDE = jnp.float32
VMEM_LIMIT = 56 * 1024 * 1024

NN = (((1,), (0,)), ((), ()))
NT = (((1,), (1,)), ((), ()))


def dot(left, right, dims):
    return lax.dot_general(left, right, dims, preferred_element_type=WIDE)


def params(**kw):
    return pltpu.CompilerParams(vmem_limit_bytes=VMEM_LIMIT, **kw)


def cost(count):
    return pl.CostEstimate(flops=7_500_000 * count, bytes_accessed=8192 * count, transcendentals=0)


def whole(shape):
    zeros = (0,) * len(shape)
    return pl.BlockSpec(shape, lambda i: zeros)


def rows(block, width):
    return pl.BlockSpec((block, width), lambda i: (i, 0))


def head_mask(width, head):
    lane = lax.broadcasted_iota(jnp.int32, (1, width), 1)
    return (lane >= head * HEAD_DIM) & (lane < (head + 1) * HEAD_DIM)


def same_document(seg_col, seg_row):
    return jnp.where(seg_col == seg_row, jnp.float32(3e38), jnp.float32(MASKED))


def attend_forward(remote, width, x_ref, scol_ref, srow_ref, *rest):
    if remote:
        place_ref, slices, rest = rest[0], rest[1 : 1 + LANES], rest[1 + LANES :]
        qkv_ref, c_ref, l_ref, w_ref, wide_ref = rest
        part = width // LANES
        bias = slices[0][4 * part : 4 * part + 1, : 3 * width]

        @pl.when(pl.program_id(0) == 0)
        def _():
            here = place_ref[0]
            for m in range(LANES):
                spot = here ^ m
                for t in range(4):
                    at = pl.multiple_of(t * width + spot * part, 8)
                    wide_ref[pl.ds(at, part), :] = slices[m][t * part : (t + 1) * part, :]
            w_ref[...] = wide_ref[...].astype(LOW)
    else:
        bias_ref, w_ref, qkv_ref, c_ref, l_ref = rest
        bias = bias_ref[...]
    heads = width // HEAD_DIM
    qkv = dot(x_ref[...], w_ref[: 3 * width, :], NT) + bias
    qkv = qkv.astype(LOW)
    qkv_ref[...] = qkv
    queries = qkv[:, :width] * LOW(HEAD_DIM**-0.5)
    keys = qkv[:, width : 2 * width]
    values_t = qkv[:, 2 * width :].T
    limit = same_document(scol_ref[...], srow_ref[0])
    parts = []
    for h in range(heads):
        key_h = jnp.where(head_mask(width, h), keys, LOW(0))
        scores = jnp.minimum(dot(key_h, queries, NT), limit)
        top = jnp.max(scores, axis=0, keepdims=True)
        weights = jnp.exp(scores - top)
        total = jnp.sum(weights, axis=0, keepdims=True)
        l_ref[0, h : h + 1, :] = top + jnp.log(total)
        value_h = values_t[h * HEAD_DIM : (h + 1) * HEAD_DIM, :]
        parts.append(dot(value_h, weights.astype(LOW), NN) / total)
    c_ref[...] = jnp.concatenate(parts, axis=0).T.astype(LOW)


def attend_backward(width, own, qkv_ref, c_ref, l_ref, scol_ref, srow_ref, da_ref, w_ref, dqkv_ref, *rest):
    heads = width // HEAD_DIM
    qkv = qkv_ref[...]
    queries = qkv[:, :width] * LOW(HEAD_DIM**-0.5)
    keys = qkv[:, width : 2 * width]
    values = qkv[:, 2 * width :]
    keys_t = keys.T
    dc = dot(da_ref[...], w_ref[...], NT).astype(LOW)
    prod_t = (dc.astype(WIDE) * c_ref[...].astype(WIDE)).T
    limit = same_document(scol_ref[...], srow_ref[0])
    dq_parts = []
    dk = jnp.zeros((SEQ_LEN, width), WIDE)
    dv = jnp.zeros((SEQ_LEN, width), WIDE)
    for h in range(heads):
        mask = head_mask(width, h)
        key_h = jnp.where(mask, keys, LOW(0))
        query_h = jnp.where(mask, queries, LOW(0))
        value_h = jnp.where(mask, values, LOW(0))
        dc_h = jnp.where(mask, dc, LOW(0))
        scores = jnp.minimum(dot(key_h, queries, NT), limit)
        probs = jnp.exp(scores - l_ref[0, h : h + 1, :])
        dprobs = dot(value_h, dc, NT)
        delta = jnp.sum(prod_t[h * HEAD_DIM : (h + 1) * HEAD_DIM, :], axis=0, keepdims=True)
        dscores = (probs * (dprobs - delta)).astype(LOW)
        dv = dv + dot(probs.astype(LOW), dc_h, NN)
        dk = dk + dot(dscores, query_h, NN)
        dq_parts.append(dot(keys_t[h * HEAD_DIM : (h + 1) * HEAD_DIM, :], dscores, NN))
    dq = jnp.concatenate(dq_parts, axis=0).T * (HEAD_DIM**-0.5)
    dqkv = jnp.concatenate([dq, dk, dv], axis=1).astype(LOW)
    dqkv_ref[...] = dqkv
    if own:
        sum_ref = rest[0]

        @pl.when(pl.program_id(0) == 0)
        def _():
            sum_ref[...] = jnp.zeros_like(sum_ref)

        sum_ref[0:1, : 3 * width] += column_sum(dqkv.astype(WIDE))


def call_attend_forward(width, tokens, scol, srow, bias, weight, place, slices):
    count, model = tokens.shape
    seqs = count // SEQ_LEN
    remote = slices is not None
    in_specs = [
        rows(SEQ_LEN, model),
        rows(SEQ_LEN, 1),
        pl.BlockSpec((1, 1, SEQ_LEN), lambda i: (i, 0, 0)),
    ]
    out_specs = [
        rows(SEQ_LEN, 3 * width),
        rows(SEQ_LEN, width),
        pl.BlockSpec((1, 8, SEQ_LEN), lambda i: (i, 0, 0)),
    ]
    out_shape = [
        jax.ShapeDtypeStruct((count, 3 * width), LOW),
        jax.ShapeDtypeStruct((count, width), LOW),
        jax.ShapeDtypeStruct((seqs, 8, SEQ_LEN), WIDE),
    ]
    scratch = []
    if remote:
        in_specs += [pl.BlockSpec(memory_space=pltpu.SMEM)]
        in_specs += [whole(slices[0].shape)] * LANES
        out_specs += [whole((4 * width, model))]
        out_shape += [jax.ShapeDtypeStruct((4 * width, model), LOW)]
        scratch = [pltpu.VMEM((4 * width, model), WIDE)]
        extra = (place, *slices)
    else:
        in_specs += [whole((1, 3 * width)), whole((4 * width, model))]
        extra = (bias, weight)
    return pl.pallas_call(
        functools.partial(attend_forward, remote, width),
        grid=(seqs,),
        in_specs=in_specs,
        out_specs=out_specs,
        out_shape=out_shape,
        scratch_shapes=scratch,
        compiler_params=params(),
        cost_estimate=cost(count),
    )(tokens, scol, srow, *extra)


def call_attend_backward(own, qkv, context, logs, scol, srow, da, weight):
    count, model = da.shape
    width = context.shape[1]
    seqs = count // SEQ_LEN
    in_specs = [
        rows(SEQ_LEN, 3 * width),
        rows(SEQ_LEN, width),
        pl.BlockSpec((1, 8, SEQ_LEN), lambda i: (i, 0, 0)),
        rows(SEQ_LEN, 1),
        pl.BlockSpec((1, 1, SEQ_LEN), lambda i: (i, 0, 0)),
        rows(SEQ_LEN, model),
        pl.BlockSpec((width, model), lambda i: (3, 0)),
    ]
    out_specs = [rows(SEQ_LEN, 3 * width)]
    out_shape = [jax.ShapeDtypeStruct((count, 3 * width), LOW)]
    if own:
        out_specs += [whole((8, model))]
        out_shape += [jax.ShapeDtypeStruct((8, model), WIDE)]
    return pl.pallas_call(
        functools.partial(attend_backward, width, own),
        grid=(seqs,),
        in_specs=in_specs,
        out_specs=out_specs,
        out_shape=out_shape,
        compiler_params=params(),
        cost_estimate=cost(count),
    )(qkv, context, logs, scol, srow, da, weight)


def input_gradient(groups, dh1_ref, *rest):
    dqkvs, weights, out_ref = rest[:groups], rest[groups : 2 * groups], rest[2 * groups]
    total = dh1_ref[...]
    for dqkv, weight in zip(dqkvs, weights):
        total = total + dot(dqkv[...], weight[: dqkv.shape[1], :], NN)
    out_ref[...] = total


def call_input_gradient(dh1, dqkvs, weights, block=512):
    count, model = dh1.shape
    groups = len(dqkvs)
    wide = dqkvs[0].shape[1]
    once = pl.BlockSpec((wide, model), lambda i: (0, 0), pipeline_mode=pl.Buffered(1))
    return pl.pallas_call(
        functools.partial(input_gradient, groups),
        grid=(count // block,),
        in_specs=[rows(block, model)] + [rows(block, wide)] * groups + [once] * groups,
        out_specs=rows(block, model),
        input_output_aliases={0: 0},
        out_shape=jax.ShapeDtypeStruct((count, model), WIDE),
        compiler_params=params(),
        cost_estimate=cost(count),
    )(dh1, *dqkvs, *weights)


def gelu_pair(u):
    tail = jnp.exp(u * u * -0.5)
    t = 1.0 / (1.0 + jnp.abs(u) * (0.3275911 * math.sqrt(0.5)))
    poly = 0.5 * 1.061405429
    for c in (-1.453152027, 1.421413741, -0.284496736, 0.254829592):
        poly = poly * t + 0.5 * c
    half = poly * t * tail
    phi = jnp.where(u < 0.0, half, 1.0 - half)
    return u * phi, phi + u * tail * (1.0 / math.sqrt(2.0 * math.pi))


def stats(values):
    mean = jnp.mean(values, axis=1, keepdims=True)
    center = values - mean
    scale = lax.rsqrt(jnp.mean(center * center, axis=1, keepdims=True) + EPS)
    return center * scale, scale


def feed_forward(remote, x_ref, *rest):
    if remote:
        acc_ref, rest = rest[0], rest[1:]
        place_ref, slices, rest = rest[0], rest[1 : 1 + LANES], rest[1 + LANES :]
        slope_ref, out_ref, wi_ref, wd_ref = rest
        part = wi_ref.shape[0] // LANES
        bias = slices[0][2 * part : 2 * part + 1, : wi_ref.shape[0]]

        @pl.when(pl.program_id(0) == 0)
        def _():
            here = place_ref[0]
            for m in range(LANES):
                at = pl.multiple_of((here ^ m) * part, part)
                wi_ref[pl.ds(at, part), :] = slices[m][:part, :].astype(LOW)
                wd_ref[pl.ds(at, part), :] = slices[m][part : 2 * part, :].astype(LOW)

        normed_low = x_ref[...]
    else:
        bias_ref, rest = rest[0], rest[1:]
        bias = bias_ref[...]
        (obias_ref, gain_ref, shift_ref, wi_ref, wd_ref) = rest[:5]
        groups = (len(rest) - 10) // 2
        contexts, outs, rest = rest[5 : 5 + groups], rest[5 + groups : 5 + 2 * groups], rest[5 + 2 * groups :]
        slope_ref, out_ref, h1_ref, n1_ref, act_ref = rest
        h1 = x_ref[...].astype(WIDE) + obias_ref[...]
        for context, weight in zip(contexts, outs):
            h1 = h1 + dot(context[...], weight[...], NN)
        h1_ref[...] = h1
        hat, _ = stats(h1)
        normed_low = (hat * gain_ref[...] + shift_ref[...]).astype(LOW)
        n1_ref[...] = normed_low
    hidden = wi_ref.shape[0]
    chunk = 256
    total = None
    for c in range(0, hidden, chunk):
        cols = slice(c, c + chunk)
        u = dot(normed_low, wi_ref[cols, :], NT) + bias[:, cols]
        act, slope = gelu_pair(u)
        act = act.astype(LOW)
        slope_ref[:, cols] = slope.astype(LOW)
        if not remote:
            act_ref[:, cols] = act
        add = dot(act, wd_ref[cols, :], NN)
        total = add if total is None else total + add
    out_ref[...] = total if not remote else acc_ref[...] + total


def call_feed_forward(hidden, x, remote, extra, contexts=(), packs=(), block=512):
    count, model = x.shape
    in_specs = [rows(block, model)]
    out_specs = [rows(block, hidden), rows(block, model)]
    out_shape = [
        jax.ShapeDtypeStruct((count, hidden), LOW),
        jax.ShapeDtypeStruct((count, model), WIDE),
    ]
    if remote:
        in_specs += [rows(block, model), pl.BlockSpec(memory_space=pltpu.SMEM)]
        in_specs += [whole(extra[2].shape)] * LANES
        out_specs += [whole((hidden, model))] * 2
        out_shape += [jax.ShapeDtypeStruct((hidden, model), LOW)] * 2
    else:
        width = contexts[0].shape[1]
        in_specs += [whole((1, hidden))] + [whole((1, model))] * 3 + [whole((hidden, model))] * 2
        in_specs += [rows(block, width)] * len(contexts)
        in_specs += [pl.BlockSpec((width, model), lambda i: (3, 0))] * len(packs)
        out_specs += [rows(block, model), rows(block, model), rows(block, hidden)]
        out_shape += [
            jax.ShapeDtypeStruct((count, model), WIDE),
            jax.ShapeDtypeStruct((count, model), LOW),
            jax.ShapeDtypeStruct((count, hidden), LOW),
        ]
    return pl.pallas_call(
        functools.partial(feed_forward, remote),
        grid=(count // block,),
        in_specs=in_specs,
        out_specs=out_specs,
        out_shape=out_shape,
        input_output_aliases={1: 1} if remote else {},
        compiler_params=params(),
        cost_estimate=cost(count),
    )(x, *extra, *contexts, *packs)


def norm_back(grad, hat, scale, gain):
    d = grad * gain
    first = jnp.mean(d, axis=1, keepdims=True)
    second = jnp.mean(d * hat, axis=1, keepdims=True)
    return scale * (d - first - hat * second)


def column_sum(values):
    return jnp.sum(values, axis=0, keepdims=True)


def back_through(dm, slope, wi_ref, wd_ref, dn1, keep=None):
    chunk = 256
    for c in range(0, wi_ref.shape[0], chunk):
        cols = slice(c, c + chunk)
        dact = dot(dm, wd_ref[cols, :], NT)
        du = (dact * slope[:, cols].astype(WIDE)).astype(LOW)
        if keep is not None:
            keep(cols, du)
        dn1 = dn1 + dot(du, wi_ref[cols, :], NN)
    return dn1


def middle_own(h1_ref, m_ref, cot_ref, g1_ref, b1_ref, db_ref, g2_ref, b2_ref, slope_ref, wi_ref, wd_ref, *outs):
    layer_ref, dm_ref, du_ref, dn1_ref, sums_ref = outs

    @pl.when(pl.program_id(0) == 0)
    def _():
        sums_ref[...] = jnp.zeros_like(sums_ref)

    hat1, _ = stats(h1_ref[...])
    normed = hat1 * g1_ref[...] + b1_ref[...]
    hat2, scale2 = stats(normed + m_ref[...] + db_ref[...])
    layer_ref[...] = (hat2 * g2_ref[...] + b2_ref[...]).astype(LOW)
    up = cot_ref[...].astype(WIDE)
    sums_ref[0:1, :] += column_sum(up * hat2)
    sums_ref[1:2, :] += column_sum(up)
    dh2 = norm_back(up, hat2, scale2, g2_ref[...])
    sums_ref[2:3, :] += column_sum(dh2)
    dm = dh2.astype(LOW)
    dm_ref[...] = dm

    def keep(cols, du):
        du_ref[:, cols] = du
        sums_ref[6:7, cols] += column_sum(du.astype(WIDE))

    dn1_ref[...] = back_through(dm, slope_ref, wi_ref, wd_ref, dh2, keep)


def middle_rest(groups, h1_ref, dn1_ref, dm_ref, g1_ref, old_ref, *rest):
    slopes, wis, wds = rest[:groups], rest[groups : 2 * groups], rest[2 * groups : 3 * groups]
    dh1_ref, da_ref, sums_ref = rest[3 * groups :]

    @pl.when(pl.program_id(0) == 0)
    def _():
        sums_ref[...] = old_ref[...]

    hat1, scale1 = stats(h1_ref[...])
    dm = dm_ref[...]
    dn1 = dn1_ref[...]
    for slope_ref, wi_ref, wd_ref in zip(slopes, wis, wds):
        dn1 = back_through(dm, slope_ref, wi_ref, wd_ref, dn1)
    sums_ref[3:4, :] += column_sum(dn1 * hat1)
    sums_ref[4:5, :] += column_sum(dn1)
    dh1 = norm_back(dn1, hat1, scale1, g1_ref[...])
    sums_ref[5:6, :] += column_sum(dh1)
    dh1_ref[...] = dh1
    da_ref[...] = dh1.astype(LOW)


def call_middle_own(h1, mixed, cot, vectors, slope, wi, wd, block=512):
    count, model = h1.shape
    hidden = wi.shape[0]
    once = pl.BlockSpec((hidden, model), lambda i: (0, 0), pipeline_mode=pl.Buffered(1))
    return pl.pallas_call(
        middle_own,
        grid=(count // block,),
        in_specs=[rows(block, model)] * 3 + [whole((1, model))] * 5 + [rows(block, hidden)] + [once] * 2,
        out_specs=[rows(block, model), rows(block, model), rows(block, hidden), rows(block, model), whole((8, model))],
        out_shape=[
            jax.ShapeDtypeStruct((count, model), LOW),
            jax.ShapeDtypeStruct((count, model), LOW),
            jax.ShapeDtypeStruct((count, hidden), LOW),
            jax.ShapeDtypeStruct((count, model), WIDE),
            jax.ShapeDtypeStruct((8, model), WIDE),
        ],
        input_output_aliases={1: 3},
        compiler_params=params(),
        cost_estimate=cost(count),
    )(h1, mixed, cot, *vectors, slope, wi, wd)


def call_middle_rest(h1, dn1, dm, gain, sums, slopes, wis, wds, block=512):
    count, model = h1.shape
    groups = len(slopes)
    hidden = wis[0].shape[0]
    once = pl.BlockSpec((hidden, model), lambda i: (0, 0), pipeline_mode=pl.Buffered(1))
    return pl.pallas_call(
        functools.partial(middle_rest, groups),
        grid=(count // block,),
        in_specs=[rows(block, model)] * 3
        + [whole((1, model)), whole((8, model))]
        + [rows(block, hidden)] * groups
        + [once] * (2 * groups),
        out_specs=[rows(block, model), rows(block, model), whole((8, model))],
        out_shape=[
            jax.ShapeDtypeStruct((count, model), WIDE),
            jax.ShapeDtypeStruct((count, model), LOW),
            jax.ShapeDtypeStruct((8, model), WIDE),
        ],
        input_output_aliases={1: 0},
        compiler_params=params(),
        cost_estimate=cost(count),
    )(h1, dn1, dm, gain, sums, *slopes, *wis, *wds)


def inner_first(left, right):
    return lax.dot_general(left, right, (((0,), (0,)), ((), ())), preferred_element_type=WIDE)


def assemble(turned, place_ref, *rest):
    pieces, outs = rest[:LANES], rest[LANES:]
    part = pieces[0].shape[0]
    out_ref = rest[-1]
    core, chip = place_ref[0] % 2, place_ref[0] // 2
    for k, piece in enumerate(pieces):
        half = core if k < 4 else 1 - core
        at = pl.multiple_of((half * 4 + (chip ^ (k % 4))) * part, 8)
        out_ref[pl.ds(at, part), :] = piece[...]
    for k in range(turned):
        width = outs[k].shape[1]
        outs[k][...] = out_ref[k * width : (k + 1) * width, :].T
    if turned:
        outs[turned][...] = out_ref[turned * width : (turned + 1) * width, :]


def call_assemble(place, pieces, turned=0):
    part, model = pieces[0].shape
    total = part * LANES
    if turned:
        width = total // (turned + 1)
        shapes = [(model, width)] * turned + [(width, model)]
    else:
        shapes = [(total, model)]
    out = pl.pallas_call(
        functools.partial(assemble, turned),
        grid=(1,),
        in_specs=[pl.BlockSpec(memory_space=pltpu.SMEM)] + [whole((part, model))] * LANES,
        out_specs=[whole(shape) for shape in shapes],
        out_shape=[jax.ShapeDtypeStruct(shape, WIDE) for shape in shapes],
        scratch_shapes=[pltpu.VMEM((total, model), WIDE)] if turned else [],
        compiler_params=params(),
    )(place, *pieces)
    return out


def after(values, *done):
    return lax.optimization_barrier((values, done))[0]


def swap(value, mask, size):
    return lax.ppermute(value, "dp", [(i, i ^ mask) for i in range(size)])


def from_tensor(value, shift, groups):
    return lax.ppermute(value, "tensor", [((i + shift) % groups, i) for i in range(groups)])


class Spread:
    def __init__(self, piece, shift, groups, size):
        self.piece, self.shift, self.groups, self.size = piece, shift, groups, size
        self.got = {}

    def along(self, *done):
        self.got[0] = from_tensor(after(self.piece, *done), self.shift, self.groups)
        return self.got[0]

    def hop(self, m, mask, *done):
        self.got[m ^ mask] = swap(after(self.got[m], *done), mask, self.size)
        return self.got[m ^ mask]

    def pair(self, *done):
        return [self.hop(m, 1, *done) for m in (0, 2, 4, 6)]

    def slices(self):
        return [self.got[m] for m in range(LANES)]


class Total:
    def __init__(self, value, size):
        self.value, self.size = value, size
        self.me = lax.axis_index("dp")
        self.half = value.shape[0] // 2
        self.part = self.half // 4

    def cut(self, value, at, count):
        return lax.dynamic_slice(value, (at, 0), (count, value.shape[1]))

    def pair(self, *done):
        value = after(self.value, *done)
        core = self.me % 2
        self.kept = self.cut(value, core * self.half, self.half)
        self.come = swap(self.cut(value, (1 - core) * self.half, self.half), 1, self.size)
        return self.come

    def scatter(self, *done):
        half = self.kept + after(self.come, *done)
        spot = (self.me // 2) % 4
        parts = [self.cut(half, (spot ^ m) * self.part, self.part) for m in range(4)]
        self.got = [parts[0]] + [swap(parts[m], 2 * m, self.size) for m in (1, 2, 3)]
        return self.got

    def gather(self, *done):
        a, b, c, d = after(self.got, *done)
        total = (a + b) + (c + d)
        mask = LANES
        while mask < self.size:
            total = total + swap(total, mask, self.size)
            mask *= 2
        self.got = [total] + [swap(total, 2 * m, self.size) for m in (1, 2, 3)]
        return self.got

    def share(self, *done):
        self.got = list(after(self.got, *done))
        self.other = [swap(part, 1, self.size) for part in self.got]
        return self.other

    def pieces(self):
        return [*self.got, *self.other]


def per_device(
    groups,
    size,
    tokens,
    segments,
    query_weight,
    key_weight,
    value_weight,
    query_bias,
    value_bias,
    output_weight,
    output_bias,
    gain_one,
    shift_one,
    inner_weight,
    inner_bias,
    down_weight,
    down_bias,
    gain_two,
    shift_two,
    cotangent,
):
    count, model = tokens.shape
    width = query_weight.shape[1]
    hidden = inner_weight.shape[1]
    place = (lax.axis_index("dp") % LANES).astype(jnp.int32)
    place_arg = place.reshape(1)
    others = range(1, groups)
    row = lambda v: v.reshape(1, -1)

    qkvo = jnp.concatenate([query_weight.T, key_weight.T, value_weight.T, output_weight], axis=0)
    inner_t = inner_weight.T
    narrow, deep = width // LANES, hidden // LANES

    def bias_rows(values):
        return jnp.pad(row(values), ((0, 7), (0, model - values.shape[0])))

    head_bias = jnp.concatenate([query_bias, jnp.zeros_like(query_bias), value_bias])
    head_piece = jnp.concatenate(
        [
            lax.dynamic_slice(
                qkvo.reshape(4, width, model), (0, place * narrow, 0), (4, narrow, model)
            ).reshape(4 * narrow, model).astype(WIDE),
            bias_rows(head_bias),
        ],
        axis=0,
    )
    deep_piece = jnp.concatenate(
        [
            lax.dynamic_slice(inner_t, (place * deep, 0), (deep, model)).astype(WIDE),
            lax.dynamic_slice(down_weight, (place * deep, 0), (deep, model)).astype(WIDE),
            bias_rows(inner_bias),
        ],
        axis=0,
    )
    scol = segments.reshape(count, 1)
    srow = segments.reshape(count // SEQ_LEN, 1, SEQ_LEN)

    order = [j for j in others if j % 2] + [j for j in others if j % 2 == 0]
    head_of = [Spread(head_piece, j, groups, size) for j in order]
    deep_of = [Spread(deep_piece, j, groups, size) for j in order]
    saved = {}

    def forward(k, *done):
        if k < 0:
            out = call_attend_forward(
                width, after(tokens, *done), scol, srow, row(head_bias), qkvo, None, None
            )
            saved[0] = (*out, qkvo)
        else:
            slices = after(head_of[k].slices(), *done)
            out = call_attend_forward(width, tokens, scol, srow, None, None, place_arg, slices)
            saved[order[k]] = out
        return out[2]

    a, b, c = head_of
    d, e, f = deep_of
    gate = [a.along()]
    late = c.along(gate)
    gate = [a.hop(0, 2, gate), a.hop(0, 4, gate), a.hop(0, 6, gate), b.along(gate), forward(-1, gate)]
    early = d.along(gate)
    gate = [a.pair(gate), b.hop(0, 2, gate), b.hop(0, 4, gate), late]
    late = e.along(gate)
    gate = [forward(0, gate), b.hop(2, 4, gate), c.hop(0, 2, gate), c.hop(0, 4, gate), early]
    gate = [b.pair(gate), c.hop(4, 2, gate), late]
    late = f.along(gate)
    gate = [forward(1, gate), c.pair(gate), d.hop(0, 2, gate), d.hop(0, 4, gate)]
    gate = [forward(2, gate), d.hop(2, 4, gate), e.hop(0, 2, gate), late]
    slope, mixed, h1, n1, act = call_feed_forward(
        hidden,
        after(tokens, gate),
        False,
        (row(inner_bias), row(output_bias), row(gain_one), row(shift_one), inner_t, down_weight),
        [saved[j][1] for j in range(groups)],
        [saved[j][3] for j in range(groups)],
    )
    slopes, wis, wds = [slope], [inner_t], [down_weight]

    def deep_forward(k, mixed, *done):
        slices = after(deep_of[k].slices(), *done)
        slope, mixed, wi, wd = call_feed_forward(hidden, n1, True, (mixed, place_arg, *slices))
        slopes.append(slope)
        wis.append(wi)
        wds.append(wd)
        return slope, mixed

    gate = [n1, d.pair(gate), e.hop(0, 4, gate), f.hop(0, 2, gate), f.hop(0, 4, gate)]
    begun = [e.hop(4, 2, gate), f.hop(2, 4, gate)]
    slope, mixed = deep_forward(0, mixed, gate)
    gate = [slope, begun]
    gate = [e.pair(gate)]
    begun = [f.pair(gate)]
    slope, mixed = deep_forward(1, mixed, gate)
    gate = [slope, begun]
    slope, mixed = deep_forward(2, mixed, gate)

    vectors = (row(gain_one), row(shift_one), row(down_bias), row(gain_two), row(shift_two))
    layer_out, dm, du, dn1, sums = call_middle_own(h1, mixed, cotangent, vectors, slopes[0], wis[0], wds[0])

    down = Total(inner_first(act, dm), size)
    gate = [down.value]
    inner = Total(inner_first(n1, after(du, gate)), size)
    gate = [down.pair(gate), inner.value]
    gate = [inner.pair(gate)]
    moved = [down.scatter(gate), inner.scatter(gate)]
    dh1, da, sums = call_middle_rest(
        h1, after(dn1, gate), dm, row(gain_one), sums, slopes[1:], wis[1:], wds[1:]
    )
    gate = [moved, sums]

    def backward(j, *done):
        qkv, context, logs, pack = saved[j]
        return call_attend_backward(j == 0, qkv, context, logs, scol, srow, after(da, *done), pack)

    moved = [down.gather(gate)]
    dqkv0, qkv_sums = backward(0, gate)
    sums = jnp.concatenate([sums, qkv_sums], axis=0)
    gate = [dqkv0, moved]
    heads_grad = jnp.concatenate([inner_first(after(dqkv0, gate), tokens), inner_first(saved[0][1], da)], axis=0)
    heads = Total(heads_grad, size)
    gate = [heads_grad]
    dqkvs, packs = [dqkv0], [qkvo]
    for k, j in enumerate(order):
        if k == 0:
            moved = [inner.gather(gate), heads.pair(gate), down.share(gate)]
        elif k == 1:
            moved = [heads.scatter(gate), inner.share(gate)]
        else:
            moved = [heads.gather(gate)]
        mask = 1 << k
        while mask < size:
            sums = after(sums, gate) + swap(after(sums, gate), mask, size)
            mask = mask * 2 if k == len(order) - 1 else size
        (grad,) = backward(j, gate)
        dqkvs.append(grad)
        packs.append(saved[j][3])
        gate = [grad, moved, sums]
    heads.share(gate)
    tokens_grad = call_input_gradient(after(dh1, gate), dqkvs, packs)
    (down_grad,) = call_assemble(place_arg, down.pieces())
    (inner_grad,) = call_assemble(place_arg, inner.pieces())
    query_grad, key_grad, value_grad, output_grad = call_assemble(
        place_arg, after(heads.pieces(), tokens_grad), 3
    )
    return (
        layer_out,
        tokens_grad,
        query_grad,
        key_grad,
        value_grad,
        sums[8, :width],
        sums[8, 2 * width : 3 * width],
        output_grad,
        sums[5],
        sums[3],
        sums[4],
        inner_grad,
        sums[6, :hidden],
        down_grad,
        sums[2],
        sums[0],
        sums[1],
    )


def solution(mesh):
    whole_rows, columns, lines, split = P("dp", None), P(None, "tensor"), P("tensor", None), P("tensor")
    in_specs = (
        whole_rows, P("dp"), columns, columns, columns, split, split, lines, P(), P(), P(),
        columns, split, lines, P(), P(), P(), whole_rows,
    )
    out_specs = (
        whole_rows, whole_rows, columns, columns, columns, split, split, lines, P(), P(), P(),
        columns, split, lines, P(), P(), P(),
    )
    body = functools.partial(per_device, mesh.shape["tensor"], mesh.shape["dp"])
    return jax.shard_map(body, mesh=mesh, in_specs=in_specs, out_specs=out_specs, check_vma=False)
```

time: 491 us -> 418 us (0.85)
  waiting for transfers between devices: 122 us -> 59.3 us
  blocking collectives: 25.8 us -> 0 us
  starting transfers between devices: 39.3 us -> 64.5 us
  between operations: 15.2 us -> 2.35 us
  Pallas kernels: 237 us -> 245 us
  local copies, waits for them, and re-layouts: 27.6 us -> 20.3 us
    psum x1 -> x0, waiting for transfers between devices: 41.3 us -> none  [per_device(): lax.psum((inner_first(dqkv, tokens), inner_first(saved[0][1], da), sums,...]
    pallas_call x1 -> x6, Pallas kernels: 39.7 us -> 70.3 us  [the longest x1 26.7 us: call_middle_rest(): pl.pallas_call(functools.partial(middle_rest, groups), grid=(count // blo...]
    ppermute x42 -> x78, starting transfers between devices: 23.4 us -> 52.6 us  [swap(): return lax.ppermute(value, 'dp', [(i, i ^ mask) for i in range(size)])]
    psum x1 -> x0, blocking collectives: 25.8 us -> none  [per_device(): lax.psum((inner_first(dqkv, tokens), inner_first(saved[0][1], da), sums,...]
    ppermute x9 -> x6, waiting for transfers between devices: 51.5 us -> 29.8 us  [from_tensor(): lax.ppermute(value, 'tensor', [((i + shift) % groups, i) for i in range(g...]
    pallas_call x4, Pallas kernels: 74.9 us -> 55.6 us  [call_attend_backward(): pl.pallas_call(functools.partial(attend_backward, width, own), grid=(seqs...]
    pallas_call x4, Pallas kernels: 59.5 us -> 51.7 us  [call_attend_forward(): pl.pallas_call(functools.partial(attend_forward, remote, width), grid=(se...]
    slice x9 -> x1, local copies, waits for them, and re-layouts: 5.52 us -> 0.57 us  [per_device(): sums[8, 2 * width:3 * width]]
  transfers between devices with their start and end apart: 52 -> 84, of which waited for: 13 -> 15; matrix products, arithmetic and copies ran while one was open for 4% -> 4% of each run, Pallas kernels for 34% -> 50%
where the time goes in v2:
time: 418 us; the launch traced here: 413 us
  Pallas kernels  245 us (59%)
  starting transfers between devices  64.5 us (15%)
  waiting for transfers between devices  59.3 us (14%)
  local copies, waits for them, and re-layouts  20.3 us (5%)
  matrix products  15.2 us (4%)
  other arithmetic  6.57 us (2%)
    pallas_call x4, Pallas kernels, call_feed_forward(): pl.pallas_call(functools.partial(feed_forward, remote), grid=(count // bl...  67.7 us
    pallas_call x4, Pallas kernels, call_attend_backward(): pl.pallas_call(functools.partial(attend_backward, width, own), grid=(seqs...  55.6 us
    ppermute x78, starting transfers between devices, swap(): return lax.ppermute(value, 'dp', [(i, i ^ mask) for i in range(size)])  52.6 us
    pallas_call x4, Pallas kernels, call_attend_forward(): pl.pallas_call(functools.partial(attend_forward, remote, width), grid=(se...  51.7 us
    ppermute x6, waiting for transfers between devices, from_tensor(): lax.ppermute(value, 'tensor', [((i + shift) % groups, i) for i in range(g...  29.8 us
    ppermute x78, waiting for transfers between devices, swap(): return lax.ppermute(value, 'dp', [(i, i ^ mask) for i in range(size)])  29.5 us
    pallas_call x1, Pallas kernels, call_middle_rest(): pl.pallas_call(functools.partial(middle_rest, groups), grid=(count // blo...  26.7 us
    pallas_call x1, Pallas kernels, call_middle_own(): pl.pallas_call(middle_own, grid=(count // block,), in_specs=[rows(block,...  18.4 us
  transfers between devices with their start and end apart: 84, of which 15 were waited for; matrix products, arithmetic and copies ran while one was open for 4% of the time, Pallas kernels for 50%

profile of v2, /device:TPU:0, one launch (start us, length us, event | category | flops | bytes accessed | tf_op | source)
XLA Modules:
  0.0 413.4 jit_solution(8510613770153769670)
XLA Ops:
  3.1 5.0 %collective-permute-start = (f32[104,768]{1,0:T(8,128)}, f32[104,768]{1,0:T(8,128)S(1)}, u32[]{:S(2)}, u32[]{:S(2)}) collective-permute-start(f32[104,768]{1,0:T(8,128)} %select_maximum_fusion.1), channel_id=1, source_target_pairs={{1,0},{2,1},{3,2},{0,3},{5,4},{6,5},{7,6},{4,7},{9,8},{10,9},{11,1... | collective-permute-start | bytes 958472 | tf_op jit(solution)/shard_map/ppermute | solution.py:496
  9.5 5.7 %collective-permute-done.rest_1_ = f32[104,768]{1,0:T(8,128)S(1)} collective-permute-done((f32[104,768]{1,0:T(8,128)}, f32[104,768]{1,0:T(8,128)S(1)}, u32[]{:S(2)}, u32[]{:S(2)}) %collective-permute-start) | collective-permute-done | bytes 319520 | tf_op jit(solution)/shard_map/ppermute | solution.py:496
  16.8 1.5 collective-permute-start.4
  19.1 4.4 %collective-permute-start.1 = (f32[104,768]{1,0:T(8,128)}, f32[104,768]{1,0:T(8,128)}, u32[]{:S(2)}, u32[]{:S(2)}) collective-permute-start(f32[104,768]{1,0:T(8,128)} %select_maximum_fusion.1), channel_id=1, source_target_pairs={{2,0},{3,1},{0,2},{1,3},{6,4},{7,5},{4,6},{5,7},{10,8},{11,9},{8,1... | collective-permute-start | bytes 958472 | tf_op jit(solution)/shard_map/ppermute | solution.py:496
  23.5 12.4 %shard_map.305 = (bf16[2048,576]{1,0:T(8,128)(2,1)}, bf16[2048,192]{1,0:T(8,128)(2,1)}, f32[4,8,512]{2,1,0:T(8,128)}) custom-call(bf16[2048,768]{1,0:T(8,128)(2,1)} %x_ref.7, s32[2048,1]{1,0:T(8,128)} %copy.50.scol_ref, s32[4,1,512]{2,1,0:T(1,128)} %bitcast.29, f32[1,576]{1,0:T(1,128)} %copy-done.31, bf16[768,768]{1,0:T(8,128)(2,1)} %copy-done.1), custom_call_target="tpu_custom_call" | custom-call | flops 15360000000 | bytes 16777216 | tf_op jit(solution)/shard_map/pallas_call | solution.py:164
  39.0 1.6 collective-permute-start.11
  41.1 1.7 collective-permute-done.1.rest_1_
  47.1 1.5 collective-permute-start.14
  48.6 2.0 collective-permute-start.21
  51.1 13.1 %shard_map.306 = (bf16[2048,576]{1,0:T(8,128)(2,1)}, bf16[2048,192]{1,0:T(8,128)(2,1)}, f32[4,8,512]{2,1,0:T(8,128)}, bf16[768,768]{1,0:T(8,128)(2,1)}) custom-call(bf16[2048,768]{1,0:T(8,128)(2,1)} %x_ref.7, s32[2048,1]{1,0:T(8,128)} %copy.50.scol_ref, s32[4,1,512]{2,1,0:T(1,128)} %bitcast.30, s32[1]{0:T(128)} %bitcast.2.rest_0_.rest_1_.place_ref, ...), custom_call_target="tpu_custom_call" | custom-call | flops 15360000000 | bytes 16777216 | tf_op jit(solution)/shard_map/pallas_call | solution.py:164
  64.3 1.6 collective-permute-start.20
  66.5 9.2 %collective-permute-done.21.rest_2_ = f32[200,768]{1,0:T(8,128)S(1)} collective-permute-done((f32[200,768]{1,0:T(8,128)S(1)}, f32[200,768]{1,0:T(8,128)S(1)}, u32[]{:S(2)}, u32[]{:S(2)}) %collective-permute-start.21) | collective-permute-done | bytes 614432 | tf_op jit(solution)/shard_map/ppermute | solution.py:496
  75.8 1.7 collective-permute-done.16.rest_2_
  79.2 1.5 collective-permute-start.27
  81.3 13.1 %shard_map.307 = (bf16[2048,576]{1,0:T(8,128)(2,1)}, bf16[2048,192]{1,0:T(8,128)(2,1)}, f32[4,8,512]{2,1,0:T(8,128)}, bf16[768,768]{1,0:T(8,128)(2,1)}) custom-call(bf16[2048,768]{1,0:T(8,128)(2,1)} %x_ref.7, s32[2048,1]{1,0:T(8,128)} %copy.50.scol_ref, s32[4,1,512]{2,1,0:T(1,128)} %bitcast.31, s32[1]{0:T(128)} %bitcast.2.rest_0_.rest_1_.place_ref, ...), custom_call_target="tpu_custom_call" | custom-call | flops 15360000000 | bytes 16777216 | tf_op jit(solution)/shard_map/pallas_call | solution.py:164
  97.2 13.1 %shard_map.308 = (bf16[2048,576]{1,0:T(8,128)(2,1)}, bf16[2048,192]{1,0:T(8,128)(2,1)}, f32[4,8,512]{2,1,0:T(8,128)}, bf16[768,768]{1,0:T(8,128)(2,1)}) custom-call(bf16[2048,768]{1,0:T(8,128)(2,1)} %x_ref.7, s32[2048,1]{1,0:T(8,128)} %copy.50.scol_ref, s32[4,1,512]{2,1,0:T(1,128)} %bitcast.32, s32[1]{0:T(128)} %bitcast.2.rest_0_.rest_1_.place_ref, ...), custom_call_target="tpu_custom_call" | custom-call | flops 15360000000 | bytes 16777216 | tf_op jit(solution)/shard_map/pallas_call | solution.py:164
  110.3 13.1 %collective-permute-done.30.rest_2_ = f32[200,768]{1,0:T(8,128)S(1)} collective-permute-done((f32[200,768]{1,0:T(8,128)S(1)}, f32[200,768]{1,0:T(8,128)S(1)}, u32[]{:S(2)}, u32[]{:S(2)}) %collective-permute-start.30) | collective-permute-done | bytes 614432 | tf_op jit(solution)/shard_map/ppermute | solution.py:496
  126.3 1.5 collective-permute-start.35
  128.3 11.0 %collective-permute-done.36.rest_4_ = f32[200,768]{1,0:T(8,128)S(1)} collective-permute-done((f32[200,768]{1,0:T(8,128)S(1)}, f32[200,768]{1,0:T(8,128)S(1)}, u32[]{:S(2)}, u32[]{:S(2)}) %collective-permute-start.36) | collective-permute-done | bytes 614432 | tf_op jit(solution)/shard_map/ppermute | solution.py:492
  140.8 20.7 %shard_map.309 = (bf16[2048,768]{1,0:T(8,128)(2,1)}, f32[2048,768]{1,0:T(8,128)}, f32[2048,768]{1,0:T(8,128)}, bf16[2048,768]{1,0:T(8,128)(2,1)}, bf16[2048,768]{1,0:T(8,128)(2,1)}) custom-call(bf16[2048,768]{1,0:T(8,128)(2,1)} %x_ref.7, f32[1,768]{1,0:T(1,128)} %copy-done.30, f32[1,768]{1,0:T(1,128)} %reshape.84.rest_1_, f32[1,768]{1,0:T(1,128)} %reshape.85.rest_2_.g1_ref, ...), custom_call_target="tpu_custom_call" | custom-call | flops 15360000000 | bytes 16777216 | tf_op jit(solution)/shard_map/pallas_call | solution.py:319
  163.7 15.6 %shard_map.310 = (bf16[2048,768]{1,0:T(8,128)(2,1)}, f32[2048,768]{1,0:T(8,128)}, bf16[768,768]{1,0:T(8,128)(2,1)}, bf16[768,768]{1,0:T(8,128)(2,1)}) custom-call(bf16[2048,768]{1,0:T(8,128)(2,1)} %get-tuple-element.264.x_ref, f32[2048,768]{1,0:T(8,128)} %get-tuple-element.265.rest_0_, ...), custom_call_target="tpu_custom_call", output_to_operand_aliasing={{1}: (1, {})} | custom-call | flops 15360000000 | bytes 16777216 | tf_op jit(solution)/shard_map/pallas_call | solution.py:319
  185.2 15.7 %shard_map.311 = (bf16[2048,768]{1,0:T(8,128)(2,1)}, f32[2048,768]{1,0:T(8,128)}, bf16[768,768]{1,0:T(8,128)(2,1)}, bf16[768,768]{1,0:T(8,128)(2,1)}) custom-call(bf16[2048,768]{1,0:T(8,128)(2,1)} %get-tuple-element.264.x_ref, f32[2048,768]{1,0:T(8,128)} %get-tuple-element.280.rest_0_, ...), custom_call_target="tpu_custom_call", output_to_operand_aliasing={{1}: (1, {})} | custom-call | flops 15360000000 | bytes 16777216 | tf_op jit(solution)/shard_map/pallas_call | solution.py:319
  202.4 15.6 %shard_map.312 = (bf16[2048,768]{1,0:T(8,128)(2,1)}, f32[2048,768]{1,0:T(8,128)}, bf16[768,768]{1,0:T(8,128)(2,1)}, bf16[768,768]{1,0:T(8,128)(2,1)}) custom-call(bf16[2048,768]{1,0:T(8,128)(2,1)} %get-tuple-element.264.x_ref, f32[2048,768]{1,0:T(8,128)} %get-tuple-element.296.rest_0_, ...), custom_call_target="tpu_custom_call", output_to_operand_aliasing={{1}: (1, {})} | custom-call | flops 15360000000 | bytes 16777216 | tf_op jit(solution)/shard_map/pallas_call | solution.py:319
  218.0 18.4 %shard_map.313 = (bf16[2048,768]{1,0:T(8,128)(2,1)}, bf16[2048,768]{1,0:T(8,128)(2,1)}, bf16[2048,768]{1,0:T(8,128)(2,1)}, f32[2048,768]{1,0:T(8,128)}, f32[8,768]{1,0:T(8,128)}) custom-call(f32[2048,768]{1,0:T(8,128)} %get-tuple-element.263.h1_ref, f32[2048,768]{1,0:T(8,128)} %get-tuple-element.310.m_ref, ...), custom_call_target="tpu_custom_call", output_to_operand_aliasing={{3}: (1, {})} | custom-call | flops 15360000000 | bytes 16777216 | tf_op jit(solution)/shard_map/pallas_call | solution.py:405
  236.4 4.7 %fusion.1 = f32[768,768]{1,0:T(8,128)S(1)} fusion(bf16[2048,768]{1,0:T(8,128)(2,1)S(1)} %copy-done.83, bf16[2048,768]{1,0:T(8,128)(2,1)} %get-tuple-element.316.dm_ref), kind=kOutput, calls=%fused_computation.41 | convolution fusion | flops 2415919104 | bytes 8650752 | tf_op jit(solution)/shard_map/dot_general | solution.py:448
  241.4 2.7 fusion.2
  247.0 2.8 collective-permute-done.49
  249.9 1.9 dynamic-slice_add_fusion.1
  257.7 26.7 %shard_map.314 = (f32[2048,768]{1,0:T(8,128)}, bf16[2048,768]{1,0:T(8,128)(2,1)}, f32[8,768]{1,0:T(8,128)}) custom-call(f32[2048,768]{1,0:T(8,128)} %get-tuple-element.263.h1_ref, f32[2048,768]{1,0:T(8,128)} %get-tuple-element.320.dn1_ref, bf16[2048,768]{1,0:T(8,128)(2,1)} %get-tuple-element.316.dm_ref, ...), custom_call_target="tpu_custom_call", output_to_operand_aliasing={{0}: (1, {})} | custom-call | flops 15360000000 | bytes 16777216 | tf_op jit(solution)/shard_map/pallas_call | solution.py:428
  285.9 2.7 fusion.4
  288.6 4.6 %collective-permute-done.52 = f32[96,768]{1,0:T(8,128)S(1)} collective-permute-done((f32[96,768]{1,0:T(8,128)S(1)}, f32[96,768]{1,0:T(8,128)S(1)}, u32[]{:S(2)}, u32[]{:S(2)}) %collective-permute-start.52) | collective-permute-done | bytes 294944 | tf_op jit(solution)/shard_map/ppermute | solution.py:492
  293.3 1.6 collective-permute-start.56
  296.8 14.3 %shard_map.315 = (bf16[2048,576]{1,0:T(8,128)(2,1)}, f32[8,768]{1,0:T(8,128)}) custom-call(bf16[2048,576]{1,0:T(8,128)(2,1)} %get-tuple-element.334.qkv_ref, bf16[2048,192]{1,0:T(8,128)(2,1)} %get-tuple-element.256.rest_6_.c_ref, f32[4,8,512]{2,1,0:T(8,128)} %get-tuple-element.205.l_ref, s32[2048,1]{1,0:T(8,128)} %copy.50.scol_ref, s32[4,1,512]{2,1,0:T(1,128)} %bitcast.33, ...), custom_call_target="tpu_custom_call" | custom-call | flops 15360000000 | bytes 16777216 | tf_op jit(solution)/shard_map/pallas_call | solution.py:194
  311.9 5.0 %fusion.3 = f32[576,768]{1,0:T(8,128)S(1)} fusion(bf16[2048,576]{1,0:T(8,128)(2,1)} %get-tuple-element.344.rest_0_, bf16[2048,768]{1,0:T(8,128)(2,1)} %x_ref.7), kind=kOutput, calls=%fused_computation.43 | convolution fusion | flops 1811939328 | bytes 7274496 | tf_op jit(solution)/shard_map/dot_general | solution.py:448
  318.3 1.6 collective-permute-start.59
  320.5 2.1 collective-permute-start.61
  323.2 13.7 %shard_map.316.rest_1_ = bf16[2048,576]{1,0:T(8,128)(2,1)} custom-call(bf16[2048,576]{1,0:T(8,128)(2,1)} %get-tuple-element.333.qkv_ref, bf16[2048,192]{1,0:T(8,128)(2,1)} %get-tuple-element.257.rest_7_.c_ref, f32[4,8,512]{2,1,0:T(8,128)} %get-tuple-element.219.l_ref, s32[2048,1]{1,0:T(8,128)} %copy.50.scol_ref, s32[4,1,512]{2,1,0:T(1,128)} %bitcast.34, ...), custom_call_target="tpu_custom_call" | custom-call | flops 15360000000 | bytes 16777216 | tf_op jit(solution)/shard_map/pallas_call | solution.py:194
  337.7 3.2 shard_map.322
  343.2 3.0 collective-permute-done.75
  347.5 2.1 collective-permute-start.70
  349.6 13.9 %shard_map.317.rest_2_ = bf16[2048,576]{1,0:T(8,128)(2,1)} custom-call(bf16[2048,576]{1,0:T(8,128)(2,1)} %get-tuple-element.332.qkv_ref, bf16[2048,192]{1,0:T(8,128)(2,1)} %get-tuple-element.259.rest_9_.c_ref, f32[4,8,512]{2,1,0:T(8,128)} %get-tuple-element.241.l_ref, s32[2048,1]{1,0:T(8,128)} %copy.50.scol_ref, s32[4,1,512]{2,1,0:T(1,128)} %bitcast.35, ...), custom_call_target="tpu_custom_call" | custom-call | flops 15360000000 | bytes 16777216 | tf_op jit(solution)/shard_map/pallas_call | solution.py:194
  365.1 2.1 collective-permute-start.78
  367.8 13.7 %shard_map.318.rest_3_ = bf16[2048,576]{1,0:T(8,128)(2,1)} custom-call(bf16[2048,576]{1,0:T(8,128)(2,1)} %get-tuple-element.330.qkv_ref, bf16[2048,192]{1,0:T(8,128)(2,1)} %get-tuple-element.258.rest_8_.c_ref, f32[4,8,512]{2,1,0:T(8,128)} %get-tuple-element.251.l_ref, s32[2048,1]{1,0:T(8,128)} %copy.50.scol_ref, s32[4,1,512]{2,1,0:T(1,128)} %bitcast.36, ...), custom_call_target="tpu_custom_call" | custom-call | flops 15360000000 | bytes 16777216 | tf_op jit(solution)/shard_map/pallas_call | solution.py:194
  381.5 3.2 shard_map.321
  387.0 15.3 %shard_map.319 = f32[2048,768]{1,0:T(8,128)} custom-call(f32[2048,768]{1,0:T(8,128)} %get-tuple-element.370.dh1_ref, bf16[2048,576]{1,0:T(8,128)(2,1)} %get-tuple-element.344.rest_0_, bf16[2048,576]{1,0:T(8,128)(2,1)} %shard_map.316.rest_1_, bf16[2048,576]{1,0:T(8,128)(2,1)} %shard_map.317.rest_2_, ...), custom_call_target="tpu_custom_call", output_to_operand_aliasing={{}: (0, {})} | custom-call | flops 15360000000 | bytes 16777216 | tf_op jit(solution)/shard_map/pallas_call | solution.py:218
  404.0 3.6 shard_map.320
  407.6 2.3 copy.56
  409.9 2.2 copy.57
  (352 shorter events, 61.1 us)
Async XLA Ops:
  15.3 20.7 %collective-permute-start.3 = (f32[104,768]{1,0:T(8,128)S(1)}, f32[104,768]{1,0:T(8,128)S(1)}, u32[]{:S(2)}, u32[]{:S(2)}) collective-permute-start(f32[104,768]{1,0:T(8,128)S(1)} %collective-permute-done.rest_1_), channel_id=1, source_target_pairs={{0,8},{4,12},{8,0},{12,4},{16,24},{20,28},{24,16},{28,20},{1,9},{5... | collective-permute-start | bytes 958472 | tf_op jit(solution)/shard_map/ppermute | solution.py:492
  16.8 19.2 %collective-permute-start.4 = (f32[104,768]{1,0:T(8,128)S(1)}, f32[104,768]{1,0:T(8,128)S(1)}, u32[]{:S(2)}, u32[]{:S(2)}) collective-permute-start(f32[104,768]{1,0:T(8,128)S(1)} %collective-permute-done.rest_1_), channel_id=1, source_target_pairs={{0,16},{4,20},{8,24},{12,28},{16,0},{20,4},{24,8},{28,12},{1,17},{... | collective-permute-start | bytes 958472 | tf_op jit(solution)/shard_map/ppermute | solution.py:492
  18.3 17.7 %collective-permute-start.5 = (f32[104,768]{1,0:T(8,128)S(1)}, f32[104,768]{1,0:T(8,128)S(1)}, u32[]{:S(2)}, u32[]{:S(2)}) collective-permute-start(f32[104,768]{1,0:T(8,128)S(1)} %collective-permute-done.rest_1_), channel_id=1, source_target_pairs={{0,24},{4,28},{8,16},{12,20},{16,8},{20,12},{24,0},{28,4},{1,25},{... | collective-permute-start | bytes 958472 | tf_op jit(solution)/shard_map/ppermute | solution.py:492
  18.8 17.2 %collective-permute-start.2 = (f32[104,768]{1,0:T(8,128)}, f32[104,768]{1,0:T(8,128)}, u32[]{:S(2)}, u32[]{:S(2)}) collective-permute-start(f32[104,768]{1,0:T(8,128)} %select_maximum_fusion.1), channel_id=1, source_target_pairs={{3,0},{0,1},{1,2},{2,3},{7,4},{4,5},{5,6},{6,7},{11,8},{8,9},{9,10... | collective-permute-start | bytes 958472 | tf_op jit(solution)/shard_map/ppermute | solution.py:496
  19.1 23.7 %collective-permute-start.1 = (f32[104,768]{1,0:T(8,128)}, f32[104,768]{1,0:T(8,128)}, u32[]{:S(2)}, u32[]{:S(2)}) collective-permute-start(f32[104,768]{1,0:T(8,128)} %select_maximum_fusion.1), channel_id=1, source_target_pairs={{2,0},{3,1},{0,2},{1,3},{6,4},{7,5},{4,6},{5,7},{10,8},{11,9},{8,1... | collective-permute-start | bytes 958472 | tf_op jit(solution)/shard_map/ppermute | solution.py:496
  46.2 18.0 %collective-permute-start.15 = (f32[200,768]{1,0:T(8,128)S(1)}, f32[200,768]{1,0:T(8,128)S(1)}, u32[]{:S(2)}, u32[]{:S(2)}) collective-permute-start(f32[200,768]{1,0:T(8,128)S(1)} %select_maximum_fusion), channel_id=1, source_target_pairs={{1,0},{2,1},{3,2},{0,3},{5,4},{6,5},{7,6},{4,7},{9,8},{10,9},{11,1... | collective-permute-start | bytes 1843208 | tf_op jit(solution)/shard_map/ppermute | solution.py:496
  46.3 17.9 %collective-permute-start.13 = (f32[104,768]{1,0:T(8,128)}, f32[104,768]{1,0:T(8,128)S(1)}, u32[]{:S(2)}, u32[]{:S(2)}) collective-permute-start(f32[104,768]{1,0:T(8,128)} %collective-permute-done.1.rest_1_), channel_id=1, source_target_pairs={{0,8},{4,12},{8,0},{12,4},{16,24},{20,28},{24,16},{28,20},{1,9},{5... | collective-permute-start | bytes 958472 | tf_op jit(solution)/shard_map/ppermute | solution.py:492
  47.1 17.2 %collective-permute-start.14 = (f32[104,768]{1,0:T(8,128)}, f32[104,768]{1,0:T(8,128)S(1)}, u32[]{:S(2)}, u32[]{:S(2)}) collective-permute-start(f32[104,768]{1,0:T(8,128)} %collective-permute-done.1.rest_1_), channel_id=1, source_target_pairs={{0,16},{4,20},{8,24},{12,28},{16,0},{20,4},{24,8},{28,12},{1,17},{... | collective-permute-start | bytes 958472 | tf_op jit(solution)/shard_map/ppermute | solution.py:492
  48.6 27.1 %collective-permute-start.21 = (f32[200,768]{1,0:T(8,128)S(1)}, f32[200,768]{1,0:T(8,128)S(1)}, u32[]{:S(2)}, u32[]{:S(2)}) collective-permute-start(f32[200,768]{1,0:T(8,128)S(1)} %select_maximum_fusion), channel_id=1, source_target_pairs={{3,0},{0,1},{1,2},{2,3},{7,4},{4,5},{5,6},{6,7},{11,8},{8,9},{9,10... | collective-permute-start | bytes 1843208 | tf_op jit(solution)/shard_map/ppermute | solution.py:496
  77.7 16.9 %collective-permute-start.26 = (f32[200,768]{1,0:T(8,128)S(1)}, f32[200,768]{1,0:T(8,128)S(1)}, u32[]{:S(2)}, u32[]{:S(2)}) collective-permute-start(f32[200,768]{1,0:T(8,128)S(1)} %collective-permute-done.15.rest_2_), channel_id=1, source_target_pairs={{0,8},{4,12},{8,0},{12,4},{16,24},{20,28},{24,16},{28,20},{1,9},{5... | collective-permute-start | bytes 1843208 | tf_op jit(solution)/shard_map/ppermute | solution.py:492
  94.5 28.9 %collective-permute-start.30 = (f32[200,768]{1,0:T(8,128)S(1)}, f32[200,768]{1,0:T(8,128)S(1)}, u32[]{:S(2)}, u32[]{:S(2)}) collective-permute-start(f32[200,768]{1,0:T(8,128)S(1)} %select_maximum_fusion), channel_id=1, source_target_pairs={{2,0},{3,1},{0,2},{1,3},{6,4},{7,5},{4,6},{5,7},{10,8},{11,9},{8,1... | collective-permute-start | bytes 1843208 | tf_op jit(solution)/shard_map/ppermute | solution.py:496
  95.4 28.0 %collective-permute-start.29 = (f32[200,768]{1,0:T(8,128)S(1)}, f32[200,768]{1,0:T(8,128)S(1)}, u32[]{:S(2)}, u32[]{:S(2)}) collective-permute-start(f32[200,768]{1,0:T(8,128)S(1)} %collective-permute-done.21.rest_2_), channel_id=1, source_target_pairs={{0,8},{4,12},{8,0},{12,4},{16,24},{20,28},{24,16},{28,20},{1,9},{5... | collective-permute-start | bytes 1843208 | tf_op jit(solution)/shard_map/ppermute | solution.py:492
  96.0 27.4 %collective-permute-start.28 = (f32[200,768]{1,0:T(8,128)S(1)}, f32[200,768]{1,0:T(8,128)S(1)}, u32[]{:S(2)}, u32[]{:S(2)}) collective-permute-start(f32[200,768]{1,0:T(8,128)S(1)} %collective-permute-done.26.rest_4_), channel_id=1, source_target_pairs={{0,16},{4,20},{8,24},{12,28},{16,0},{20,4},{24,8},{28,12},{1,17},{... | collective-permute-start | bytes 1843208 | tf_op jit(solution)/shard_map/ppermute | solution.py:492
  124.0 16.7 %collective-permute-start.37 = (f32[200,768]{1,0:T(8,128)S(1)}, f32[200,768]{1,0:T(8,128)S(1)}, u32[]{:S(2)}, u32[]{:S(2)}) collective-permute-start(f32[200,768]{1,0:T(8,128)S(1)} %collective-permute-done.30.rest_2_), channel_id=1, source_target_pairs={{0,16},{4,20},{8,24},{12,28},{16,0},{20,4},{24,8},{28,12},{1,17},{... | collective-permute-start | bytes 1843208 | tf_op jit(solution)/shard_map/ppermute | solution.py:492
  126.3 35.3 %collective-permute-start.35 = (f32[200,768]{1,0:T(8,128)S(1)}, f32[200,768]{1,0:T(8,128)}, u32[]{:S(2)}, u32[]{:S(2)}) collective-permute-start(f32[200,768]{1,0:T(8,128)S(1)} %collective-permute-done.21.rest_2_), channel_id=1, source_target_pairs={{0,16},{4,20},{8,24},{12,28},{16,0},{20,4},{24,8},{28,12},{1,17},{... | collective-permute-start | bytes 1843208 | tf_op jit(solution)/shard_map/ppermute | solution.py:492
  127.8 33.7 %collective-permute-start.34 = (f32[200,768]{1,0:T(8,128)S(1)}, f32[200,768]{1,0:T(8,128)S(1)}, u32[]{:S(2)}, u32[]{:S(2)}) collective-permute-start(f32[200,768]{1,0:T(8,128)S(1)} %collective-permute-done.28.rest_8_), channel_id=1, source_target_pairs={{0,4},{4,0},{8,12},{12,8},{16,20},{20,16},{24,28},{28,24},{1,5},{5... | collective-permute-start | bytes 1843208 | tf_op jit(solution)/shard_map/ppermute | solution.py:492
  127.8 33.8 %collective-permute-start.33 = (f32[200,768]{1,0:T(8,128)S(1)}, f32[200,768]{1,0:T(8,128)S(1)}, u32[]{:S(2)}, u32[]{:S(2)}) collective-permute-start(f32[200,768]{1,0:T(8,128)S(1)} %collective-permute-done.27.rest_6_), channel_id=1, source_target_pairs={{0,4},{4,0},{8,12},{12,8},{16,20},{20,16},{24,28},{28,24},{1,5},{5... | collective-permute-start | bytes 1843208 | tf_op jit(solution)/shard_map/ppermute | solution.py:492
  139.3 22.3 %collective-permute-start.32 = (f32[200,768]{1,0:T(8,128)S(1)}, f32[200,768]{1,0:T(8,128)}, u32[]{:S(2)}, u32[]{:S(2)}) collective-permute-start(f32[200,768]{1,0:T(8,128)S(1)} %collective-permute-done.26.rest_4_), channel_id=1, source_target_pairs={{0,4},{4,0},{8,12},{12,8},{16,20},{20,16},{24,28},{28,24},{1,5},{5... | collective-permute-start | bytes 1843208 | tf_op jit(solution)/shard_map/ppermute | solution.py:492
  140.8 20.8 %collective-permute-start.31 = (f32[200,768]{1,0:T(8,128)S(1)}, f32[200,768]{1,0:T(8,128)}, u32[]{:S(2)}, u32[]{:S(2)}) collective-permute-start(f32[200,768]{1,0:T(8,128)S(1)} %collective-permute-done.15.rest_2_), channel_id=1, source_target_pairs={{0,4},{4,0},{8,12},{12,8},{16,20},{20,16},{24,28},{28,24},{1,5},{5... | collective-permute-start | bytes 1843208 | tf_op jit(solution)/shard_map/ppermute | solution.py:492
  161.6 17.7 %collective-permute-start.39 = (f32[200,768]{1,0:T(8,128)S(1)}, f32[200,768]{1,0:T(8,128)}, u32[]{:S(2)}, u32[]{:S(2)}) collective-permute-start(f32[200,768]{1,0:T(8,128)S(1)} %collective-permute-done.36.rest_4_), channel_id=1, source_target_pairs={{0,16},{4,20},{8,24},{12,28},{16,0},{20,4},{24,8},{28,12},{1,17},{... | collective-permute-start | bytes 1843208 | tf_op jit(solution)/shard_map/ppermute | solution.py:492
  162.2 17.2 %collective-permute-start.38 = (f32[200,768]{1,0:T(8,128)}, f32[200,768]{1,0:T(8,128)}, u32[]{:S(2)}, u32[]{:S(2)}) collective-permute-start(f32[200,768]{1,0:T(8,128)} %collective-permute-done.35.rest_6_), channel_id=1, source_target_pairs={{0,8},{4,12},{8,0},{12,4},{16,24},{20,28},{24,16},{28,20},{1,9},{5... | collective-permute-start | bytes 1843208 | tf_op jit(solution)/shard_map/ppermute | solution.py:492
  184.2 16.7 %collective-permute-start.47 = (f32[200,768]{1,0:T(8,128)}, f32[200,768]{1,0:T(8,128)S(1)}, u32[]{:S(2)}, u32[]{:S(2)}) collective-permute-start(f32[200,768]{1,0:T(8,128)} %collective-permute-done.39.rest_8_), channel_id=1, source_target_pairs={{0,4},{4,0},{8,12},{12,8},{16,20},{20,16},{24,28},{28,24},{1,5},{5... | collective-permute-start | bytes 1843208 | tf_op jit(solution)/shard_map/ppermute | solution.py:492
  184.3 16.6 %collective-permute-start.46 = (f32[200,768]{1,0:T(8,128)}, f32[200,768]{1,0:T(8,128)S(1)}, u32[]{:S(2)}, u32[]{:S(2)}) collective-permute-start(f32[200,768]{1,0:T(8,128)} %copy-done.47), channel_id=1, source_target_pairs={{0,4},{4,0},{8,12},{12,8},{16,20},{20,16},{24,28},{28,24},{1,5},{5... | collective-permute-start | bytes 1843208 | tf_op jit(solution)/shard_map/ppermute | solution.py:492
  184.7 16.3 %collective-permute-start.45 = (f32[200,768]{1,0:T(8,128)S(1)}, f32[200,768]{1,0:T(8,128)S(1)}, u32[]{:S(2)}, u32[]{:S(2)}) collective-permute-start(f32[200,768]{1,0:T(8,128)S(1)} %collective-permute-done.36.rest_4_), channel_id=1, source_target_pairs={{0,4},{4,0},{8,12},{12,8},{16,20},{20,16},{24,28},{28,24},{1,5},{5... | collective-permute-start | bytes 1843208 | tf_op jit(solution)/shard_map/ppermute | solution.py:492
  184.9 16.1 %collective-permute-start.44 = (f32[200,768]{1,0:T(8,128)S(1)}, f32[200,768]{1,0:T(8,128)S(1)}, u32[]{:S(2)}, u32[]{:S(2)}) collective-permute-start(f32[200,768]{1,0:T(8,128)S(1)} %collective-permute-done.30.rest_2_), channel_id=1, source_target_pairs={{0,4},{4,0},{8,12},{12,8},{16,20},{20,16},{24,28},{28,24},{1,5},{5... | collective-permute-start | bytes 1843208 | tf_op jit(solution)/shard_map/ppermute | solution.py:492
  251.9 32.5 %collective-permute-start.53 = (f32[96,768]{1,0:T(8,128)S(1)}, f32[96,768]{1,0:T(8,128)S(1)}, u32[]{:S(2)}, u32[]{:S(2)}) collective-permute-start(f32[96,768]{1,0:T(8,128)S(1)} %get-tuple-element.434), channel_id=1, source_target_pairs={{0,8},{4,12},{8,0},{12,4},{16,24},{20,28},{24,16},{28,20},{1,9},{5... | collective-permute-start | bytes 884744 | tf_op jit(solution)/shard_map/ppermute | solution.py:492
  252.7 35.8 %collective-permute-start.54 = (f32[96,768]{1,0:T(8,128)S(1)}, f32[96,768]{1,0:T(8,128)S(1)}, u32[]{:S(2)}, u32[]{:S(2)}) collective-permute-start(f32[96,768]{1,0:T(8,128)S(1)} %get-tuple-element.433), channel_id=1, source_target_pairs={{0,16},{4,20},{8,24},{12,28},{16,0},{20,4},{24,8},{28,12},{1,17},{... | collective-permute-start | bytes 884744 | tf_op jit(solution)/shard_map/ppermute | solution.py:492
  254.0 34.5 %collective-permute-start.55 = (f32[96,768]{1,0:T(8,128)S(1)}, f32[96,768]{1,0:T(8,128)S(1)}, u32[]{:S(2)}, u32[]{:S(2)}) collective-permute-start(f32[96,768]{1,0:T(8,128)S(1)} %get-tuple-element.432), channel_id=1, source_target_pairs={{0,24},{4,28},{8,16},{12,20},{16,8},{20,12},{24,0},{28,4},{1,25},{... | collective-permute-start | bytes 884744 | tf_op jit(solution)/shard_map/ppermute | solution.py:492
  255.5 33.0 %collective-permute-start.50 = (f32[96,768]{1,0:T(8,128)S(1)}, f32[96,768]{1,0:T(8,128)S(1)}, u32[]{:S(2)}, u32[]{:S(2)}) collective-permute-start(f32[96,768]{1,0:T(8,128)S(1)} %get-tuple-element.438), channel_id=1, source_target_pairs={{0,8},{4,12},{8,0},{12,4},{16,24},{20,28},{24,16},{28,20},{1,9},{5... | collective-permute-start | bytes 884744 | tf_op jit(solution)/shard_map/ppermute | solution.py:492
  256.4 32.2 %collective-permute-start.51 = (f32[96,768]{1,0:T(8,128)S(1)}, f32[96,768]{1,0:T(8,128)S(1)}, u32[]{:S(2)}, u32[]{:S(2)}) collective-permute-start(f32[96,768]{1,0:T(8,128)S(1)} %get-tuple-element.437), channel_id=1, source_target_pairs={{0,16},{4,20},{8,24},{12,28},{16,0},{20,4},{24,8},{28,12},{1,17},{... | collective-permute-start | bytes 884744 | tf_op jit(solution)/shard_map/ppermute | solution.py:492
  293.3 18.6 %collective-permute-start.56 = (f32[96,768]{1,0:T(8,128)S(1)}, f32[96,768]{1,0:T(8,128)S(1)}, u32[]{:S(2)}, u32[]{:S(2)}) collective-permute-start(f32[96,768]{1,0:T(8,128)S(1)} %add_add_fusion.2.rest_0_), channel_id=1, source_target_pairs={{0,8},{4,12},{8,0},{12,4},{16,24},{20,28},{24,16},{28,20},{1,9},{5... | collective-permute-start | bytes 884744 | tf_op jit(solution)/shard_map/ppermute | solution.py:492
  294.8 17.0 %collective-permute-start.57 = (f32[96,768]{1,0:T(8,128)S(1)}, f32[96,768]{1,0:T(8,128)S(1)}, u32[]{:S(2)}, u32[]{:S(2)}) collective-permute-start(f32[96,768]{1,0:T(8,128)S(1)} %add_add_fusion.2.rest_0_), channel_id=1, source_target_pairs={{0,16},{4,20},{8,24},{12,28},{16,0},{20,4},{24,8},{28,12},{1,17},{... | collective-permute-start | bytes 884744 | tf_op jit(solution)/shard_map/ppermute | solution.py:492
  295.3 16.6 %collective-permute-start.58 = (f32[96,768]{1,0:T(8,128)S(1)}, f32[96,768]{1,0:T(8,128)S(1)}, u32[]{:S(2)}, u32[]{:S(2)}) collective-permute-start(f32[96,768]{1,0:T(8,128)S(1)} %add_add_fusion.2.rest_0_), channel_id=1, source_target_pairs={{0,24},{4,28},{8,16},{12,20},{16,8},{20,12},{24,0},{28,4},{1,25},{... | collective-permute-start | bytes 884744 | tf_op jit(solution)/shard_map/ppermute | solution.py:492
  318.3 22.6 %collective-permute-start.59 = (f32[96,768]{1,0:T(8,128)S(1)}, f32[96,768]{1,0:T(8,128)S(1)}, u32[]{:S(2)}, u32[]{:S(2)}) collective-permute-start(f32[96,768]{1,0:T(8,128)S(1)} %add_add_fusion.1.rest_0_), channel_id=1, source_target_pairs={{0,8},{4,12},{8,0},{12,4},{16,24},{20,28},{24,16},{28,20},{1,9},{5... | collective-permute-start | bytes 884744 | tf_op jit(solution)/shard_map/ppermute | solution.py:492
  319.9 20.9 %collective-permute-start.60 = (f32[96,768]{1,0:T(8,128)S(1)}, f32[96,768]{1,0:T(8,128)S(1)}, u32[]{:S(2)}, u32[]{:S(2)}) collective-permute-start(f32[96,768]{1,0:T(8,128)S(1)} %add_add_fusion.1.rest_0_), channel_id=1, source_target_pairs={{0,16},{4,20},{8,24},{12,28},{16,0},{20,4},{24,8},{28,12},{1,17},{... | collective-permute-start | bytes 884744 | tf_op jit(solution)/shard_map/ppermute | solution.py:492
  320.5 20.4 %collective-permute-start.61 = (f32[96,768]{1,0:T(8,128)S(1)}, f32[96,768]{1,0:T(8,128)S(1)}, u32[]{:S(2)}, u32[]{:S(2)}) collective-permute-start(f32[96,768]{1,0:T(8,128)S(1)} %add_add_fusion.1.rest_0_), channel_id=1, source_target_pairs={{0,24},{4,28},{8,16},{12,20},{16,8},{20,12},{24,0},{28,4},{1,25},{... | collective-permute-start | bytes 884744 | tf_op jit(solution)/shard_map/ppermute | solution.py:492
  322.8 18.2 %collective-permute-start.62 = (f32[384,768]{1,0:T(8,128)S(1)}, f32[384,768]{1,0:T(8,128)S(1)}, u32[]{:S(2)}, u32[]{:S(2)}) collective-permute-start(f32[384,768]{1,0:T(8,128)S(1)} %constant_dynamic-slice_fusion.4), channel_id=1, source_target_pairs={{0,4},{4,0},{8,12},{12,8},{16,20},{20,16},{24,28},{28,24},{1,5},{5... | collective-permute-start | bytes 3538952 | tf_op jit(solution)/shard_map/ppermute | solution.py:492
  341.5 22.0 %collective-permute-start.73 = (f32[96,768]{1,0:T(8,128)S(1)}, f32[96,768]{1,0:T(8,128)S(1)}, u32[]{:S(2)}, u32[]{:S(2)}) collective-permute-start(f32[96,768]{1,0:T(8,128)S(1)} %collective-permute-done.60.rest_2_), channel_id=1, source_target_pairs={{0,4},{4,0},{8,12},{12,8},{16,20},{20,16},{24,28},{28,24},{1,5},{5... | collective-permute-start | bytes 884744 | tf_op jit(solution)/shard_map/ppermute | solution.py:492
  341.6 22.0 %collective-permute-start.74 = (f32[96,768]{1,0:T(8,128)S(1)}, f32[96,768]{1,0:T(8,128)S(1)}, u32[]{:S(2)}, u32[]{:S(2)}) collective-permute-start(f32[96,768]{1,0:T(8,128)S(1)} %collective-permute-done.61.rest_3_), channel_id=1, source_target_pairs={{0,4},{4,0},{8,12},{12,8},{16,20},{20,16},{24,28},{28,24},{1,5},{5... | collective-permute-start | bytes 884744 | tf_op jit(solution)/shard_map/ppermute | solution.py:492
  346.1 17.5 %collective-permute-start.68 = (f32[96,768]{1,0:T(8,128)S(1)}, f32[96,768]{1,0:T(8,128)S(1)}, u32[]{:S(2)}, u32[]{:S(2)}) collective-permute-start(f32[96,768]{1,0:T(8,128)S(1)} %get-tuple-element.430), channel_id=1, source_target_pairs={{0,8},{4,12},{8,0},{12,4},{16,24},{20,28},{24,16},{28,20},{1,9},{5... | collective-permute-start | bytes 884744 | tf_op jit(solution)/shard_map/ppermute | solution.py:492
  347.0 16.6 %collective-permute-start.69 = (f32[96,768]{1,0:T(8,128)S(1)}, f32[96,768]{1,0:T(8,128)S(1)}, u32[]{:S(2)}, u32[]{:S(2)}) collective-permute-start(f32[96,768]{1,0:T(8,128)S(1)} %get-tuple-element.429), channel_id=1, source_target_pairs={{0,16},{4,20},{8,24},{12,28},{16,0},{20,4},{24,8},{28,12},{1,17},{... | collective-permute-start | bytes 884744 | tf_op jit(solution)/shard_map/ppermute | solution.py:492
  347.5 16.1 %collective-permute-start.70 = (f32[96,768]{1,0:T(8,128)S(1)}, f32[96,768]{1,0:T(8,128)S(1)}, u32[]{:S(2)}, u32[]{:S(2)}) collective-permute-start(f32[96,768]{1,0:T(8,128)S(1)} %get-tuple-element.428), channel_id=1, source_target_pairs={{0,24},{4,28},{8,16},{12,20},{16,8},{20,12},{24,0},{28,4},{1,25},{... | collective-permute-start | bytes 884744 | tf_op jit(solution)/shard_map/ppermute | solution.py:492
  363.7 22.1 %collective-permute-start.76 = (f32[96,768]{1,0:T(8,128)S(1)}, f32[96,768]{1,0:T(8,128)S(1)}, u32[]{:S(2)}, u32[]{:S(2)}) collective-permute-start(f32[96,768]{1,0:T(8,128)S(1)} %add_add_fusion.rest_0_), channel_id=1, source_target_pairs={{0,8},{4,12},{8,0},{12,4},{16,24},{20,28},{24,16},{28,20},{1,9},{5... | collective-permute-start | bytes 884744 | tf_op jit(solution)/shard_map/ppermute | solution.py:492
  364.6 21.2 %collective-permute-start.77 = (f32[96,768]{1,0:T(8,128)S(1)}, f32[96,768]{1,0:T(8,128)S(1)}, u32[]{:S(2)}, u32[]{:S(2)}) collective-permute-start(f32[96,768]{1,0:T(8,128)S(1)} %add_add_fusion.rest_0_), channel_id=1, source_target_pairs={{0,16},{4,20},{8,24},{12,28},{16,0},{20,4},{24,8},{28,12},{1,17},{... | collective-permute-start | bytes 884744 | tf_op jit(solution)/shard_map/ppermute | solution.py:492
  365.1 20.7 %collective-permute-start.78 = (f32[96,768]{1,0:T(8,128)S(1)}, f32[96,768]{1,0:T(8,128)S(1)}, u32[]{:S(2)}, u32[]{:S(2)}) collective-permute-start(f32[96,768]{1,0:T(8,128)S(1)} %add_add_fusion.rest_0_), channel_id=1, source_target_pairs={{0,24},{4,28},{8,16},{12,20},{16,8},{20,12},{24,0},{28,4},{1,25},{... | collective-permute-start | bytes 884744 | tf_op jit(solution)/shard_map/ppermute | solution.py:492
  367.3 17.3 %collective-permute-start.79 = (f32[16,768]{1,0:T(8,128)S(1)}, f32[16,768]{1,0:T(8,128)S(1)}, u32[]{:S(2)}, u32[]{:S(2)}) collective-permute-start(f32[16,768]{1,0:T(8,128)S(1)} %add.122), channel_id=1, source_target_pairs={{0,16},{4,20},{8,24},{12,28},{16,0},{20,4},{24,8},{28,12},{1,17},{... | collective-permute-start | bytes 147464 | tf_op jit(solution)/shard_map/ppermute | solution.py:492
  385.9 16.4 %collective-permute-start.80 = (f32[96,768]{1,0:T(8,128)S(1)}, f32[96,768]{1,0:T(8,128)S(1)}, u32[]{:S(2)}, u32[]{:S(2)}) collective-permute-start(f32[96,768]{1,0:T(8,128)S(1)} %add_add_fusion.rest_0_), channel_id=1, source_target_pairs={{0,4},{4,0},{8,12},{12,8},{16,20},{20,16},{24,28},{28,24},{1,5},{5... | collective-permute-start | bytes 884744 | tf_op jit(solution)/shard_map/ppermute | solution.py:492
  386.0 16.4 %collective-permute-start.81 = (f32[96,768]{1,0:T(8,128)S(1)}, f32[96,768]{1,0:T(8,128)S(1)}, u32[]{:S(2)}, u32[]{:S(2)}) collective-permute-start(f32[96,768]{1,0:T(8,128)S(1)} %collective-permute-done.76.rest_1_), channel_id=1, source_target_pairs={{0,4},{4,0},{8,12},{12,8},{16,20},{20,16},{24,28},{28,24},{1,5},{5... | collective-permute-start | bytes 884744 | tf_op jit(solution)/shard_map/ppermute | solution.py:492
  (121 other events, 1612.4 us)

commit v3 on v2

--- a/solution.py
+++ b/solution.py
@@ -15,7 +15,7 @@
 LANES = 8
 LOW = jnp.bfloat16
 WIDE = jnp.float32
-VMEM_LIMIT = 56 * 1024 * 1024
+VMEM_LIMIT = 26 * 1024 * 1024
 
 NN = (((1,), (0,)), ((), ()))
 NT = (((1,), (1,)), ((), ()))
@@ -25,8 +25,8 @@
     return lax.dot_general(left, right, dims, preferred_element_type=WIDE)
 
 
-def params(**kw):
-    return pltpu.CompilerParams(vmem_limit_bytes=VMEM_LIMIT, **kw)
+def params(limit=VMEM_LIMIT):
+    return pltpu.CompilerParams(vmem_limit_bytes=limit)
 
 
 def cost(count):
@@ -323,7 +323,7 @@
         out_specs=out_specs,
         out_shape=out_shape,
         input_output_aliases={1: 1} if remote else {},
-        compiler_params=params(),
+        compiler_params=params((61 if remote else 26) * 1024 * 1024),
         cost_estimate=cost(count),
     )(x, *extra, *contexts, *packs)
 
@@ -415,7 +415,7 @@
             jax.ShapeDtypeStruct((8, model), WIDE),
         ],
         input_output_aliases={1: 3},
-        compiler_params=params(),
+        compiler_params=params(61 * 1024 * 1024),
         cost_estimate=cost(count),
     )(h1, mixed, cot, *vectors, slope, wi, wd)
 
@@ -439,7 +439,7 @@
             jax.ShapeDtypeStruct((8, model), WIDE),
         ],
         input_output_aliases={1: 0},
-        compiler_params=params(),
+        compiler_params=params(61 * 1024 * 1024),
         cost_estimate=cost(count),
     )(h1, dn1, dm, gain, sums, *slopes, *wis, *wds)
 
@@ -448,40 +448,32 @@
     return lax.dot_general(left, right, (((0,), (0,)), ((), ())), preferred_element_type=WIDE)
 
 
-def assemble(turned, place_ref, *rest):
-    pieces, outs = rest[:LANES], rest[LANES:]
+def assemble(place_ref, *rest):
+    pieces, outs, out_ref = rest[:LANES], rest[LANES:-1], rest[-1]
     part = pieces[0].shape[0]
-    out_ref = rest[-1]
     core, chip = place_ref[0] % 2, place_ref[0] // 2
     for k, piece in enumerate(pieces):
         half = core if k < 4 else 1 - core
         at = pl.multiple_of((half * 4 + (chip ^ (k % 4))) * part, 8)
         out_ref[pl.ds(at, part), :] = piece[...]
-    for k in range(turned):
-        width = outs[k].shape[1]
-        outs[k][...] = out_ref[k * width : (k + 1) * width, :].T
-    if turned:
-        outs[turned][...] = out_ref[turned * width : (turned + 1) * width, :]
-
-
-def call_assemble(place, pieces, turned=0):
+    width = outs[3].shape[0]
+    for k in range(4):
+        outs[k][...] = out_ref[k * width : (k + 1) * width, :]
+    outs[4][...] = out_ref[4 * width : 4 * width + 16, :]
+
+
+def call_assemble(place, pieces, width):
     part, model = pieces[0].shape
-    total = part * LANES
-    if turned:
-        width = total // (turned + 1)
-        shapes = [(model, width)] * turned + [(width, model)]
-    else:
-        shapes = [(total, model)]
-    out = pl.pallas_call(
-        functools.partial(assemble, turned),
+    shapes = [(width, model)] * 4 + [(16, model)]
+    return pl.pallas_call(
+        assemble,
         grid=(1,),
         in_specs=[pl.BlockSpec(memory_space=pltpu.SMEM)] + [whole((part, model))] * LANES,
         out_specs=[whole(shape) for shape in shapes],
         out_shape=[jax.ShapeDtypeStruct(shape, WIDE) for shape in shapes],
-        scratch_shapes=[pltpu.VMEM((total, model), WIDE)] if turned else [],
+        scratch_shapes=[pltpu.VMEM((part * LANES, model), WIDE)],
         compiler_params=params(),
     )(place, *pieces)
-    return out
 
 
 def after(values, *done):
@@ -508,9 +500,6 @@
     def hop(self, m, mask, *done):
         self.got[m ^ mask] = swap(after(self.got[m], *done), mask, self.size)
         return self.got[m ^ mask]
-
-    def pair(self, *done):
-        return [self.hop(m, 1, *done) for m in (0, 2, 4, 6)]
 
     def slices(self):
         return [self.got[m] for m in range(LANES)]
@@ -638,15 +627,19 @@
     d, e, f = deep_of
     gate = [a.along()]
     late = c.along(gate)
-    gate = [a.hop(0, 2, gate), a.hop(0, 4, gate), a.hop(0, 6, gate), b.along(gate), forward(-1, gate)]
-    early = d.along(gate)
-    gate = [a.pair(gate), b.hop(0, 2, gate), b.hop(0, 4, gate), late]
-    late = e.along(gate)
-    gate = [forward(0, gate), b.hop(2, 4, gate), c.hop(0, 2, gate), c.hop(0, 4, gate), early]
-    gate = [b.pair(gate), c.hop(4, 2, gate), late]
+    gate = [
+        a.hop(0, 2, gate), a.hop(0, 4, gate), a.hop(0, 6, gate), b.along(gate), forward(-1, gate, deep_piece)
+    ]
+    gate = [a.hop(m, 1, gate) for m in (0, 2, 4, 6)] + [late]
+    late = d.along(gate)
+    gate = [forward(0, gate), b.hop(0, 2, gate), b.hop(0, 4, gate), b.hop(0, 6, gate), b.hop(0, 1, gate)]
+    later = e.along(gate)
+    gate = [b.hop(m, 1, gate) for m in (2, 4, 6)] + [late]
+    gate = [forward(1, gate), c.hop(0, 2, gate), c.hop(0, 4, gate), c.hop(0, 6, gate), c.hop(0, 1, gate), later]
+    begun = [d.hop(0, 2, gate), d.hop(0, 4, gate)]
+    gate = [c.hop(m, 1, gate) for m in (2, 4, 6)]
     late = f.along(gate)
-    gate = [forward(1, gate), c.pair(gate), d.hop(0, 2, gate), d.hop(0, 4, gate)]
-    gate = [forward(2, gate), d.hop(2, 4, gate), e.hop(0, 2, gate), late]
+    gate = [forward(2, gate), begun, d.hop(0, 1, gate)]
     slope, mixed, h1, n1, act = call_feed_forward(
         hidden,
         after(tokens, gate),
@@ -665,70 +658,60 @@
         wds.append(wd)
         return slope, mixed
 
-    gate = [n1, d.pair(gate), e.hop(0, 4, gate), f.hop(0, 2, gate), f.hop(0, 4, gate)]
-    begun = [e.hop(4, 2, gate), f.hop(2, 4, gate)]
+    gate = [n1, d.hop(2, 4, gate), d.hop(2, 1, gate), d.hop(4, 1, gate), e.hop(0, 2, gate), late]
+    begun = [e.hop(0, 4, gate), f.hop(0, 2, gate), e.hop(0, 1, gate), e.hop(2, 1, gate)]
+    gate = [d.hop(6, 1, gate)]
     slope, mixed = deep_forward(0, mixed, gate)
     gate = [slope, begun]
-    gate = [e.pair(gate)]
-    begun = [f.pair(gate)]
+    begun = [f.hop(0, 4, gate), f.hop(0, 1, gate), f.hop(2, 1, gate)]
+    gate = [e.hop(4, 2, gate), e.hop(4, 1, gate), begun]
+    begun = [f.hop(4, 2, gate), f.hop(4, 1, gate)]
+    gate = [e.hop(6, 1, gate)]
     slope, mixed = deep_forward(1, mixed, gate)
     gate = [slope, begun]
+    gate = [f.hop(6, 1, gate)]
     slope, mixed = deep_forward(2, mixed, gate)
 
     vectors = (row(gain_one), row(shift_one), row(down_bias), row(gain_two), row(shift_two))
     layer_out, dm, du, dn1, sums = call_middle_own(h1, mixed, cotangent, vectors, slopes[0], wis[0], wds[0])
 
-    down = Total(inner_first(act, dm), size)
-    gate = [down.value]
-    inner = Total(inner_first(n1, after(du, gate)), size)
-    gate = [down.pair(gate), inner.value]
-    gate = [inner.pair(gate)]
-    moved = [down.scatter(gate), inner.scatter(gate)]
-    dh1, da, sums = call_middle_rest(
-        h1, after(dn1, gate), dm, row(gain_one), sums, slopes[1:], wis[1:], wds[1:]
-    )
-    gate = [moved, sums]
+    own = after((inner_first(act, dm), inner_first(n1, du)), dm)
+    down_grad, inner_grad = lax.psum(own, "dp")
+    dh1, da, sums = call_middle_rest(h1, after(dn1, own), dm, row(gain_one), sums, slopes[1:], wis[1:], wds[1:])
 
     def backward(j, *done):
         qkv, context, logs, pack = saved[j]
         return call_attend_backward(j == 0, qkv, context, logs, scol, srow, after(da, *done), pack)
 
-    moved = [down.gather(gate)]
-    dqkv0, qkv_sums = backward(0, gate)
-    sums = jnp.concatenate([sums, qkv_sums], axis=0)
-    gate = [dqkv0, moved]
-    heads_grad = jnp.concatenate([inner_first(after(dqkv0, gate), tokens), inner_first(saved[0][1], da)], axis=0)
-    heads = Total(heads_grad, size)
-    gate = [heads_grad]
+    dqkv0, qkv_sums = backward(0)
+    parts = [inner_first(dqkv0, tokens), inner_first(saved[0][1], da), sums, qkv_sums]
+    used = sum(part.shape[0] for part in parts)
+    parts.append(jnp.zeros((-used % (8 * LANES), model), WIDE))
+    heads = Total(jnp.concatenate(parts, axis=0), size)
+    gate = [heads.value]
     dqkvs, packs = [dqkv0], [qkvo]
+    moved = heads.pair(gate)
     for k, j in enumerate(order):
-        if k == 0:
-            moved = [inner.gather(gate), heads.pair(gate), down.share(gate)]
-        elif k == 1:
-            moved = [heads.scatter(gate), inner.share(gate)]
-        else:
-            moved = [heads.gather(gate)]
-        mask = 1 << k
-        while mask < size:
-            sums = after(sums, gate) + swap(after(sums, gate), mask, size)
-            mask = mask * 2 if k == len(order) - 1 else size
         (grad,) = backward(j, gate)
         dqkvs.append(grad)
         packs.append(saved[j][3])
-        gate = [grad, moved, sums]
-    heads.share(gate)
+        gate = [grad]
+        if k == 0:
+            gate = [grad, moved]
+            moved = heads.scatter(gate)
+    gate = [gate, moved]
+    moved = heads.gather(gate)
     tokens_grad = call_input_gradient(after(dh1, gate), dqkvs, packs)
-    (down_grad,) = call_assemble(place_arg, down.pieces())
-    (inner_grad,) = call_assemble(place_arg, inner.pieces())
-    query_grad, key_grad, value_grad, output_grad = call_assemble(
-        place_arg, after(heads.pieces(), tokens_grad), 3
+    heads.share(tokens_grad)
+    query_grad, key_grad, value_grad, output_grad, sums = call_assemble(
+        place_arg, heads.pieces(), width
     )
     return (
         layer_out,
         tokens_grad,
-        query_grad,
-        key_grad,
-        value_grad,
+        query_grad.T,
+        key_grad.T,
+        value_grad.T,
         sums[8, :width],
         sums[8, 2 * width : 3 * width],
         output_grad,

time: 418 us -> 371 us (0.89)
  Pallas kernels: 245 us -> 212 us
  waiting for transfers between devices: 59.3 us -> 39 us
  starting transfers between devices: 64.5 us -> 45.3 us
  local copies, waits for them, and re-layouts: 20.3 us -> 37.3 us
  between operations: 2.35 us -> 15.3 us
    ppermute x6, waiting for transfers between devices: 29.8 us -> 8.45 us  [from_tensor(): lax.ppermute(value, 'tensor', [((i + shift) % groups, i) for i in range(g...]
    unnamed x174 -> x155, local copies, waits for them, and re-layouts: 12.7 us -> 32 us
    ppermute x78 -> x53, starting transfers between devices: 52.6 us -> 33.9 us  [swap(): return lax.ppermute(value, 'dp', [(i, i ^ mask) for i in range(size)])]
    pallas_call x4, Pallas kernels: 51.7 us -> 41.7 us  [call_attend_forward(): pl.pallas_call(functools.partial(attend_forward, remote, width), grid=(se...]
    pallas_call x4, Pallas kernels: 55.6 us -> 45.6 us  [call_attend_backward(): pl.pallas_call(functools.partial(attend_backward, width, own), grid=(seqs...]
    pallas_call x3 -> x1, Pallas kernels: 9.93 us -> 1.62 us  [call_assemble(): pl.pallas_call(assemble, grid=(1,), in_specs=[pl.BlockSpec(memory_space=p...]
    ppermute x78 -> x53, waiting for transfers between devices: 29.5 us -> 30.6 us  [swap(): return lax.ppermute(value, 'dp', [(i, i ^ mask) for i in range(size)])]
  transfers between devices with their start and end apart: 84 -> 60, of which waited for: 15 -> 21; matrix products, arithmetic and copies ran while one was open for 4% -> 3% of each run, Pallas kernels for 50% -> 49%
where the time goes in v3:
time: 371 us; the launch traced here: 365 us
  Pallas kernels  212 us (57%)
  starting transfers between devices  45.3 us (12%)
  waiting for transfers between devices  39 us (11%)
  local copies, waits for them, and re-layouts  37.3 us (10%)
  between operations  15.3 us (4%)
  matrix products  14 us (4%)
    pallas_call x4, Pallas kernels, call_feed_forward(): pl.pallas_call(functools.partial(feed_forward, remote), grid=(count // bl...  64.1 us
    pallas_call x4, Pallas kernels, call_attend_backward(): pl.pallas_call(functools.partial(attend_backward, width, own), grid=(seqs...  45.6 us
    pallas_call x4, Pallas kernels, call_attend_forward(): pl.pallas_call(functools.partial(attend_forward, remote, width), grid=(se...  41.7 us
    ppermute x53, starting transfers between devices, swap(): return lax.ppermute(value, 'dp', [(i, i ^ mask) for i in range(size)])  33.9 us
    unnamed x155, local copies, waits for them, and re-layouts  32 us
    ppermute x53, waiting for transfers between devices, swap(): return lax.ppermute(value, 'dp', [(i, i ^ mask) for i in range(size)])  30.6 us
    pallas_call x1, Pallas kernels, call_middle_rest(): pl.pallas_call(functools.partial(middle_rest, groups), grid=(count // blo...  27.4 us
    pallas_call x1, Pallas kernels, call_middle_own(): pl.pallas_call(middle_own, grid=(count // block,), in_specs=[rows(block,...  18.2 us
  transfers between devices with their start and end apart: 60, of which 21 were waited for; matrix products, arithmetic and copies ran while one was open for 3% of the time, Pallas kernels for 49%

profile of v3, /device:TPU:0, one launch (start us, length us, event | category | flops | bytes accessed | tf_op | source)
XLA Modules:
  0.0 365.3 jit_solution(4920259174503616526)
XLA Ops:
  9.5 5.0 %collective-permute-start = (f32[104,768]{1,0:T(8,128)}, f32[104,768]{1,0:T(8,128)}, u32[]{:S(2)}, u32[]{:S(2)}) collective-permute-start(f32[104,768]{1,0:T(8,128)} %select_maximum_fusion.1), channel_id=1, source_target_pairs={{1,0},{2,1},{3,2},{0,3},{5,4},{6,5},{7,6},{4,7},{9,8},{10,9},{11,1... | collective-permute-start | bytes 958472 | tf_op jit(solution)/shard_map/ppermute | solution.py:488
  14.6 1.6 copy.43
  18.4 3.3 collective-permute-done.rest_1_
  21.7 1.5 collective-permute-start.3
  23.2 1.5 collective-permute-start.4
  25.6 4.4 %collective-permute-start.1 = (f32[104,768]{1,0:T(8,128)}, f32[104,768]{1,0:T(8,128)S(1)}, u32[]{:S(2)}, u32[]{:S(2)}) collective-permute-start(f32[104,768]{1,0:T(8,128)} %select_maximum_fusion.1), channel_id=1, source_target_pairs={{2,0},{3,1},{0,2},{1,3},{6,4},{7,5},{4,6},{5,7},{10,8},{11,9},{8,1... | collective-permute-start | bytes 958472 | tf_op jit(solution)/shard_map/ppermute | solution.py:488
  31.3 1.9 copy-done.7
  33.1 9.9 %shard_map.305 = (bf16[2048,576]{1,0:T(8,128)(2,1)S(1)}, bf16[2048,192]{1,0:T(8,128)(2,1)S(1)}, f32[4,8,512]{2,1,0:T(8,128)S(1)}) custom-call(bf16[2048,768]{1,0:T(8,128)(2,1)S(1)} %copy-done.7, s32[2048,1]{1,0:T(8,128)S(1)} %copy-done.1, s32[4,1,512]{2,1,0:T(1,128)S(1)} %bitcast.30, f32[1,576]{1,0:T(1,128)S(1)} %reshape.82.rest_0_, ...), custom_call_target="tpu_custom_call" | custom-call | flops 15360000000 | bytes 16777216 | tf_op jit(solution)/shard_map/pallas_call | solution.py:164
  43.1 1.5 copy-done.30
  46.4 2.8 collective-permute-done.1.rest_1_
  49.2 1.6 collective-permute-start.10
  50.8 1.5 collective-permute-start.11
  52.8 11.2 %shard_map.306 = (bf16[2048,576]{1,0:T(8,128)(2,1)S(1)}, bf16[2048,192]{1,0:T(8,128)(2,1)S(1)}, f32[4,8,512]{2,1,0:T(8,128)S(1)}, bf16[768,768]{1,0:T(8,128)(2,1)S(1)}) custom-call(bf16[2048,768]{1,0:T(8,128)(2,1)S(1)} %copy-done.7, s32[2048,1]{1,0:T(8,128)S(1)} %copy-done.1, s32[4,1,512]{2,1,0:T(1,128)S(1)} %bitcast.31, s32[1]{0:T(128)} %bitcast.2.rest_0_.rest_1_.place_ref, ...), custom_call_target="tpu_custom_call" | custom-call | flops 15360000000 | bytes 16777216 | tf_op jit(solution)/shard_map/pallas_call | solution.py:164
  64.0 1.4 copy-done.24
  70.8 1.4 collective-permute-start.20
  73.1 10.2 %shard_map.307 = (bf16[2048,576]{1,0:T(8,128)(2,1)S(1)}, bf16[2048,192]{1,0:T(8,128)(2,1)S(1)}, f32[4,8,512]{2,1,0:T(8,128)S(1)}, bf16[768,768]{1,0:T(8,128)(2,1)S(1)}) custom-call(bf16[2048,768]{1,0:T(8,128)(2,1)S(1)} %copy-done.7, s32[2048,1]{1,0:T(8,128)S(1)} %copy-done.1, s32[4,1,512]{2,1,0:T(1,128)S(1)} %bitcast.32, s32[1]{0:T(128)} %bitcast.2.rest_0_.rest_1_.place_ref, ...), custom_call_target="tpu_custom_call" | custom-call | flops 15360000000 | bytes 16777216 | tf_op jit(solution)/shard_map/pallas_call | solution.py:164
  84.0 2.1 collective-permute-done.22.rest_2_
  90.3 10.3 %shard_map.308 = (bf16[2048,576]{1,0:T(8,128)(2,1)S(1)}, bf16[2048,192]{1,0:T(8,128)(2,1)S(1)}, f32[4,8,512]{2,1,0:T(8,128)S(1)}, bf16[768,768]{1,0:T(8,128)(2,1)S(1)}) custom-call(bf16[2048,768]{1,0:T(8,128)(2,1)S(1)} %copy-done.7, s32[2048,1]{1,0:T(8,128)S(1)} %copy-done.1, s32[4,1,512]{2,1,0:T(1,128)S(1)} %bitcast.33, s32[1]{0:T(128)} %bitcast.2.rest_0_.rest_1_.place_ref, ...), custom_call_target="tpu_custom_call" | custom-call | flops 15360000000 | bytes 16777216 | tf_op jit(solution)/shard_map/pallas_call | solution.py:164
  100.7 1.5 copy-done.28
  102.2 1.9 collective-permute-done.26.rest_4_
  107.6 17.0 %shard_map.309 = (bf16[2048,768]{1,0:T(8,128)(2,1)S(1)}, f32[2048,768]{1,0:T(8,128)}, f32[2048,768]{1,0:T(8,128)}, bf16[2048,768]{1,0:T(8,128)(2,1)S(1)}, bf16[2048,768]{1,0:T(8,128)(2,1)S(1)}) custom-call(bf16[2048,768]{1,0:T(8,128)(2,1)S(1)} %copy-done.8, f32[1,768]{1,0:T(1,128)S(1)} %reshape.83.rest_0_, f32[1,768]{1,0:T(1,128)S(1)} %reshape.84.rest_1_, ...), custom_call_target="tpu_custom_call" | custom-call | flops 15360000000 | bytes 16777216 | tf_op jit(solution)/shard_map/pallas_call | solution.py:319
  124.7 1.7 copy-done.14
  126.4 1.6 copy-done.16
  128.1 1.6 copy-done.17
  133.2 15.8 %shard_map.310 = (bf16[2048,768]{1,0:T(8,128)(2,1)}, f32[2048,768]{1,0:T(8,128)}, bf16[768,768]{1,0:T(8,128)(2,1)}, bf16[768,768]{1,0:T(8,128)(2,1)}) custom-call(bf16[2048,768]{1,0:T(8,128)(2,1)} %copy-done.16, f32[2048,768]{1,0:T(8,128)} %get-tuple-element.220.rest_0_, s32[1]{0:T(128)} %bitcast.2.rest_0_.rest_1_.place_ref, ...), custom_call_target="tpu_custom_call", output_to_operand_aliasing={{1}: (1, {})} | custom-call | flops 15360000000 | bytes 16777216 | tf_op jit(solution)/shard_map/pallas_call | solution.py:319
  153.8 1.9 collective-permute-done.43.rest_5_
  155.6 11.6 %collective-permute-done.41.rest_6_ = f32[200,768]{1,0:T(8,128)S(1)} collective-permute-done((f32[200,768]{1,0:T(8,128)}, f32[200,768]{1,0:T(8,128)S(1)}, u32[]{:S(2)}, u32[]{:S(2)}) %collective-permute-start.41) | collective-permute-done | bytes 614432 | tf_op jit(solution)/shard_map/ppermute | solution.py:484
  167.2 1.6 collective-permute-done.40.rest_8_
  172.6 15.6 %shard_map.311 = (bf16[2048,768]{1,0:T(8,128)(2,1)}, f32[2048,768]{1,0:T(8,128)}, bf16[768,768]{1,0:T(8,128)(2,1)}, bf16[768,768]{1,0:T(8,128)(2,1)}) custom-call(bf16[2048,768]{1,0:T(8,128)(2,1)} %copy-done.16, f32[2048,768]{1,0:T(8,128)} %get-tuple-element.234.rest_0_, s32[1]{0:T(128)} %bitcast.2.rest_0_.rest_1_.place_ref, ...), custom_call_target="tpu_custom_call", output_to_operand_aliasing={{1}: (1, {})} | custom-call | flops 15360000000 | bytes 16777216 | tf_op jit(solution)/shard_map/pallas_call | solution.py:319
  191.4 15.6 %shard_map.312 = (bf16[2048,768]{1,0:T(8,128)(2,1)}, f32[2048,768]{1,0:T(8,128)}, bf16[768,768]{1,0:T(8,128)(2,1)}, bf16[768,768]{1,0:T(8,128)(2,1)}) custom-call(bf16[2048,768]{1,0:T(8,128)(2,1)} %copy-done.16, f32[2048,768]{1,0:T(8,128)} %get-tuple-element.251.rest_0_, s32[1]{0:T(128)} %bitcast.2.rest_0_.rest_1_.place_ref, ...), custom_call_target="tpu_custom_call", output_to_operand_aliasing={{1}: (1, {})} | custom-call | flops 15360000000 | bytes 16777216 | tf_op jit(solution)/shard_map/pallas_call | solution.py:319
  207.0 18.2 %shard_map.313 = (bf16[2048,768]{1,0:T(8,128)(2,1)}, bf16[2048,768]{1,0:T(8,128)(2,1)}, bf16[2048,768]{1,0:T(8,128)(2,1)}, f32[2048,768]{1,0:T(8,128)}, f32[8,768]{1,0:T(8,128)}) custom-call(f32[2048,768]{1,0:T(8,128)} %get-tuple-element.218.h1_ref, f32[2048,768]{1,0:T(8,128)} %get-tuple-element.263.m_ref, ...), custom_call_target="tpu_custom_call", output_to_operand_aliasing={{3}: (1, {})} | custom-call | flops 15360000000 | bytes 16777216 | tf_op jit(solution)/shard_map/pallas_call | solution.py:405
  225.3 7.1 %fusion.2 = f32[768,768]{1,0:T(8,128)} fusion(bf16[2048,768]{1,0:T(8,128)(2,1)} %copy-done.16, bf16[2048,768]{1,0:T(8,128)(2,1)} %get-tuple-element.269), kind=kOutput, calls=%fused_computation.31 | convolution fusion | flops 2415919104 | bytes 8650752 | tf_op jit(solution)/shard_map/dot_general | solution.py:448
  232.4 4.1 %fusion.1 = f32[768,768]{1,0:T(8,128)} fusion(bf16[2048,768]{1,0:T(8,128)(2,1)S(1)} %copy-done.15, bf16[2048,768]{1,0:T(8,128)(2,1)S(1)} %copy-done.74), kind=kOutput, calls=%fused_computation.30 | convolution fusion | flops 2415919104 | bytes 8650752 | tf_op jit(solution)/shard_map/dot_general | solution.py:448
  236.5 27.4 %shard_map.314 = (f32[2048,768]{1,0:T(8,128)}, bf16[2048,768]{1,0:T(8,128)(2,1)}, f32[8,768]{1,0:T(8,128)}) custom-call(f32[2048,768]{1,0:T(8,128)} %get-tuple-element.218.h1_ref, f32[2048,768]{1,0:T(8,128)} %get-tuple-element.272.dn1_ref, bf16[2048,768]{1,0:T(8,128)(2,1)} %get-tuple-element.268.dm_ref, ...), custom_call_target="tpu_custom_call", output_to_operand_aliasing={{0}: (1, {})} | custom-call | flops 15360000000 | bytes 16777216 | tf_op jit(solution)/shard_map/pallas_call | solution.py:428
  263.9 1.9 copy-done.10
  267.0 1.8 copy-done.31
  268.8 12.0 %shard_map.315 = (bf16[2048,576]{1,0:T(8,128)(2,1)S(1)}, f32[8,768]{1,0:T(8,128)S(1)}) custom-call(bf16[2048,576]{1,0:T(8,128)(2,1)S(1)} %copy-done.31, bf16[2048,192]{1,0:T(8,128)(2,1)S(1)} %copy-done.13, f32[4,8,512]{2,1,0:T(8,128)S(1)} %copy-done.45, s32[2048,1]{1,0:T(8,128)S(1)} %copy-done.2, s32[4,1,512]{2,1,0:T(1,128)S(1)} %bitcast.34, ...), custom_call_target="tpu_custom_call" | custom-call | flops 15360000000 | bytes 16777216 | tf_op jit(solution)/shard_map/pallas_call | solution.py:194
  280.8 2.1 convolution_dynamic-update-slice_fusion
  286.4 11.2 %shard_map.316.rest_1_ = bf16[2048,576]{1,0:T(8,128)(2,1)S(1)} custom-call(bf16[2048,576]{1,0:T(8,128)(2,1)S(1)} %copy-done.25, bf16[2048,192]{1,0:T(8,128)(2,1)S(1)} %copy-done.33, f32[4,8,512]{2,1,0:T(8,128)S(1)} %copy-done.39, s32[2048,1]{1,0:T(8,128)S(1)} %copy-done.2, s32[4,1,512]{2,1,0:T(1,128)S(1)} %bitcast.35, bf16[2048,768]{1,0:T(8,128)(2,1)S(1)} %copy-done.11, ...), custom_call_target="tpu_custom_call" | custom-call | flops 15360000000 | bytes 16777216 | tf_op jit(solution)/shard_map/pallas_call | solution.py:194
  298.8 2.7 collective-permute-start.51
  301.5 11.2 %shard_map.317.rest_2_ = bf16[2048,576]{1,0:T(8,128)(2,1)S(1)} custom-call(bf16[2048,576]{1,0:T(8,128)(2,1)S(1)} %copy-done.27, bf16[2048,192]{1,0:T(8,128)(2,1)S(1)} %copy-done.35, f32[4,8,512]{2,1,0:T(8,128)S(1)} %copy-done.41, s32[2048,1]{1,0:T(8,128)S(1)} %copy-done.2, s32[4,1,512]{2,1,0:T(1,128)S(1)} %bitcast.36, bf16[2048,768]{1,0:T(8,128)(2,1)S(1)} %copy-done.11, ...), custom_call_target="tpu_custom_call" | custom-call | flops 15360000000 | bytes 16777216 | tf_op jit(solution)/shard_map/pallas_call | solution.py:194
  312.8 11.3 %shard_map.318.rest_3_ = bf16[2048,576]{1,0:T(8,128)(2,1)S(1)} custom-call(bf16[2048,576]{1,0:T(8,128)(2,1)S(1)} %copy-done.29, bf16[2048,192]{1,0:T(8,128)(2,1)S(1)} %copy-done.37, f32[4,8,512]{2,1,0:T(8,128)S(1)} %copy-done.43, s32[2048,1]{1,0:T(8,128)S(1)} %copy-done.2, s32[4,1,512]{2,1,0:T(1,128)S(1)} %bitcast.37, bf16[2048,768]{1,0:T(8,128)(2,1)S(1)} %copy-done.11, ...), custom_call_target="tpu_custom_call" | custom-call | flops 15360000000 | bytes 16777216 | tf_op jit(solution)/shard_map/pallas_call | solution.py:194
  324.1 2.0 collective-permute-done.51
  326.8 3.4 collective-permute-start.53
  330.2 13.1 %shard_map.319 = f32[2048,768]{1,0:T(8,128)} custom-call(f32[2048,768]{1,0:T(8,128)} %get-tuple-element.295.dh1_ref, bf16[2048,576]{1,0:T(8,128)(2,1)S(1)} %get-tuple-element.287.rest_0_, bf16[2048,576]{1,0:T(8,128)(2,1)S(1)} %shard_map.316.rest_1_, bf16[2048,576]{1,0:T(8,128)(2,1)S(1)} %shard_map.317.rest_2_, ...), custom_call_target="tpu_custom_call", output_to_operand_aliasing={{}: (0, {})} | custom-call | flops 15360000000 | bytes 16777216 | tf_op jit(solution)/shard_map/pallas_call | solution.py:218
  343.3 4.3 %collective-permute-done.53.rest_2_ = f32[104,768]{1,0:T(8,128)S(1)} collective-permute-done((f32[104,768]{1,0:T(8,128)S(1)}, f32[104,768]{1,0:T(8,128)S(1)}, u32[]{:S(2)}, u32[]{:S(2)}) %collective-permute-start.53) | collective-permute-done | bytes 319520 | tf_op jit(solution)/shard_map/ppermute | solution.py:484
  350.6 1.6 shard_map.320
  353.5 3.4 copy.65
  (273 shorter events, 50.4 us)
Async XLA Ops:
  7.2 346.3 %all-reduce.5.cloned.1.call-start = ((), (), s32[]{:S(2)}) async-start(), calls=%async_computation | async-start | bytes 9437184 | tf_op jit(solution)/shard_map/psum | solution.py:679
  9.5 12.2 %collective-permute-start = (f32[104,768]{1,0:T(8,128)}, f32[104,768]{1,0:T(8,128)}, u32[]{:S(2)}, u32[]{:S(2)}) collective-permute-start(f32[104,768]{1,0:T(8,128)} %select_maximum_fusion.1), channel_id=1, source_target_pairs={{1,0},{2,1},{3,2},{0,3},{5,4},{6,5},{7,6},{4,7},{9,8},{10,9},{11,1... | collective-permute-start | bytes 958472 | tf_op jit(solution)/shard_map/ppermute | solution.py:488
  21.7 23.5 %collective-permute-start.3 = (f32[104,768]{1,0:T(8,128)}, f32[104,768]{1,0:T(8,128)S(1)}, u32[]{:S(2)}, u32[]{:S(2)}) collective-permute-start(f32[104,768]{1,0:T(8,128)} %collective-permute-done.rest_1_), channel_id=1, source_target_pairs={{0,8},{4,12},{8,0},{12,4},{16,24},{20,28},{24,16},{28,20},{1,9},{5... | collective-permute-start | bytes 958472 | tf_op jit(solution)/shard_map/ppermute | solution.py:484
  23.2 22.1 %collective-permute-start.4 = (f32[104,768]{1,0:T(8,128)}, f32[104,768]{1,0:T(8,128)S(1)}, u32[]{:S(2)}, u32[]{:S(2)}) collective-permute-start(f32[104,768]{1,0:T(8,128)} %collective-permute-done.rest_1_), channel_id=1, source_target_pairs={{0,16},{4,20},{8,24},{12,28},{16,0},{20,4},{24,8},{28,12},{1,17},{... | collective-permute-start | bytes 958472 | tf_op jit(solution)/shard_map/ppermute | solution.py:484
  24.7 20.5 %collective-permute-start.5 = (f32[104,768]{1,0:T(8,128)}, f32[104,768]{1,0:T(8,128)S(1)}, u32[]{:S(2)}, u32[]{:S(2)}) collective-permute-start(f32[104,768]{1,0:T(8,128)} %collective-permute-done.rest_1_), channel_id=1, source_target_pairs={{0,24},{4,28},{8,16},{12,20},{16,8},{20,12},{24,0},{28,4},{1,25},{... | collective-permute-start | bytes 958472 | tf_op jit(solution)/shard_map/ppermute | solution.py:484
  25.2 20.1 %collective-permute-start.2 = (f32[104,768]{1,0:T(8,128)}, f32[104,768]{1,0:T(8,128)S(1)}, u32[]{:S(2)}, u32[]{:S(2)}) collective-permute-start(f32[104,768]{1,0:T(8,128)} %select_maximum_fusion.1), channel_id=1, source_target_pairs={{3,0},{0,1},{1,2},{2,3},{7,4},{4,5},{5,6},{6,7},{11,8},{8,9},{9,10... | collective-permute-start | bytes 958472 | tf_op jit(solution)/shard_map/ppermute | solution.py:488
  25.6 23.5 %collective-permute-start.1 = (f32[104,768]{1,0:T(8,128)}, f32[104,768]{1,0:T(8,128)S(1)}, u32[]{:S(2)}, u32[]{:S(2)}) collective-permute-start(f32[104,768]{1,0:T(8,128)} %select_maximum_fusion.1), channel_id=1, source_target_pairs={{2,0},{3,1},{0,2},{1,3},{6,4},{7,5},{4,6},{5,7},{10,8},{11,9},{8,1... | collective-permute-start | bytes 958472 | tf_op jit(solution)/shard_map/ppermute | solution.py:488
  45.3 3.9 %collective-permute-start.9 = (f32[104,768]{1,0:T(8,128)S(1)}, f32[104,768]{1,0:T(8,128)S(1)}, u32[]{:S(2)}, u32[]{:S(2)}) collective-permute-start(f32[104,768]{1,0:T(8,128)S(1)} %collective-permute-done.5.rest_7_), channel_id=1, source_target_pairs={{0,4},{4,0},{8,12},{12,8},{16,20},{20,16},{24,28},{28,24},{1,5},{5... | collective-permute-start | bytes 958472 | tf_op jit(solution)/shard_map/ppermute | solution.py:484
  45.3 3.9 %collective-permute-start.8 = (f32[104,768]{1,0:T(8,128)S(1)}, f32[104,768]{1,0:T(8,128)S(1)}, u32[]{:S(2)}, u32[]{:S(2)}) collective-permute-start(f32[104,768]{1,0:T(8,128)S(1)} %collective-permute-done.4.rest_5_), channel_id=1, source_target_pairs={{0,4},{4,0},{8,12},{12,8},{16,20},{20,16},{24,28},{28,24},{1,5},{5... | collective-permute-start | bytes 958472 | tf_op jit(solution)/shard_map/ppermute | solution.py:484
  45.8 3.4 collective-permute-start.7
  45.9 3.3 collective-permute-start.6
  49.2 16.3 %collective-permute-start.10 = (f32[104,768]{1,0:T(8,128)S(1)}, f32[104,768]{1,0:T(8,128)S(1)}, u32[]{:S(2)}, u32[]{:S(2)}) collective-permute-start(f32[104,768]{1,0:T(8,128)S(1)} %collective-permute-done.2.rest_1_), channel_id=1, source_target_pairs={{0,8},{4,12},{8,0},{12,4},{16,24},{20,28},{24,16},{28,20},{1,9},{5... | collective-permute-start | bytes 958472 | tf_op jit(solution)/shard_map/ppermute | solution.py:484
  50.8 16.0 %collective-permute-start.11 = (f32[104,768]{1,0:T(8,128)S(1)}, f32[104,768]{1,0:T(8,128)S(1)}, u32[]{:S(2)}, u32[]{:S(2)}) collective-permute-start(f32[104,768]{1,0:T(8,128)S(1)} %collective-permute-done.2.rest_1_), channel_id=1, source_target_pairs={{0,16},{4,20},{8,24},{12,28},{16,0},{20,4},{24,8},{28,12},{1,17},{... | collective-permute-start | bytes 958472 | tf_op jit(solution)/shard_map/ppermute | solution.py:484
  52.3 14.5 %collective-permute-start.12 = (f32[104,768]{1,0:T(8,128)S(1)}, f32[104,768]{1,0:T(8,128)S(1)}, u32[]{:S(2)}, u32[]{:S(2)}) collective-permute-start(f32[104,768]{1,0:T(8,128)S(1)} %collective-permute-done.2.rest_1_), channel_id=1, source_target_pairs={{0,24},{4,28},{8,16},{12,20},{16,8},{20,12},{24,0},{28,4},{1,25},{... | collective-permute-start | bytes 958472 | tf_op jit(solution)/shard_map/ppermute | solution.py:484
  52.8 14.0 %collective-permute-start.13 = (f32[104,768]{1,0:T(8,128)S(1)}, f32[104,768]{1,0:T(8,128)S(1)}, u32[]{:S(2)}, u32[]{:S(2)}) collective-permute-start(f32[104,768]{1,0:T(8,128)S(1)} %collective-permute-done.2.rest_1_), channel_id=1, source_target_pairs={{0,4},{4,0},{8,12},{12,8},{16,20},{20,16},{24,28},{28,24},{1,5},{5... | collective-permute-start | bytes 958472 | tf_op jit(solution)/shard_map/ppermute | solution.py:484
  52.8 16.3 %collective-permute-start.17 = (f32[200,768]{1,0:T(8,128)S(1)}, f32[200,768]{1,0:T(8,128)S(1)}, u32[]{:S(2)}, u32[]{:S(2)}) collective-permute-start(f32[200,768]{1,0:T(8,128)S(1)} %select_maximum_fusion), channel_id=1, source_target_pairs={{1,0},{2,1},{3,2},{0,3},{5,4},{6,5},{7,6},{4,7},{9,8},{10,9},{11,1... | collective-permute-start | bytes 1843208 | tf_op jit(solution)/shard_map/ppermute | solution.py:488
  67.5 18.6 %collective-permute-start.22 = (f32[200,768]{1,0:T(8,128)S(1)}, f32[200,768]{1,0:T(8,128)}, u32[]{:S(2)}, u32[]{:S(2)}) collective-permute-start(f32[200,768]{1,0:T(8,128)S(1)} %select_maximum_fusion), channel_id=1, source_target_pairs={{3,0},{0,1},{1,2},{2,3},{7,4},{4,5},{5,6},{6,7},{11,8},{8,9},{9,10... | collective-permute-start | bytes 1843208 | tf_op jit(solution)/shard_map/ppermute | solution.py:488
  69.4 16.7 %collective-permute-start.18 = (f32[104,768]{1,0:T(8,128)S(1)}, f32[104,768]{1,0:T(8,128)S(1)}, u32[]{:S(2)}, u32[]{:S(2)}) collective-permute-start(f32[104,768]{1,0:T(8,128)S(1)} %collective-permute-done.1.rest_1_), channel_id=1, source_target_pairs={{0,4},{4,0},{8,12},{12,8},{16,20},{20,16},{24,28},{28,24},{1,5},{5... | collective-permute-start | bytes 958472 | tf_op jit(solution)/shard_map/ppermute | solution.py:484
  69.6 16.5 %collective-permute-start.19 = (f32[104,768]{1,0:T(8,128)S(1)}, f32[104,768]{1,0:T(8,128)S(1)}, u32[]{:S(2)}, u32[]{:S(2)}) collective-permute-start(f32[104,768]{1,0:T(8,128)S(1)} %collective-permute-done.1.rest_1_), channel_id=1, source_target_pairs={{0,8},{4,12},{8,0},{12,4},{16,24},{20,28},{24,16},{28,20},{1,9},{5... | collective-permute-start | bytes 958472 | tf_op jit(solution)/shard_map/ppermute | solution.py:484
  70.8 15.4 %collective-permute-start.20 = (f32[104,768]{1,0:T(8,128)S(1)}, f32[104,768]{1,0:T(8,128)S(1)}, u32[]{:S(2)}, u32[]{:S(2)}) collective-permute-start(f32[104,768]{1,0:T(8,128)S(1)} %collective-permute-done.1.rest_1_), channel_id=1, source_target_pairs={{0,16},{4,20},{8,24},{12,28},{16,0},{20,4},{24,8},{28,12},{1,17},{... | collective-permute-start | bytes 958472 | tf_op jit(solution)/shard_map/ppermute | solution.py:484
  72.2 15.0 %collective-permute-start.21 = (f32[104,768]{1,0:T(8,128)S(1)}, f32[104,768]{1,0:T(8,128)S(1)}, u32[]{:S(2)}, u32[]{:S(2)}) collective-permute-start(f32[104,768]{1,0:T(8,128)S(1)} %collective-permute-done.1.rest_1_), channel_id=1, source_target_pairs={{0,24},{4,28},{8,16},{12,20},{16,8},{20,12},{24,0},{28,4},{1,25},{... | collective-permute-start | bytes 958472 | tf_op jit(solution)/shard_map/ppermute | solution.py:484
  87.2 3.0 collective-permute-start.25
  87.8 16.3 %collective-permute-start.26 = (f32[200,768]{1,0:T(8,128)S(1)}, f32[200,768]{1,0:T(8,128)S(1)}, u32[]{:S(2)}, u32[]{:S(2)}) collective-permute-start(f32[200,768]{1,0:T(8,128)S(1)} %collective-permute-done.17.rest_2_), channel_id=1, source_target_pairs={{0,8},{4,12},{8,0},{12,4},{16,24},{20,28},{24,16},{28,20},{1,9},{5... | collective-permute-start | bytes 1843208 | tf_op jit(solution)/shard_map/ppermute | solution.py:484
  89.1 16.0 %collective-permute-start.27 = (f32[200,768]{1,0:T(8,128)S(1)}, f32[200,768]{1,0:T(8,128)S(1)}, u32[]{:S(2)}, u32[]{:S(2)}) collective-permute-start(f32[200,768]{1,0:T(8,128)S(1)} %collective-permute-done.17.rest_2_), channel_id=1, source_target_pairs={{0,16},{4,20},{8,24},{12,28},{16,0},{20,4},{24,8},{28,12},{1,17},{... | collective-permute-start | bytes 1843208 | tf_op jit(solution)/shard_map/ppermute | solution.py:484
  90.2 39.5 %collective-permute-start.33 = (f32[200,768]{1,0:T(8,128)S(1)}, f32[200,768]{1,0:T(8,128)}, u32[]{:S(2)}, u32[]{:S(2)}) collective-permute-start(f32[200,768]{1,0:T(8,128)S(1)} %select_maximum_fusion), channel_id=1, source_target_pairs={{2,0},{3,1},{0,2},{1,3},{6,4},{7,5},{4,6},{5,7},{10,8},{11,9},{8,1... | collective-permute-start | bytes 1843208 | tf_op jit(solution)/shard_map/ppermute | solution.py:488
  90.3 14.8 %collective-permute-start.28 = (f32[200,768]{1,0:T(8,128)S(1)}, f32[200,768]{1,0:T(8,128)S(1)}, u32[]{:S(2)}, u32[]{:S(2)}) collective-permute-start(f32[200,768]{1,0:T(8,128)S(1)} %collective-permute-done.17.rest_2_), channel_id=1, source_target_pairs={{0,4},{4,0},{8,12},{12,8},{16,20},{20,16},{24,28},{28,24},{1,5},{5... | collective-permute-start | bytes 1843208 | tf_op jit(solution)/shard_map/ppermute | solution.py:484
  105.0 24.7 %collective-permute-start.29 = (f32[200,768]{1,0:T(8,128)S(1)}, f32[200,768]{1,0:T(8,128)S(1)}, u32[]{:S(2)}, u32[]{:S(2)}) collective-permute-start(f32[200,768]{1,0:T(8,128)S(1)} %collective-permute-done.26.rest_4_), channel_id=1, source_target_pairs={{0,4},{4,0},{8,12},{12,8},{16,20},{20,16},{24,28},{28,24},{1,5},{5... | collective-permute-start | bytes 1843208 | tf_op jit(solution)/shard_map/ppermute | solution.py:484
  105.1 24.6 %collective-permute-start.31 = (f32[200,768]{1,0:T(8,128)S(1)}, f32[200,768]{1,0:T(8,128)S(1)}, u32[]{:S(2)}, u32[]{:S(2)}) collective-permute-start(f32[200,768]{1,0:T(8,128)S(1)} %collective-permute-done.26.rest_4_), channel_id=1, source_target_pairs={{0,16},{4,20},{8,24},{12,28},{16,0},{20,4},{24,8},{28,12},{1,17},{... | collective-permute-start | bytes 1843208 | tf_op jit(solution)/shard_map/ppermute | solution.py:484
  106.3 23.4 %collective-permute-start.32 = (f32[200,768]{1,0:T(8,128)}, f32[200,768]{1,0:T(8,128)}, u32[]{:S(2)}, u32[]{:S(2)}) collective-permute-start(f32[200,768]{1,0:T(8,128)} %collective-permute-done.22.rest_2_), channel_id=1, source_target_pairs={{0,8},{4,12},{8,0},{12,4},{16,24},{20,28},{24,16},{28,20},{1,9},{5... | collective-permute-start | bytes 1843208 | tf_op jit(solution)/shard_map/ppermute | solution.py:484
  107.5 22.2 %collective-permute-start.30 = (f32[200,768]{1,0:T(8,128)S(1)}, f32[200,768]{1,0:T(8,128)S(1)}, u32[]{:S(2)}, u32[]{:S(2)}) collective-permute-start(f32[200,768]{1,0:T(8,128)S(1)} %collective-permute-done.27.rest_6_), channel_id=1, source_target_pairs={{0,4},{4,0},{8,12},{12,8},{16,20},{20,16},{24,28},{28,24},{1,5},{5... | collective-permute-start | bytes 1843208 | tf_op jit(solution)/shard_map/ppermute | solution.py:484
  130.3 18.7 %collective-permute-start.35 = (f32[200,768]{1,0:T(8,128)}, f32[200,768]{1,0:T(8,128)S(1)}, u32[]{:S(2)}, u32[]{:S(2)}) collective-permute-start(f32[200,768]{1,0:T(8,128)} %collective-permute-done.22.rest_2_), channel_id=1, source_target_pairs={{0,4},{4,0},{8,12},{12,8},{16,20},{20,16},{24,28},{28,24},{1,5},{5... | collective-permute-start | bytes 1843208 | tf_op jit(solution)/shard_map/ppermute | solution.py:484
  130.6 18.4 %collective-permute-start.37 = (f32[200,768]{1,0:T(8,128)}, f32[200,768]{1,0:T(8,128)S(1)}, u32[]{:S(2)}, u32[]{:S(2)}) collective-permute-start(f32[200,768]{1,0:T(8,128)} %collective-permute-done.22.rest_2_), channel_id=1, source_target_pairs={{0,16},{4,20},{8,24},{12,28},{16,0},{20,4},{24,8},{28,12},{1,17},{... | collective-permute-start | bytes 1843208 | tf_op jit(solution)/shard_map/ppermute | solution.py:484
  131.1 17.8 %collective-permute-start.38 = (f32[200,768]{1,0:T(8,128)}, f32[200,768]{1,0:T(8,128)S(1)}, u32[]{:S(2)}, u32[]{:S(2)}) collective-permute-start(f32[200,768]{1,0:T(8,128)} %collective-permute-done.33.rest_2_), channel_id=1, source_target_pairs={{0,8},{4,12},{8,0},{12,4},{16,24},{20,28},{24,16},{28,20},{1,9},{5... | collective-permute-start | bytes 1843208 | tf_op jit(solution)/shard_map/ppermute | solution.py:484
  132.3 16.7 %collective-permute-start.36 = (f32[200,768]{1,0:T(8,128)}, f32[200,768]{1,0:T(8,128)}, u32[]{:S(2)}, u32[]{:S(2)}) collective-permute-start(f32[200,768]{1,0:T(8,128)} %collective-permute-done.32.rest_4_), channel_id=1, source_target_pairs={{0,4},{4,0},{8,12},{12,8},{16,20},{20,16},{24,28},{28,24},{1,5},{5... | collective-permute-start | bytes 1843208 | tf_op jit(solution)/shard_map/ppermute | solution.py:484
  150.7 16.5 %collective-permute-start.41 = (f32[200,768]{1,0:T(8,128)}, f32[200,768]{1,0:T(8,128)S(1)}, u32[]{:S(2)}, u32[]{:S(2)}) collective-permute-start(f32[200,768]{1,0:T(8,128)} %collective-permute-done.33.rest_2_), channel_id=1, source_target_pairs={{0,16},{4,20},{8,24},{12,28},{16,0},{20,4},{24,8},{28,12},{1,17},{... | collective-permute-start | bytes 1843208 | tf_op jit(solution)/shard_map/ppermute | solution.py:484
  151.8 15.4 %collective-permute-start.42 = (f32[200,768]{1,0:T(8,128)}, f32[200,768]{1,0:T(8,128)S(1)}, u32[]{:S(2)}, u32[]{:S(2)}) collective-permute-start(f32[200,768]{1,0:T(8,128)} %collective-permute-done.33.rest_2_), channel_id=1, source_target_pairs={{0,4},{4,0},{8,12},{12,8},{16,20},{20,16},{24,28},{28,24},{1,5},{5... | collective-permute-start | bytes 1843208 | tf_op jit(solution)/shard_map/ppermute | solution.py:484
  152.0 3.6 collective-permute-start.43
  152.3 14.9 %collective-permute-start.39 = (f32[200,768]{1,0:T(8,128)}, f32[200,768]{1,0:T(8,128)S(1)}, u32[]{:S(2)}, u32[]{:S(2)}) collective-permute-start(f32[200,768]{1,0:T(8,128)} %copy-done.65), channel_id=1, source_target_pairs={{0,4},{4,0},{8,12},{12,8},{16,20},{20,16},{24,28},{28,24},{1,5},{5... | collective-permute-start | bytes 1843208 | tf_op jit(solution)/shard_map/ppermute | solution.py:484
  152.6 16.3 %collective-permute-start.40 = (f32[200,768]{1,0:T(8,128)}, f32[200,768]{1,0:T(8,128)S(1)}, u32[]{:S(2)}, u32[]{:S(2)}) collective-permute-start(f32[200,768]{1,0:T(8,128)} %copy-done.65), channel_id=1, source_target_pairs={{0,8},{4,12},{8,0},{12,4},{16,24},{20,28},{24,16},{28,20},{1,9},{5... | collective-permute-start | bytes 1843208 | tf_op jit(solution)/shard_map/ppermute | solution.py:484
  168.8 19.4 %collective-permute-start.45 = (f32[200,768]{1,0:T(8,128)S(1)}, f32[200,768]{1,0:T(8,128)}, u32[]{:S(2)}, u32[]{:S(2)}) collective-permute-start(f32[200,768]{1,0:T(8,128)S(1)} %collective-permute-done.41.rest_6_), channel_id=1, source_target_pairs={{0,4},{4,0},{8,12},{12,8},{16,20},{20,16},{24,28},{28,24},{1,5},{5... | collective-permute-start | bytes 1843208 | tf_op jit(solution)/shard_map/ppermute | solution.py:484
  169.3 18.9 %collective-permute-start.46 = (f32[200,768]{1,0:T(8,128)S(1)}, f32[200,768]{1,0:T(8,128)}, u32[]{:S(2)}, u32[]{:S(2)}) collective-permute-start(f32[200,768]{1,0:T(8,128)S(1)} %collective-permute-done.41.rest_6_), channel_id=1, source_target_pairs={{0,8},{4,12},{8,0},{12,4},{16,24},{20,28},{24,16},{28,20},{1,9},{5... | collective-permute-start | bytes 1843208 | tf_op jit(solution)/shard_map/ppermute | solution.py:484
  283.9 13.7 %collective-permute-start.48 = (f32[416,768]{1,0:T(8,128)S(1)}, f32[416,768]{1,0:T(8,128)S(1)}, u32[]{:S(2)}, u32[]{:S(2)}) collective-permute-start(f32[416,768]{1,0:T(8,128)S(1)} %constant_dynamic-slice_fusion.4), channel_id=1, source_target_pairs={{0,4},{4,0},{8,12},{12,8},{16,20},{20,16},{24,28},{28,24},{1,5},{5... | collective-permute-start | bytes 3833864 | tf_op jit(solution)/shard_map/ppermute | solution.py:484
  297.9 26.1 %collective-permute-start.49 = (f32[104,768]{1,0:T(8,128)S(1)}, f32[104,768]{1,0:T(8,128)S(1)}, u32[]{:S(2)}, u32[]{:S(2)}) collective-permute-start(f32[104,768]{1,0:T(8,128)S(1)} %get-tuple-element.320), channel_id=1, source_target_pairs={{0,8},{4,12},{8,0},{12,4},{16,24},{20,28},{24,16},{28,20},{1,9},{5... | collective-permute-start | bytes 958472 | tf_op jit(solution)/shard_map/ppermute | solution.py:484
  298.8 25.3 %collective-permute-start.50 = (f32[104,768]{1,0:T(8,128)S(1)}, f32[104,768]{1,0:T(8,128)S(1)}, u32[]{:S(2)}, u32[]{:S(2)}) collective-permute-start(f32[104,768]{1,0:T(8,128)S(1)} %get-tuple-element.319), channel_id=1, source_target_pairs={{0,16},{4,20},{8,24},{12,28},{16,0},{20,4},{24,8},{28,12},{1,17},{... | collective-permute-start | bytes 958472 | tf_op jit(solution)/shard_map/ppermute | solution.py:484
  298.8 27.3 %collective-permute-start.51 = (f32[104,768]{1,0:T(8,128)S(1)}, f32[104,768]{1,0:T(8,128)S(1)}, u32[]{:S(2)}, u32[]{:S(2)}) collective-permute-start(f32[104,768]{1,0:T(8,128)S(1)} %get-tuple-element.318), channel_id=1, source_target_pairs={{0,24},{4,28},{8,16},{12,20},{16,8},{20,12},{24,0},{28,4},{1,25},{... | collective-permute-start | bytes 958472 | tf_op jit(solution)/shard_map/ppermute | solution.py:484
  326.2 17.2 %collective-permute-start.52 = (f32[104,768]{1,0:T(8,128)S(1)}, f32[104,768]{1,0:T(8,128)S(1)}, u32[]{:S(2)}, u32[]{:S(2)}) collective-permute-start(f32[104,768]{1,0:T(8,128)S(1)} %add_add_fusion.rest_0_), channel_id=1, source_target_pairs={{0,8},{4,12},{8,0},{12,4},{16,24},{20,28},{24,16},{28,20},{1,9},{5... | collective-permute-start | bytes 958472 | tf_op jit(solution)/shard_map/ppermute | solution.py:484
  326.8 20.9 %collective-permute-start.53 = (f32[104,768]{1,0:T(8,128)S(1)}, f32[104,768]{1,0:T(8,128)S(1)}, u32[]{:S(2)}, u32[]{:S(2)}) collective-permute-start(f32[104,768]{1,0:T(8,128)S(1)} %add_add_fusion.rest_0_), channel_id=1, source_target_pairs={{0,16},{4,20},{8,24},{12,28},{16,0},{20,4},{24,8},{28,12},{1,17},{... | collective-permute-start | bytes 958472 | tf_op jit(solution)/shard_map/ppermute | solution.py:484
  330.2 17.5 %collective-permute-start.54 = (f32[104,768]{1,0:T(8,128)S(1)}, f32[104,768]{1,0:T(8,128)S(1)}, u32[]{:S(2)}, u32[]{:S(2)}) collective-permute-start(f32[104,768]{1,0:T(8,128)S(1)} %add_add_fusion.rest_0_), channel_id=1, source_target_pairs={{0,24},{4,28},{8,16},{12,20},{16,8},{20,12},{24,0},{28,4},{1,25},{... | collective-permute-start | bytes 958472 | tf_op jit(solution)/shard_map/ppermute | solution.py:484
  (87 other events, 983.5 us)
Sparse Core Ops, SparseCore 0:
  236.6 103.3 all-reduce.4

commit v4 on v3

--- a/solution.py
+++ b/solution.py
@@ -277,7 +277,7 @@
         normed_low = (hat * gain_ref[...] + shift_ref[...]).astype(LOW)
         n1_ref[...] = normed_low
     hidden = wi_ref.shape[0]
-    chunk = 256
+    chunk = 768
     total = None
     for c in range(0, hidden, chunk):
         cols = slice(c, c + chunk)
@@ -340,7 +340,7 @@
 
 
 def back_through(dm, slope, wi_ref, wd_ref, dn1, keep=None):
-    chunk = 256
+    chunk = 768
     for c in range(0, wi_ref.shape[0], chunk):
         cols = slice(c, c + chunk)
         dact = dot(dm, wd_ref[cols, :], NT)
@@ -351,12 +351,14 @@
     return dn1
 
 
-def middle_own(h1_ref, m_ref, cot_ref, g1_ref, b1_ref, db_ref, g2_ref, b2_ref, slope_ref, wi_ref, wd_ref, *outs):
-    layer_ref, dm_ref, du_ref, dn1_ref, sums_ref = outs
+def middle_own(h1_ref, m_ref, cot_ref, g1_ref, b1_ref, db_ref, g2_ref, b2_ref, slope_ref, wi_ref, wd_ref, act_ref, n1_ref, *outs):
+    layer_ref, dm_ref, dn1_ref, sums_ref, down_ref, inner_ref = outs
 
     @pl.when(pl.program_id(0) == 0)
     def _():
         sums_ref[...] = jnp.zeros_like(sums_ref)
+        down_ref[...] = jnp.zeros_like(down_ref)
+        inner_ref[...] = jnp.zeros_like(inner_ref)
 
     hat1, _ = stats(h1_ref[...])
     normed = hat1 * g1_ref[...] + b1_ref[...]
@@ -369,9 +371,10 @@
     sums_ref[2:3, :] += column_sum(dh2)
     dm = dh2.astype(LOW)
     dm_ref[...] = dm
+    down_ref[...] += inner_first(act_ref[...], dm)
 
     def keep(cols, du):
-        du_ref[:, cols] = du
+        inner_ref[:, cols] += inner_first(n1_ref[...], du)
         sums_ref[6:7, cols] += column_sum(du.astype(WIDE))
 
     dn1_ref[...] = back_through(dm, slope_ref, wi_ref, wd_ref, dh2, keep)
@@ -398,26 +401,28 @@
     da_ref[...] = dh1.astype(LOW)
 
 
-def call_middle_own(h1, mixed, cot, vectors, slope, wi, wd, block=512):
+def call_middle_own(h1, mixed, cot, vectors, slope, wi, wd, act, n1, block=512):
     count, model = h1.shape
     hidden = wi.shape[0]
     once = pl.BlockSpec((hidden, model), lambda i: (0, 0), pipeline_mode=pl.Buffered(1))
     return pl.pallas_call(
         middle_own,
         grid=(count // block,),
-        in_specs=[rows(block, model)] * 3 + [whole((1, model))] * 5 + [rows(block, hidden)] + [once] * 2,
-        out_specs=[rows(block, model), rows(block, model), rows(block, hidden), rows(block, model), whole((8, model))],
+        in_specs=[rows(block, model)] * 3 + [whole((1, model))] * 5 + [rows(block, hidden)] + [once] * 2
+        + [rows(block, hidden), rows(block, model)],
+        out_specs=[rows(block, model)] * 3 + [whole((8, model)), whole((hidden, model)), whole((model, hidden))],
         out_shape=[
             jax.ShapeDtypeStruct((count, model), LOW),
             jax.ShapeDtypeStruct((count, model), LOW),
-            jax.ShapeDtypeStruct((count, hidden), LOW),
             jax.ShapeDtypeStruct((count, model), WIDE),
             jax.ShapeDtypeStruct((8, model), WIDE),
+            jax.ShapeDtypeStruct((hidden, model), WIDE),
+            jax.ShapeDtypeStruct((model, hidden), WIDE),
         ],
-        input_output_aliases={1: 3},
+        input_output_aliases={1: 2},
         compiler_params=params(61 * 1024 * 1024),
         cost_estimate=cost(count),
-    )(h1, mixed, cot, *vectors, slope, wi, wd)
+    )(h1, mixed, cot, *vectors, slope, wi, wd, act, n1)
 
 
 def call_middle_rest(h1, dn1, dm, gain, sums, slopes, wis, wds, block=512):
@@ -638,7 +643,7 @@
     gate = [forward(1, gate), c.hop(0, 2, gate), c.hop(0, 4, gate), c.hop(0, 6, gate), c.hop(0, 1, gate), later]
     begun = [d.hop(0, 2, gate), d.hop(0, 4, gate)]
     gate = [c.hop(m, 1, gate) for m in (2, 4, 6)]
-    late = f.along(gate)
+    late = [f.along(gate), e.hop(0, 2, gate)]
     gate = [forward(2, gate), begun, d.hop(0, 1, gate)]
     slope, mixed, h1, n1, act = call_feed_forward(
         hidden,
@@ -658,24 +663,28 @@
         wds.append(wd)
         return slope, mixed
 
-    gate = [n1, d.hop(2, 4, gate), d.hop(2, 1, gate), d.hop(4, 1, gate), e.hop(0, 2, gate), late]
-    begun = [e.hop(0, 4, gate), f.hop(0, 2, gate), e.hop(0, 1, gate), e.hop(2, 1, gate)]
-    gate = [d.hop(6, 1, gate)]
+    gate = [n1, d.hop(2, 4, gate), d.hop(2, 1, gate), e.hop(0, 4, gate), late]
+    begun = [f.hop(0, 4, gate)]
+    late = e.hop(4, 2, gate)
+    gate = [d.hop(4, 1, gate), d.hop(6, 1, gate)]
+    begun += [e.hop(0, 1, gate), e.hop(2, 1, gate)]
+    queued = f.hop(0, 2, gate)
     slope, mixed = deep_forward(0, mixed, gate)
-    gate = [slope, begun]
-    begun = [f.hop(0, 4, gate), f.hop(0, 1, gate), f.hop(2, 1, gate)]
-    gate = [e.hop(4, 2, gate), e.hop(4, 1, gate), begun]
-    begun = [f.hop(4, 2, gate), f.hop(4, 1, gate)]
-    gate = [e.hop(6, 1, gate)]
+    gate = [slope, begun, late]
+    begun = [f.hop(4, 2, gate), f.hop(0, 1, gate), queued]
+    gate = [e.hop(4, 1, gate), e.hop(6, 1, gate)]
+    begun += [f.hop(4, 1, gate)]
     slope, mixed = deep_forward(1, mixed, gate)
     gate = [slope, begun]
-    gate = [f.hop(6, 1, gate)]
+    gate = [f.hop(2, 1, gate), f.hop(6, 1, gate)]
     slope, mixed = deep_forward(2, mixed, gate)
 
     vectors = (row(gain_one), row(shift_one), row(down_bias), row(gain_two), row(shift_two))
-    layer_out, dm, du, dn1, sums = call_middle_own(h1, mixed, cotangent, vectors, slopes[0], wis[0], wds[0])
-
-    own = after((inner_first(act, dm), inner_first(n1, du)), dm)
+    layer_out, dm, dn1, sums, *own = call_middle_own(
+        h1, mixed, cotangent, vectors, slopes[0], wis[0], wds[0], act, n1
+    )
+
+    own = after(tuple(own), dm)
     down_grad, inner_grad = lax.psum(own, "dp")
     dh1, da, sums = call_middle_rest(h1, after(dn1, own), dm, row(gain_one), sums, slopes[1:], wis[1:], wds[1:])
 

time: 371 us -> 359 us (0.968)
  matrix products: 14 us -> 2.91 us
  waiting for transfers between devices: 39 us -> 35.2 us
    dot_general x4 -> x2, matrix products: 14 us -> 2.91 us  [inner_first(): lax.dot_general(left, right, (((0,), (0,)), ((), ())), preferred_element_...]
    pallas_call x1, Pallas kernels: 18.2 us -> 23.3 us  [call_middle_own(): pl.pallas_call(middle_own, grid=(count // block,), in_specs=[rows(block,...]
    unnamed x155 -> x147, local copies, waits for them, and re-layouts: 32 us -> 31.4 us
  transfers between devices with their start and end apart: 60 -> 60, of which waited for: 21 -> 17; matrix products, arithmetic and copies ran while one was open for 3% -> 3% of each run, Pallas kernels for 49% -> 50%
where the time goes in v4:
time: 359 us; the launch traced here: 353 us
  Pallas kernels  214 us (60%)
  starting transfers between devices  46.1 us (13%)
  local copies, waits for them, and re-layouts  36.8 us (10%)
  waiting for transfers between devices  35.2 us (10%)
  between operations  15.5 us (4%)
    pallas_call x4, Pallas kernels, call_feed_forward(): pl.pallas_call(functools.partial(feed_forward, remote), grid=(count // bl...  63 us
    pallas_call x4, Pallas kernels, call_attend_backward(): pl.pallas_call(functools.partial(attend_backward, width, own), grid=(seqs...  45.3 us
    pallas_call x4, Pallas kernels, call_attend_forward(): pl.pallas_call(functools.partial(attend_forward, remote, width), grid=(se...  41.7 us
    ppermute x53, starting transfers between devices, swap(): return lax.ppermute(value, 'dp', [(i, i ^ mask) for i in range(size)])  34.1 us
    unnamed x147, local copies, waits for them, and re-layouts  31.4 us
    ppermute x53, waiting for transfers between devices, swap(): return lax.ppermute(value, 'dp', [(i, i ^ mask) for i in range(size)])  28.5 us
    pallas_call x1, Pallas kernels, call_middle_rest(): pl.pallas_call(functools.partial(middle_rest, groups), grid=(count // blo...  26 us
    pallas_call x1, Pallas kernels, call_middle_own(): pl.pallas_call(middle_own, grid=(count // block,), in_specs=[rows(block,...  23.3 us
  transfers between devices with their start and end apart: 60, of which 17 were waited for; matrix products, arithmetic and copies ran while one was open for 3% of the time, Pallas kernels for 50%

profile of v4, /device:TPU:0, one launch (start us, length us, event | category | flops | bytes accessed | tf_op | source)
XLA Modules:
  0.0 353.3 jit_solution(4729259725468007976)
XLA Ops:
  9.5 5.0 %collective-permute-start = (f32[104,768]{1,0:T(8,128)}, f32[104,768]{1,0:T(8,128)}, u32[]{:S(2)}, u32[]{:S(2)}) collective-permute-start(f32[104,768]{1,0:T(8,128)} %select_maximum_fusion.1), channel_id=1, source_target_pairs={{1,0},{2,1},{3,2},{0,3},{5,4},{6,5},{7,6},{4,7},{9,8},{10,9},{11,1... | collective-permute-start | bytes 958472 | tf_op jit(solution)/shard_map/ppermute | solution.py:493
  14.6 1.6 copy.43
  18.4 3.3 collective-permute-done.rest_1_
  21.7 1.5 collective-permute-start.3
  23.2 1.5 collective-permute-start.4
  25.6 4.4 %collective-permute-start.1 = (f32[104,768]{1,0:T(8,128)}, f32[104,768]{1,0:T(8,128)S(1)}, u32[]{:S(2)}, u32[]{:S(2)}) collective-permute-start(f32[104,768]{1,0:T(8,128)} %select_maximum_fusion.1), channel_id=1, source_target_pairs={{2,0},{3,1},{0,2},{1,3},{6,4},{7,5},{4,6},{5,7},{10,8},{11,9},{8,1... | collective-permute-start | bytes 958472 | tf_op jit(solution)/shard_map/ppermute | solution.py:493
  31.3 1.9 copy-done.7
  33.1 9.9 %shard_map.305 = (bf16[2048,576]{1,0:T(8,128)(2,1)S(1)}, bf16[2048,192]{1,0:T(8,128)(2,1)S(1)}, f32[4,8,512]{2,1,0:T(8,128)S(1)}) custom-call(bf16[2048,768]{1,0:T(8,128)(2,1)S(1)} %copy-done.7, s32[2048,1]{1,0:T(8,128)S(1)} %copy-done.1, s32[4,1,512]{2,1,0:T(1,128)S(1)} %bitcast.26, f32[1,576]{1,0:T(1,128)S(1)} %reshape.82.rest_0_, ...), custom_call_target="tpu_custom_call" | custom-call | flops 15360000000 | bytes 16777216 | tf_op jit(solution)/shard_map/pallas_call | solution.py:164
  43.1 1.5 copy-done.29
  46.3 2.9 collective-permute-done.1.rest_1_
  49.2 1.6 collective-permute-start.10
  50.8 1.5 collective-permute-start.11
  52.8 11.2 %shard_map.306 = (bf16[2048,576]{1,0:T(8,128)(2,1)S(1)}, bf16[2048,192]{1,0:T(8,128)(2,1)S(1)}, f32[4,8,512]{2,1,0:T(8,128)S(1)}, bf16[768,768]{1,0:T(8,128)(2,1)S(1)}) custom-call(bf16[2048,768]{1,0:T(8,128)(2,1)S(1)} %copy-done.7, s32[2048,1]{1,0:T(8,128)S(1)} %copy-done.1, s32[4,1,512]{2,1,0:T(1,128)S(1)} %bitcast.27, s32[1]{0:T(128)} %bitcast.2.rest_0_.rest_1_.place_ref, ...), custom_call_target="tpu_custom_call" | custom-call | flops 15360000000 | bytes 16777216 | tf_op jit(solution)/shard_map/pallas_call | solution.py:164
  64.0 1.5 copy-done.23
  67.5 2.1 collective-permute-start.22
  69.7 1.6 collective-permute-start.19
  71.2 1.5 collective-permute-start.20
  73.2 10.2 %shard_map.307 = (bf16[2048,576]{1,0:T(8,128)(2,1)S(1)}, bf16[2048,192]{1,0:T(8,128)(2,1)S(1)}, f32[4,8,512]{2,1,0:T(8,128)S(1)}, bf16[768,768]{1,0:T(8,128)(2,1)S(1)}) custom-call(bf16[2048,768]{1,0:T(8,128)(2,1)S(1)} %copy-done.7, s32[2048,1]{1,0:T(8,128)S(1)} %copy-done.1, s32[4,1,512]{2,1,0:T(1,128)S(1)} %bitcast.28, s32[1]{0:T(128)} %bitcast.2.rest_0_.rest_1_.place_ref, ...), custom_call_target="tpu_custom_call" | custom-call | flops 15360000000 | bytes 16777216 | tf_op jit(solution)/shard_map/pallas_call | solution.py:164
  83.5 1.5 copy-done.25
  86.1 1.6 collective-permute-done.20.rest_5_
  90.4 1.6 collective-permute-start.33
  92.0 10.3 %shard_map.308 = (bf16[2048,576]{1,0:T(8,128)(2,1)S(1)}, bf16[2048,192]{1,0:T(8,128)(2,1)S(1)}, f32[4,8,512]{2,1,0:T(8,128)S(1)}, bf16[768,768]{1,0:T(8,128)(2,1)S(1)}) custom-call(bf16[2048,768]{1,0:T(8,128)(2,1)S(1)} %copy-done.7, s32[2048,1]{1,0:T(8,128)S(1)} %copy-done.1, s32[4,1,512]{2,1,0:T(1,128)S(1)} %bitcast.29, s32[1]{0:T(128)} %bitcast.2.rest_0_.rest_1_.place_ref, ...), custom_call_target="tpu_custom_call" | custom-call | flops 15360000000 | bytes 16777216 | tf_op jit(solution)/shard_map/pallas_call | solution.py:164
  102.3 1.5 copy-done.27
  107.8 17.9 %shard_map.309 = (bf16[2048,768]{1,0:T(8,128)(2,1)S(1)}, f32[2048,768]{1,0:T(8,128)}, f32[2048,768]{1,0:T(8,128)}, bf16[2048,768]{1,0:T(8,128)(2,1)S(1)}, bf16[2048,768]{1,0:T(8,128)(2,1)S(1)}) custom-call(bf16[2048,768]{1,0:T(8,128)(2,1)S(1)} %copy-done.8, f32[1,768]{1,0:T(1,128)S(1)} %reshape.83.rest_0_, f32[1,768]{1,0:T(1,128)S(1)} %reshape.84.rest_1_, ...), custom_call_target="tpu_custom_call" | custom-call | flops 15360000000 | bytes 16777216 | tf_op jit(solution)/shard_map/pallas_call | solution.py:319
  125.8 1.6 copy-done.14
  127.4 1.8 copy-done.15
  129.1 1.6 copy-done.16
  130.8 4.4 %collective-permute-done.31.rest_6_ = f32[200,768]{1,0:T(8,128)} collective-permute-done((f32[200,768]{1,0:T(8,128)}, f32[200,768]{1,0:T(8,128)}, u32[]{:S(2)}, u32[]{:S(2)}) %collective-permute-start.31) | collective-permute-done | bytes 614432 | tf_op jit(solution)/shard_map/ppermute | solution.py:489
  136.6 1.5 collective-permute-start.38
  139.1 15.1 %shard_map.310 = (bf16[2048,768]{1,0:T(8,128)(2,1)}, f32[2048,768]{1,0:T(8,128)}, bf16[768,768]{1,0:T(8,128)(2,1)}, bf16[768,768]{1,0:T(8,128)(2,1)}) custom-call(bf16[2048,768]{1,0:T(8,128)(2,1)} %copy-done.15, f32[2048,768]{1,0:T(8,128)} %get-tuple-element.225.rest_0_, s32[1]{0:T(128)} %bitcast.2.rest_0_.rest_1_.place_ref, ...), custom_call_target="tpu_custom_call", output_to_operand_aliasing={{1}: (1, {})} | custom-call | flops 15360000000 | bytes 16777216 | tf_op jit(solution)/shard_map/pallas_call | solution.py:319
  158.5 15.0 %shard_map.311 = (bf16[2048,768]{1,0:T(8,128)(2,1)}, f32[2048,768]{1,0:T(8,128)}, bf16[768,768]{1,0:T(8,128)(2,1)}, bf16[768,768]{1,0:T(8,128)(2,1)}) custom-call(bf16[2048,768]{1,0:T(8,128)(2,1)} %copy-done.15, f32[2048,768]{1,0:T(8,128)} %get-tuple-element.240.rest_0_, s32[1]{0:T(128)} %bitcast.2.rest_0_.rest_1_.place_ref, ...), custom_call_target="tpu_custom_call", output_to_operand_aliasing={{1}: (1, {})} | custom-call | flops 15360000000 | bytes 16777216 | tf_op jit(solution)/shard_map/pallas_call | solution.py:319
  173.5 11.3 %collective-permute-done.44.rest_8_ = f32[200,768]{1,0:T(8,128)S(1)} collective-permute-done((f32[200,768]{1,0:T(8,128)S(1)}, f32[200,768]{1,0:T(8,128)S(1)}, u32[]{:S(2)}, u32[]{:S(2)}) %collective-permute-start.44) | collective-permute-done | bytes 614432 | tf_op jit(solution)/shard_map/ppermute | solution.py:489
  188.0 15.0 %shard_map.312 = (bf16[2048,768]{1,0:T(8,128)(2,1)}, f32[2048,768]{1,0:T(8,128)}, bf16[768,768]{1,0:T(8,128)(2,1)}, bf16[768,768]{1,0:T(8,128)(2,1)}) custom-call(bf16[2048,768]{1,0:T(8,128)(2,1)} %copy-done.15, f32[2048,768]{1,0:T(8,128)} %get-tuple-element.256.rest_0_, s32[1]{0:T(128)} %bitcast.2.rest_0_.rest_1_.place_ref, ...), custom_call_target="tpu_custom_call", output_to_operand_aliasing={{1}: (1, {})} | custom-call | flops 15360000000 | bytes 16777216 | tf_op jit(solution)/shard_map/pallas_call | solution.py:319
  202.9 23.3 %shard_map.313 = (bf16[2048,768]{1,0:T(8,128)(2,1)}, bf16[2048,768]{1,0:T(8,128)(2,1)}, f32[2048,768]{1,0:T(8,128)}, f32[8,768]{1,0:T(8,128)}, f32[768,768]{1,0:T(8,128)}, /*index=5*/f32[768,768]{1,0:T(8,128)}) custom-call(f32[2048,768]{1,0:T(8,128)} %get-tuple-element.223.h1_ref, ...), custom_call_target="tpu_custom_call", output_to_operand_aliasing={{2}: (1, {})} | custom-call | flops 15360000000 | bytes 16777216 | tf_op jit(solution)/shard_map/pallas_call | solution.py:408
  226.3 26.0 %shard_map.314 = (f32[2048,768]{1,0:T(8,128)}, bf16[2048,768]{1,0:T(8,128)(2,1)}, f32[8,768]{1,0:T(8,128)}) custom-call(f32[2048,768]{1,0:T(8,128)} %get-tuple-element.223.h1_ref, f32[2048,768]{1,0:T(8,128)} %get-tuple-element.282.dn1_ref, bf16[2048,768]{1,0:T(8,128)(2,1)} %get-tuple-element.279.dm_ref, ...), custom_call_target="tpu_custom_call", output_to_operand_aliasing={{0}: (1, {})} | custom-call | flops 15360000000 | bytes 16777216 | tf_op jit(solution)/shard_map/pallas_call | solution.py:433
  252.4 2.0 copy-done.10
  255.6 1.7 copy-done.30
  257.3 11.9 %shard_map.315 = (bf16[2048,576]{1,0:T(8,128)(2,1)S(1)}, f32[8,768]{1,0:T(8,128)S(1)}) custom-call(bf16[2048,576]{1,0:T(8,128)(2,1)S(1)} %copy-done.30, bf16[2048,192]{1,0:T(8,128)(2,1)S(1)} %copy-done.13, f32[4,8,512]{2,1,0:T(8,128)S(1)} %copy-done.44, s32[2048,1]{1,0:T(8,128)S(1)} %copy-done.2, s32[4,1,512]{2,1,0:T(1,128)S(1)} %bitcast.30, ...), custom_call_target="tpu_custom_call" | custom-call | flops 15360000000 | bytes 16777216 | tf_op jit(solution)/shard_map/pallas_call | solution.py:194
  269.2 2.1 convolution_dynamic-update-slice_fusion
  274.6 11.2 %shard_map.316.rest_1_ = bf16[2048,576]{1,0:T(8,128)(2,1)S(1)} custom-call(bf16[2048,576]{1,0:T(8,128)(2,1)S(1)} %copy-done.24, bf16[2048,192]{1,0:T(8,128)(2,1)S(1)} %copy-done.32, f32[4,8,512]{2,1,0:T(8,128)S(1)} %copy-done.38, s32[2048,1]{1,0:T(8,128)S(1)} %copy-done.2, s32[4,1,512]{2,1,0:T(1,128)S(1)} %bitcast.31, bf16[2048,768]{1,0:T(8,128)(2,1)S(1)} %copy-done.11, ...), custom_call_target="tpu_custom_call" | custom-call | flops 15360000000 | bytes 16777216 | tf_op jit(solution)/shard_map/pallas_call | solution.py:194
  287.5 2.2 collective-permute-start.51
  289.7 11.2 %shard_map.317.rest_2_ = bf16[2048,576]{1,0:T(8,128)(2,1)S(1)} custom-call(bf16[2048,576]{1,0:T(8,128)(2,1)S(1)} %copy-done.26, bf16[2048,192]{1,0:T(8,128)(2,1)S(1)} %copy-done.34, f32[4,8,512]{2,1,0:T(8,128)S(1)} %copy-done.40, s32[2048,1]{1,0:T(8,128)S(1)} %copy-done.2, s32[4,1,512]{2,1,0:T(1,128)S(1)} %bitcast.32, bf16[2048,768]{1,0:T(8,128)(2,1)S(1)} %copy-done.11, ...), custom_call_target="tpu_custom_call" | custom-call | flops 15360000000 | bytes 16777216 | tf_op jit(solution)/shard_map/pallas_call | solution.py:194
  301.0 11.1 %shard_map.318.rest_3_ = bf16[2048,576]{1,0:T(8,128)(2,1)S(1)} custom-call(bf16[2048,576]{1,0:T(8,128)(2,1)S(1)} %copy-done.28, bf16[2048,192]{1,0:T(8,128)(2,1)S(1)} %copy-done.36, f32[4,8,512]{2,1,0:T(8,128)S(1)} %copy-done.42, s32[2048,1]{1,0:T(8,128)S(1)} %copy-done.2, s32[4,1,512]{2,1,0:T(1,128)S(1)} %bitcast.33, bf16[2048,768]{1,0:T(8,128)(2,1)S(1)} %copy-done.11, ...), custom_call_target="tpu_custom_call" | custom-call | flops 15360000000 | bytes 16777216 | tf_op jit(solution)/shard_map/pallas_call | solution.py:194
  313.3 1.5 collective-permute-start.53
  316.2 13.4 %shard_map.319 = f32[2048,768]{1,0:T(8,128)} custom-call(f32[2048,768]{1,0:T(8,128)} %get-tuple-element.305.dh1_ref, bf16[2048,576]{1,0:T(8,128)(2,1)S(1)} %get-tuple-element.297.rest_0_, bf16[2048,576]{1,0:T(8,128)(2,1)S(1)} %shard_map.316.rest_1_, bf16[2048,576]{1,0:T(8,128)(2,1)S(1)} %shard_map.317.rest_2_, ...), custom_call_target="tpu_custom_call", output_to_operand_aliasing={{}: (0, {})} | custom-call | flops 15360000000 | bytes 16777216 | tf_op jit(solution)/shard_map/pallas_call | solution.py:218
  329.7 5.7 %collective-permute-done.53.rest_2_ = f32[104,768]{1,0:T(8,128)S(1)} collective-permute-done((f32[104,768]{1,0:T(8,128)S(1)}, f32[104,768]{1,0:T(8,128)S(1)}, u32[]{:S(2)}, u32[]{:S(2)}) %collective-permute-start.53) | collective-permute-done | bytes 319520 | tf_op jit(solution)/shard_map/ppermute | solution.py:489
  338.4 1.6 shard_map.320
  341.2 3.4 copy.65
  (263 shorter events, 43.2 us)
Async XLA Ops:
  7.2 334.0 %all-reduce.5.cloned.1.call-start = ((), (), s32[]{:S(2)}) async-start(), calls=%async_computation | async-start | bytes 9437184 | tf_op jit(solution)/shard_map/psum | solution.py:688
  9.5 12.2 %collective-permute-start = (f32[104,768]{1,0:T(8,128)}, f32[104,768]{1,0:T(8,128)}, u32[]{:S(2)}, u32[]{:S(2)}) collective-permute-start(f32[104,768]{1,0:T(8,128)} %select_maximum_fusion.1), channel_id=1, source_target_pairs={{1,0},{2,1},{3,2},{0,3},{5,4},{6,5},{7,6},{4,7},{9,8},{10,9},{11,1... | collective-permute-start | bytes 958472 | tf_op jit(solution)/shard_map/ppermute | solution.py:493
  21.7 23.5 %collective-permute-start.3 = (f32[104,768]{1,0:T(8,128)}, f32[104,768]{1,0:T(8,128)S(1)}, u32[]{:S(2)}, u32[]{:S(2)}) collective-permute-start(f32[104,768]{1,0:T(8,128)} %collective-permute-done.rest_1_), channel_id=1, source_target_pairs={{0,8},{4,12},{8,0},{12,4},{16,24},{20,28},{24,16},{28,20},{1,9},{5... | collective-permute-start | bytes 958472 | tf_op jit(solution)/shard_map/ppermute | solution.py:489
  23.2 22.0 %collective-permute-start.4 = (f32[104,768]{1,0:T(8,128)}, f32[104,768]{1,0:T(8,128)S(1)}, u32[]{:S(2)}, u32[]{:S(2)}) collective-permute-start(f32[104,768]{1,0:T(8,128)} %collective-permute-done.rest_1_), channel_id=1, source_target_pairs={{0,16},{4,20},{8,24},{12,28},{16,0},{20,4},{24,8},{28,12},{1,17},{... | collective-permute-start | bytes 958472 | tf_op jit(solution)/shard_map/ppermute | solution.py:489
  24.7 20.5 %collective-permute-start.5 = (f32[104,768]{1,0:T(8,128)}, f32[104,768]{1,0:T(8,128)S(1)}, u32[]{:S(2)}, u32[]{:S(2)}) collective-permute-start(f32[104,768]{1,0:T(8,128)} %collective-permute-done.rest_1_), channel_id=1, source_target_pairs={{0,24},{4,28},{8,16},{12,20},{16,8},{20,12},{24,0},{28,4},{1,25},{... | collective-permute-start | bytes 958472 | tf_op jit(solution)/shard_map/ppermute | solution.py:489
  25.2 20.0 %collective-permute-start.2 = (f32[104,768]{1,0:T(8,128)}, f32[104,768]{1,0:T(8,128)S(1)}, u32[]{:S(2)}, u32[]{:S(2)}) collective-permute-start(f32[104,768]{1,0:T(8,128)} %select_maximum_fusion.1), channel_id=1, source_target_pairs={{3,0},{0,1},{1,2},{2,3},{7,4},{4,5},{5,6},{6,7},{11,8},{8,9},{9,10... | collective-permute-start | bytes 958472 | tf_op jit(solution)/shard_map/ppermute | solution.py:493
  25.6 23.5 %collective-permute-start.1 = (f32[104,768]{1,0:T(8,128)}, f32[104,768]{1,0:T(8,128)S(1)}, u32[]{:S(2)}, u32[]{:S(2)}) collective-permute-start(f32[104,768]{1,0:T(8,128)} %select_maximum_fusion.1), channel_id=1, source_target_pairs={{2,0},{3,1},{0,2},{1,3},{6,4},{7,5},{4,6},{5,7},{10,8},{11,9},{8,1... | collective-permute-start | bytes 958472 | tf_op jit(solution)/shard_map/ppermute | solution.py:493
  45.2 4.0 %collective-permute-start.9 = (f32[104,768]{1,0:T(8,128)S(1)}, f32[104,768]{1,0:T(8,128)S(1)}, u32[]{:S(2)}, u32[]{:S(2)}) collective-permute-start(f32[104,768]{1,0:T(8,128)S(1)} %collective-permute-done.5.rest_7_), channel_id=1, source_target_pairs={{0,4},{4,0},{8,12},{12,8},{16,20},{20,16},{24,28},{28,24},{1,5},{5... | collective-permute-start | bytes 958472 | tf_op jit(solution)/shard_map/ppermute | solution.py:489
  45.3 3.9 %collective-permute-start.8 = (f32[104,768]{1,0:T(8,128)S(1)}, f32[104,768]{1,0:T(8,128)S(1)}, u32[]{:S(2)}, u32[]{:S(2)}) collective-permute-start(f32[104,768]{1,0:T(8,128)S(1)} %collective-permute-done.4.rest_5_), channel_id=1, source_target_pairs={{0,4},{4,0},{8,12},{12,8},{16,20},{20,16},{24,28},{28,24},{1,5},{5... | collective-permute-start | bytes 958472 | tf_op jit(solution)/shard_map/ppermute | solution.py:489
  45.8 3.4 collective-permute-start.7
  45.9 3.3 collective-permute-start.6
  49.2 16.9 %collective-permute-start.10 = (f32[104,768]{1,0:T(8,128)S(1)}, f32[104,768]{1,0:T(8,128)S(1)}, u32[]{:S(2)}, u32[]{:S(2)}) collective-permute-start(f32[104,768]{1,0:T(8,128)S(1)} %collective-permute-done.2.rest_1_), channel_id=1, source_target_pairs={{0,8},{4,12},{8,0},{12,4},{16,24},{20,28},{24,16},{28,20},{1,9},{5... | collective-permute-start | bytes 958472 | tf_op jit(solution)/shard_map/ppermute | solution.py:489
  50.8 16.0 %collective-permute-start.11 = (f32[104,768]{1,0:T(8,128)S(1)}, f32[104,768]{1,0:T(8,128)S(1)}, u32[]{:S(2)}, u32[]{:S(2)}) collective-permute-start(f32[104,768]{1,0:T(8,128)S(1)} %collective-permute-done.2.rest_1_), channel_id=1, source_target_pairs={{0,16},{4,20},{8,24},{12,28},{16,0},{20,4},{24,8},{28,12},{1,17},{... | collective-permute-start | bytes 958472 | tf_op jit(solution)/shard_map/ppermute | solution.py:489
  52.3 14.5 %collective-permute-start.12 = (f32[104,768]{1,0:T(8,128)S(1)}, f32[104,768]{1,0:T(8,128)S(1)}, u32[]{:S(2)}, u32[]{:S(2)}) collective-permute-start(f32[104,768]{1,0:T(8,128)S(1)} %collective-permute-done.2.rest_1_), channel_id=1, source_target_pairs={{0,24},{4,28},{8,16},{12,20},{16,8},{20,12},{24,0},{28,4},{1,25},{... | collective-permute-start | bytes 958472 | tf_op jit(solution)/shard_map/ppermute | solution.py:489
  52.8 14.0 %collective-permute-start.13 = (f32[104,768]{1,0:T(8,128)S(1)}, f32[104,768]{1,0:T(8,128)S(1)}, u32[]{:S(2)}, u32[]{:S(2)}) collective-permute-start(f32[104,768]{1,0:T(8,128)S(1)} %collective-permute-done.2.rest_1_), channel_id=1, source_target_pairs={{0,4},{4,0},{8,12},{12,8},{16,20},{20,16},{24,28},{28,24},{1,5},{5... | collective-permute-start | bytes 958472 | tf_op jit(solution)/shard_map/ppermute | solution.py:489
  52.8 16.8 %collective-permute-start.17 = (f32[200,768]{1,0:T(8,128)S(1)}, f32[200,768]{1,0:T(8,128)S(1)}, u32[]{:S(2)}, u32[]{:S(2)}) collective-permute-start(f32[200,768]{1,0:T(8,128)S(1)} %select_maximum_fusion), channel_id=1, source_target_pairs={{1,0},{2,1},{3,2},{0,3},{5,4},{6,5},{7,6},{4,7},{9,8},{10,9},{11,1... | collective-permute-start | bytes 1843208 | tf_op jit(solution)/shard_map/ppermute | solution.py:493
  67.5 18.6 %collective-permute-start.22 = (f32[200,768]{1,0:T(8,128)S(1)}, f32[200,768]{1,0:T(8,128)}, u32[]{:S(2)}, u32[]{:S(2)}) collective-permute-start(f32[200,768]{1,0:T(8,128)S(1)} %select_maximum_fusion), channel_id=1, source_target_pairs={{3,0},{0,1},{1,2},{2,3},{7,4},{4,5},{5,6},{6,7},{11,8},{8,9},{9,10... | collective-permute-start | bytes 1843208 | tf_op jit(solution)/shard_map/ppermute | solution.py:493
  69.6 16.5 %collective-permute-start.18 = (f32[104,768]{1,0:T(8,128)S(1)}, f32[104,768]{1,0:T(8,128)S(1)}, u32[]{:S(2)}, u32[]{:S(2)}) collective-permute-start(f32[104,768]{1,0:T(8,128)S(1)} %collective-permute-done.1.rest_1_), channel_id=1, source_target_pairs={{0,4},{4,0},{8,12},{12,8},{16,20},{20,16},{24,28},{28,24},{1,5},{5... | collective-permute-start | bytes 958472 | tf_op jit(solution)/shard_map/ppermute | solution.py:489
  69.7 16.4 %collective-permute-start.19 = (f32[104,768]{1,0:T(8,128)S(1)}, f32[104,768]{1,0:T(8,128)S(1)}, u32[]{:S(2)}, u32[]{:S(2)}) collective-permute-start(f32[104,768]{1,0:T(8,128)S(1)} %collective-permute-done.1.rest_1_), channel_id=1, source_target_pairs={{0,8},{4,12},{8,0},{12,4},{16,24},{20,28},{24,16},{28,20},{1,9},{5... | collective-permute-start | bytes 958472 | tf_op jit(solution)/shard_map/ppermute | solution.py:489
  71.2 16.5 %collective-permute-start.20 = (f32[104,768]{1,0:T(8,128)S(1)}, f32[104,768]{1,0:T(8,128)S(1)}, u32[]{:S(2)}, u32[]{:S(2)}) collective-permute-start(f32[104,768]{1,0:T(8,128)S(1)} %collective-permute-done.1.rest_1_), channel_id=1, source_target_pairs={{0,16},{4,20},{8,24},{12,28},{16,0},{20,4},{24,8},{28,12},{1,17},{... | collective-permute-start | bytes 958472 | tf_op jit(solution)/shard_map/ppermute | solution.py:489
  72.7 14.9 %collective-permute-start.21 = (f32[104,768]{1,0:T(8,128)S(1)}, f32[104,768]{1,0:T(8,128)S(1)}, u32[]{:S(2)}, u32[]{:S(2)}) collective-permute-start(f32[104,768]{1,0:T(8,128)S(1)} %collective-permute-done.1.rest_1_), channel_id=1, source_target_pairs={{0,24},{4,28},{8,16},{12,20},{16,8},{20,12},{24,0},{28,4},{1,25},{... | collective-permute-start | bytes 958472 | tf_op jit(solution)/shard_map/ppermute | solution.py:489
  88.3 16.7 %collective-permute-start.26 = (f32[200,768]{1,0:T(8,128)S(1)}, f32[200,768]{1,0:T(8,128)S(1)}, u32[]{:S(2)}, u32[]{:S(2)}) collective-permute-start(f32[200,768]{1,0:T(8,128)S(1)} %collective-permute-done.17.rest_2_), channel_id=1, source_target_pairs={{0,8},{4,12},{8,0},{12,4},{16,24},{20,28},{24,16},{28,20},{1,9},{5... | collective-permute-start | bytes 1843208 | tf_op jit(solution)/shard_map/ppermute | solution.py:489
  89.6 16.0 %collective-permute-start.27 = (f32[200,768]{1,0:T(8,128)S(1)}, f32[200,768]{1,0:T(8,128)S(1)}, u32[]{:S(2)}, u32[]{:S(2)}) collective-permute-start(f32[200,768]{1,0:T(8,128)S(1)} %collective-permute-done.17.rest_2_), channel_id=1, source_target_pairs={{0,16},{4,20},{8,24},{12,28},{16,0},{20,4},{24,8},{28,12},{1,17},{... | collective-permute-start | bytes 1843208 | tf_op jit(solution)/shard_map/ppermute | solution.py:489
  90.4 40.3 %collective-permute-start.33 = (f32[200,768]{1,0:T(8,128)}, f32[200,768]{1,0:T(8,128)}, u32[]{:S(2)}, u32[]{:S(2)}) collective-permute-start(f32[200,768]{1,0:T(8,128)} %collective-permute-done.22.rest_2_), channel_id=1, source_target_pairs={{0,8},{4,12},{8,0},{12,4},{16,24},{20,28},{24,16},{28,20},{1,9},{5... | collective-permute-start | bytes 1843208 | tf_op jit(solution)/shard_map/ppermute | solution.py:489
  92.0 38.8 %collective-permute-start.32 = (f32[200,768]{1,0:T(8,128)S(1)}, f32[200,768]{1,0:T(8,128)}, u32[]{:S(2)}, u32[]{:S(2)}) collective-permute-start(f32[200,768]{1,0:T(8,128)S(1)} %select_maximum_fusion), channel_id=1, source_target_pairs={{2,0},{3,1},{0,2},{1,3},{6,4},{7,5},{4,6},{5,7},{10,8},{11,9},{8,1... | collective-permute-start | bytes 1843208 | tf_op jit(solution)/shard_map/ppermute | solution.py:493
  92.0 13.6 %collective-permute-start.28 = (f32[200,768]{1,0:T(8,128)S(1)}, f32[200,768]{1,0:T(8,128)S(1)}, u32[]{:S(2)}, u32[]{:S(2)}) collective-permute-start(f32[200,768]{1,0:T(8,128)S(1)} %collective-permute-done.17.rest_2_), channel_id=1, source_target_pairs={{0,4},{4,0},{8,12},{12,8},{16,20},{20,16},{24,28},{28,24},{1,5},{5... | collective-permute-start | bytes 1843208 | tf_op jit(solution)/shard_map/ppermute | solution.py:489
  105.6 29.6 %collective-permute-start.29 = (f32[200,768]{1,0:T(8,128)S(1)}, f32[200,768]{1,0:T(8,128)S(1)}, u32[]{:S(2)}, u32[]{:S(2)}) collective-permute-start(f32[200,768]{1,0:T(8,128)S(1)} %collective-permute-done.26.rest_4_), channel_id=1, source_target_pairs={{0,4},{4,0},{8,12},{12,8},{16,20},{20,16},{24,28},{28,24},{1,5},{5... | collective-permute-start | bytes 1843208 | tf_op jit(solution)/shard_map/ppermute | solution.py:489
  105.6 29.6 %collective-permute-start.30 = (f32[200,768]{1,0:T(8,128)S(1)}, f32[200,768]{1,0:T(8,128)S(1)}, u32[]{:S(2)}, u32[]{:S(2)}) collective-permute-start(f32[200,768]{1,0:T(8,128)S(1)} %collective-permute-done.26.rest_4_), channel_id=1, source_target_pairs={{0,16},{4,20},{8,24},{12,28},{16,0},{20,4},{24,8},{28,12},{1,17},{... | collective-permute-start | bytes 1843208 | tf_op jit(solution)/shard_map/ppermute | solution.py:489
  106.7 28.5 %collective-permute-start.31 = (f32[200,768]{1,0:T(8,128)}, f32[200,768]{1,0:T(8,128)}, u32[]{:S(2)}, u32[]{:S(2)}) collective-permute-start(f32[200,768]{1,0:T(8,128)} %collective-permute-done.22.rest_2_), channel_id=1, source_target_pairs={{0,16},{4,20},{8,24},{12,28},{16,0},{20,4},{24,8},{28,12},{1,17},{... | collective-permute-start | bytes 1843208 | tf_op jit(solution)/shard_map/ppermute | solution.py:489
  135.2 2.9 collective-permute-start.35
  135.3 2.9 collective-permute-start.34
  135.8 18.5 %collective-permute-start.39 = (f32[200,768]{1,0:T(8,128)}, f32[200,768]{1,0:T(8,128)}, u32[]{:S(2)}, u32[]{:S(2)}) collective-permute-start(f32[200,768]{1,0:T(8,128)} %collective-permute-done.31.rest_6_), channel_id=1, source_target_pairs={{0,8},{4,12},{8,0},{12,4},{16,24},{20,28},{24,16},{28,20},{1,9},{5... | collective-permute-start | bytes 1843208 | tf_op jit(solution)/shard_map/ppermute | solution.py:489
  136.6 17.7 %collective-permute-start.38 = (f32[200,768]{1,0:T(8,128)}, f32[200,768]{1,0:T(8,128)S(1)}, u32[]{:S(2)}, u32[]{:S(2)}) collective-permute-start(f32[200,768]{1,0:T(8,128)} %collective-permute-done.32.rest_2_), channel_id=1, source_target_pairs={{0,16},{4,20},{8,24},{12,28},{16,0},{20,4},{24,8},{28,12},{1,17},{... | collective-permute-start | bytes 1843208 | tf_op jit(solution)/shard_map/ppermute | solution.py:489
  138.2 16.1 %collective-permute-start.37 = (f32[200,768]{1,0:T(8,128)}, f32[200,768]{1,0:T(8,128)S(1)}, u32[]{:S(2)}, u32[]{:S(2)}) collective-permute-start(f32[200,768]{1,0:T(8,128)} %collective-permute-done.33.rest_4_), channel_id=1, source_target_pairs={{0,4},{4,0},{8,12},{12,8},{16,20},{20,16},{24,28},{28,24},{1,5},{5... | collective-permute-start | bytes 1843208 | tf_op jit(solution)/shard_map/ppermute | solution.py:489
  138.3 16.0 %collective-permute-start.36 = (f32[200,768]{1,0:T(8,128)}, f32[200,768]{1,0:T(8,128)S(1)}, u32[]{:S(2)}, u32[]{:S(2)}) collective-permute-start(f32[200,768]{1,0:T(8,128)} %collective-permute-done.22.rest_2_), channel_id=1, source_target_pairs={{0,4},{4,0},{8,12},{12,8},{16,20},{20,16},{24,28},{28,24},{1,5},{5... | collective-permute-start | bytes 1843208 | tf_op jit(solution)/shard_map/ppermute | solution.py:489
  154.3 3.1 collective-permute-start.41
  155.4 18.1 %collective-permute-start.43 = (f32[200,768]{1,0:T(8,128)}, f32[200,768]{1,0:T(8,128)S(1)}, u32[]{:S(2)}, u32[]{:S(2)}) collective-permute-start(f32[200,768]{1,0:T(8,128)} %collective-permute-done.32.rest_2_), channel_id=1, source_target_pairs={{0,8},{4,12},{8,0},{12,4},{16,24},{20,28},{24,16},{28,20},{1,9},{5... | collective-permute-start | bytes 1843208 | tf_op jit(solution)/shard_map/ppermute | solution.py:489
  156.1 28.7 %collective-permute-start.44 = (f32[200,768]{1,0:T(8,128)S(1)}, f32[200,768]{1,0:T(8,128)S(1)}, u32[]{:S(2)}, u32[]{:S(2)}) collective-permute-start(f32[200,768]{1,0:T(8,128)S(1)} %collective-permute-done.38.rest_6_), channel_id=1, source_target_pairs={{0,8},{4,12},{8,0},{12,4},{16,24},{20,28},{24,16},{28,20},{1,9},{5... | collective-permute-start | bytes 1843208 | tf_op jit(solution)/shard_map/ppermute | solution.py:489
  157.4 27.4 %collective-permute-start.42 = (f32[200,768]{1,0:T(8,128)}, f32[200,768]{1,0:T(8,128)}, u32[]{:S(2)}, u32[]{:S(2)}) collective-permute-start(f32[200,768]{1,0:T(8,128)} %collective-permute-done.32.rest_2_), channel_id=1, source_target_pairs={{0,4},{4,0},{8,12},{12,8},{16,20},{20,16},{24,28},{28,24},{1,5},{5... | collective-permute-start | bytes 1843208 | tf_op jit(solution)/shard_map/ppermute | solution.py:489
  157.5 27.3 %collective-permute-start.45 = (f32[200,768]{1,0:T(8,128)S(1)}, f32[200,768]{1,0:T(8,128)}, u32[]{:S(2)}, u32[]{:S(2)}) collective-permute-start(f32[200,768]{1,0:T(8,128)S(1)} %collective-permute-done.38.rest_6_), channel_id=1, source_target_pairs={{0,4},{4,0},{8,12},{12,8},{16,20},{20,16},{24,28},{28,24},{1,5},{5... | collective-permute-start | bytes 1843208 | tf_op jit(solution)/shard_map/ppermute | solution.py:489
  184.9 3.0 collective-permute-start.46
  272.3 13.5 %collective-permute-start.48 = (f32[416,768]{1,0:T(8,128)S(1)}, f32[416,768]{1,0:T(8,128)S(1)}, u32[]{:S(2)}, u32[]{:S(2)}) collective-permute-start(f32[416,768]{1,0:T(8,128)S(1)} %constant_dynamic-slice_fusion.4), channel_id=1, source_target_pairs={{0,4},{4,0},{8,12},{12,8},{16,20},{20,16},{24,28},{28,24},{1,5},{5... | collective-permute-start | bytes 3833864 | tf_op jit(solution)/shard_map/ppermute | solution.py:489
  286.1 26.0 %collective-permute-start.49 = (f32[104,768]{1,0:T(8,128)S(1)}, f32[104,768]{1,0:T(8,128)S(1)}, u32[]{:S(2)}, u32[]{:S(2)}) collective-permute-start(f32[104,768]{1,0:T(8,128)S(1)} %get-tuple-element.330), channel_id=1, source_target_pairs={{0,8},{4,12},{8,0},{12,4},{16,24},{20,28},{24,16},{28,20},{1,9},{5... | collective-permute-start | bytes 958472 | tf_op jit(solution)/shard_map/ppermute | solution.py:489
  286.2 25.9 %collective-permute-start.50 = (f32[104,768]{1,0:T(8,128)S(1)}, f32[104,768]{1,0:T(8,128)S(1)}, u32[]{:S(2)}, u32[]{:S(2)}) collective-permute-start(f32[104,768]{1,0:T(8,128)S(1)} %get-tuple-element.329), channel_id=1, source_target_pairs={{0,16},{4,20},{8,24},{12,28},{16,0},{20,4},{24,8},{28,12},{1,17},{... | collective-permute-start | bytes 958472 | tf_op jit(solution)/shard_map/ppermute | solution.py:489
  287.5 24.6 %collective-permute-start.51 = (f32[104,768]{1,0:T(8,128)S(1)}, f32[104,768]{1,0:T(8,128)S(1)}, u32[]{:S(2)}, u32[]{:S(2)}) collective-permute-start(f32[104,768]{1,0:T(8,128)S(1)} %get-tuple-element.328), channel_id=1, source_target_pairs={{0,24},{4,28},{8,16},{12,20},{16,8},{20,12},{24,0},{28,4},{1,25},{... | collective-permute-start | bytes 958472 | tf_op jit(solution)/shard_map/ppermute | solution.py:489
  312.2 17.5 %collective-permute-start.52 = (f32[104,768]{1,0:T(8,128)S(1)}, f32[104,768]{1,0:T(8,128)S(1)}, u32[]{:S(2)}, u32[]{:S(2)}) collective-permute-start(f32[104,768]{1,0:T(8,128)S(1)} %add_add_fusion.rest_0_), channel_id=1, source_target_pairs={{0,8},{4,12},{8,0},{12,4},{16,24},{20,28},{24,16},{28,20},{1,9},{5... | collective-permute-start | bytes 958472 | tf_op jit(solution)/shard_map/ppermute | solution.py:489
  313.3 22.0 %collective-permute-start.53 = (f32[104,768]{1,0:T(8,128)S(1)}, f32[104,768]{1,0:T(8,128)S(1)}, u32[]{:S(2)}, u32[]{:S(2)}) collective-permute-start(f32[104,768]{1,0:T(8,128)S(1)} %add_add_fusion.rest_0_), channel_id=1, source_target_pairs={{0,16},{4,20},{8,24},{12,28},{16,0},{20,4},{24,8},{28,12},{1,17},{... | collective-permute-start | bytes 958472 | tf_op jit(solution)/shard_map/ppermute | solution.py:489
  314.9 20.5 %collective-permute-start.54 = (f32[104,768]{1,0:T(8,128)S(1)}, f32[104,768]{1,0:T(8,128)S(1)}, u32[]{:S(2)}, u32[]{:S(2)}) collective-permute-start(f32[104,768]{1,0:T(8,128)S(1)} %add_add_fusion.rest_0_), channel_id=1, source_target_pairs={{0,24},{4,28},{8,16},{12,20},{16,8},{20,12},{24,0},{28,4},{1,25},{... | collective-permute-start | bytes 958472 | tf_op jit(solution)/shard_map/ppermute | solution.py:489
  (83 other events, 892.1 us)
Sparse Core Ops, SparseCore 0:
  226.4 103.1 all-reduce.4

commit v5 on v4

--- a/solution.py
+++ b/solution.py
@@ -263,19 +263,9 @@
 
         normed_low = x_ref[...]
     else:
-        bias_ref, rest = rest[0], rest[1:]
+        bias_ref, wi_ref, wd_ref, slope_ref, out_ref, act_ref = rest
         bias = bias_ref[...]
-        (obias_ref, gain_ref, shift_ref, wi_ref, wd_ref) = rest[:5]
-        groups = (len(rest) - 10) // 2
-        contexts, outs, rest = rest[5 : 5 + groups], rest[5 + groups : 5 + 2 * groups], rest[5 + 2 * groups :]
-        slope_ref, out_ref, h1_ref, n1_ref, act_ref = rest
-        h1 = x_ref[...].astype(WIDE) + obias_ref[...]
-        for context, weight in zip(contexts, outs):
-            h1 = h1 + dot(context[...], weight[...], NN)
-        h1_ref[...] = h1
-        hat, _ = stats(h1)
-        normed_low = (hat * gain_ref[...] + shift_ref[...]).astype(LOW)
-        n1_ref[...] = normed_low
+        normed_low = x_ref[...]
     hidden = wi_ref.shape[0]
     chunk = 768
     total = None
@@ -292,7 +282,7 @@
     out_ref[...] = total if not remote else acc_ref[...] + total
 
 
-def call_feed_forward(hidden, x, remote, extra, contexts=(), packs=(), block=512):
+def call_feed_forward(hidden, x, remote, extra, block=512):
     count, model = x.shape
     in_specs = [rows(block, model)]
     out_specs = [rows(block, hidden), rows(block, model)]
@@ -306,16 +296,9 @@
         out_specs += [whole((hidden, model))] * 2
         out_shape += [jax.ShapeDtypeStruct((hidden, model), LOW)] * 2
     else:
-        width = contexts[0].shape[1]
-        in_specs += [whole((1, hidden))] + [whole((1, model))] * 3 + [whole((hidden, model))] * 2
-        in_specs += [rows(block, width)] * len(contexts)
-        in_specs += [pl.BlockSpec((width, model), lambda i: (3, 0))] * len(packs)
-        out_specs += [rows(block, model), rows(block, model), rows(block, hidden)]
-        out_shape += [
-            jax.ShapeDtypeStruct((count, model), WIDE),
-            jax.ShapeDtypeStruct((count, model), LOW),
-            jax.ShapeDtypeStruct((count, hidden), LOW),
-        ]
+        in_specs += [whole((1, hidden))] + [whole((hidden, model))] * 2
+        out_specs += [rows(block, hidden)]
+        out_shape += [jax.ShapeDtypeStruct((count, hidden), LOW)]
     return pl.pallas_call(
         functools.partial(feed_forward, remote),
         grid=(count // block,),
@@ -325,7 +308,41 @@
         input_output_aliases={1: 1} if remote else {},
         compiler_params=params((61 if remote else 26) * 1024 * 1024),
         cost_estimate=cost(count),
-    )(x, *extra, *contexts, *packs)
+    )(x, *extra)
+
+
+GAIN_ONE, SHIFT_ONE, DOWN_BIAS, GAIN_TWO, SHIFT_TWO, OUT_BIAS = range(6)
+
+
+def vector(vec_ref, at):
+    return vec_ref[at : at + 1, :]
+
+
+def first_norm(groups, x_ref, vec_ref, *rest):
+    contexts, outs, (h1_ref, n1_ref) = rest[:groups], rest[groups : 2 * groups], rest[2 * groups :]
+    h1 = x_ref[...].astype(WIDE) + vector(vec_ref, OUT_BIAS)
+    for context, weight in zip(contexts, outs):
+        h1 = h1 + dot(context[...], weight[...], NN)
+    h1_ref[...] = h1
+    hat, _ = stats(h1)
+    n1_ref[...] = (hat * vector(vec_ref, GAIN_ONE) + vector(vec_ref, SHIFT_ONE)).astype(LOW)
+
+
+def call_first_norm(tokens, vec, contexts, packs, block=512):
+    count, model = tokens.shape
+    groups = len(contexts)
+    width = contexts[0].shape[1]
+    return pl.pallas_call(
+        functools.partial(first_norm, groups),
+        grid=(count // block,),
+        in_specs=[rows(block, model), whole(vec.shape)]
+        + [rows(block, width)] * groups
+        + [pl.BlockSpec((width, model), lambda i: (3, 0))] * groups,
+        out_specs=[rows(block, model)] * 2,
+        out_shape=[jax.ShapeDtypeStruct((count, model), WIDE), jax.ShapeDtypeStruct((count, model), LOW)],
+        compiler_params=params(),
+        cost_estimate=cost(count),
+    )(tokens, vec, *contexts, *packs)
 
 
 def norm_back(grad, hat, scale, gain):
@@ -351,7 +368,7 @@
     return dn1
 
 
-def middle_own(h1_ref, m_ref, cot_ref, g1_ref, b1_ref, db_ref, g2_ref, b2_ref, slope_ref, wi_ref, wd_ref, act_ref, n1_ref, *outs):
+def middle_own(h1_ref, m_ref, cot_ref, vec_ref, slope_ref, wi_ref, wd_ref, act_ref, n1_ref, *outs):
     layer_ref, dm_ref, dn1_ref, sums_ref, down_ref, inner_ref = outs
 
     @pl.when(pl.program_id(0) == 0)
@@ -361,13 +378,13 @@
         inner_ref[...] = jnp.zeros_like(inner_ref)
 
     hat1, _ = stats(h1_ref[...])
-    normed = hat1 * g1_ref[...] + b1_ref[...]
-    hat2, scale2 = stats(normed + m_ref[...] + db_ref[...])
-    layer_ref[...] = (hat2 * g2_ref[...] + b2_ref[...]).astype(LOW)
+    normed = hat1 * vector(vec_ref, GAIN_ONE) + vector(vec_ref, SHIFT_ONE)
+    hat2, scale2 = stats(normed + m_ref[...] + vector(vec_ref, DOWN_BIAS))
+    layer_ref[...] = (hat2 * vector(vec_ref, GAIN_TWO) + vector(vec_ref, SHIFT_TWO)).astype(LOW)
     up = cot_ref[...].astype(WIDE)
     sums_ref[0:1, :] += column_sum(up * hat2)
     sums_ref[1:2, :] += column_sum(up)
-    dh2 = norm_back(up, hat2, scale2, g2_ref[...])
+    dh2 = norm_back(up, hat2, scale2, vector(vec_ref, GAIN_TWO))
     sums_ref[2:3, :] += column_sum(dh2)
     dm = dh2.astype(LOW)
     dm_ref[...] = dm
@@ -380,7 +397,7 @@
     dn1_ref[...] = back_through(dm, slope_ref, wi_ref, wd_ref, dh2, keep)
 
 
-def middle_rest(groups, h1_ref, dn1_ref, dm_ref, g1_ref, old_ref, *rest):
+def middle_rest(groups, h1_ref, dn1_ref, dm_ref, vec_ref, old_ref, *rest):
     slopes, wis, wds = rest[:groups], rest[groups : 2 * groups], rest[2 * groups : 3 * groups]
     dh1_ref, da_ref, sums_ref = rest[3 * groups :]
 
@@ -395,20 +412,20 @@
         dn1 = back_through(dm, slope_ref, wi_ref, wd_ref, dn1)
     sums_ref[3:4, :] += column_sum(dn1 * hat1)
     sums_ref[4:5, :] += column_sum(dn1)
-    dh1 = norm_back(dn1, hat1, scale1, g1_ref[...])
+    dh1 = norm_back(dn1, hat1, scale1, vector(vec_ref, GAIN_ONE))
     sums_ref[5:6, :] += column_sum(dh1)
     dh1_ref[...] = dh1
     da_ref[...] = dh1.astype(LOW)
 
 
-def call_middle_own(h1, mixed, cot, vectors, slope, wi, wd, act, n1, block=512):
+def call_middle_own(h1, mixed, cot, vec, slope, wi, wd, act, n1, block=512):
     count, model = h1.shape
     hidden = wi.shape[0]
     once = pl.BlockSpec((hidden, model), lambda i: (0, 0), pipeline_mode=pl.Buffered(1))
     return pl.pallas_call(
         middle_own,
         grid=(count // block,),
-        in_specs=[rows(block, model)] * 3 + [whole((1, model))] * 5 + [rows(block, hidden)] + [once] * 2
+        in_specs=[rows(block, model)] * 3 + [whole(vec.shape), rows(block, hidden)] + [once] * 2
         + [rows(block, hidden), rows(block, model)],
         out_specs=[rows(block, model)] * 3 + [whole((8, model)), whole((hidden, model)), whole((model, hidden))],
         out_shape=[
@@ -422,10 +439,10 @@
         input_output_aliases={1: 2},
         compiler_params=params(61 * 1024 * 1024),
         cost_estimate=cost(count),
-    )(h1, mixed, cot, *vectors, slope, wi, wd, act, n1)
-
-
-def call_middle_rest(h1, dn1, dm, gain, sums, slopes, wis, wds, block=512):
+    )(h1, mixed, cot, vec, slope, wi, wd, act, n1)
+
+
+def call_middle_rest(h1, dn1, dm, vec, sums, slopes, wis, wds, block=512):
     count, model = h1.shape
     groups = len(slopes)
     hidden = wis[0].shape[0]
@@ -434,7 +451,7 @@
         functools.partial(middle_rest, groups),
         grid=(count // block,),
         in_specs=[rows(block, model)] * 3
-        + [whole((1, model)), whole((8, model))]
+        + [whole(vec.shape), whole((8, model))]
         + [rows(block, hidden)] * groups
         + [once] * (2 * groups),
         out_specs=[rows(block, model), rows(block, model), whole((8, model))],
@@ -446,7 +463,7 @@
         input_output_aliases={1: 0},
         compiler_params=params(61 * 1024 * 1024),
         cost_estimate=cost(count),
-    )(h1, dn1, dm, gain, sums, *slopes, *wis, *wds)
+    )(h1, dn1, dm, vec, sums, *slopes, *wis, *wds)
 
 
 def inner_first(left, right):
@@ -608,6 +625,7 @@
         ],
         axis=0,
     )
+    vec = jnp.stack([gain_one, shift_one, down_bias, gain_two, shift_two, output_bias, output_bias, output_bias])
     scol = segments.reshape(count, 1)
     srow = segments.reshape(count // SEQ_LEN, 1, SEQ_LEN)
 
@@ -645,15 +663,9 @@
     gate = [c.hop(m, 1, gate) for m in (2, 4, 6)]
     late = [f.along(gate), e.hop(0, 2, gate)]
     gate = [forward(2, gate), begun, d.hop(0, 1, gate)]
-    slope, mixed, h1, n1, act = call_feed_forward(
-        hidden,
-        after(tokens, gate),
-        False,
-        (row(inner_bias), row(output_bias), row(gain_one), row(shift_one), inner_t, down_weight),
-        [saved[j][1] for j in range(groups)],
-        [saved[j][3] for j in range(groups)],
-    )
-    slopes, wis, wds = [slope], [inner_t], [down_weight]
+    contexts, packs = [saved[j][1] for j in range(groups)], [saved[j][3] for j in range(groups)]
+    h1, n1 = call_first_norm(after(tokens, gate), vec, contexts, packs)
+    slopes, wis, wds = [], [inner_t], [down_weight]
 
     def deep_forward(k, mixed, *done):
         slices = after(deep_of[k].slices(), *done)
@@ -663,30 +675,32 @@
         wds.append(wd)
         return slope, mixed
 
-    gate = [n1, d.hop(2, 4, gate), d.hop(2, 1, gate), e.hop(0, 4, gate), late]
-    begun = [f.hop(0, 4, gate)]
-    late = e.hop(4, 2, gate)
+    begun = [d.hop(2, 4, gate), d.hop(2, 1, gate), e.hop(0, 4, gate)]
+    gate = [n1, late]
+    begun += [f.hop(0, 2, gate), e.hop(0, 1, gate)]
+    slope, mixed, act = call_feed_forward(
+        hidden, after(n1, gate), False, (row(inner_bias), inner_t, down_weight)
+    )
+    slopes.append(slope)
+    gate = [slope, begun]
+    begun = [f.hop(0, 4, gate), e.hop(4, 2, gate), e.hop(2, 1, gate)]
     gate = [d.hop(4, 1, gate), d.hop(6, 1, gate)]
-    begun += [e.hop(0, 1, gate), e.hop(2, 1, gate)]
-    queued = f.hop(0, 2, gate)
     slope, mixed = deep_forward(0, mixed, gate)
-    gate = [slope, begun, late]
-    begun = [f.hop(4, 2, gate), f.hop(0, 1, gate), queued]
+    gate = [slope, begun]
+    begun = [f.hop(2, 4, gate), f.hop(0, 1, gate), f.hop(2, 1, gate)]
     gate = [e.hop(4, 1, gate), e.hop(6, 1, gate)]
-    begun += [f.hop(4, 1, gate)]
     slope, mixed = deep_forward(1, mixed, gate)
     gate = [slope, begun]
-    gate = [f.hop(2, 1, gate), f.hop(6, 1, gate)]
+    gate = [f.hop(4, 1, gate), f.hop(6, 1, gate)]
     slope, mixed = deep_forward(2, mixed, gate)
 
-    vectors = (row(gain_one), row(shift_one), row(down_bias), row(gain_two), row(shift_two))
     layer_out, dm, dn1, sums, *own = call_middle_own(
-        h1, mixed, cotangent, vectors, slopes[0], wis[0], wds[0], act, n1
+        h1, mixed, cotangent, vec, slopes[0], wis[0], wds[0], act, n1
     )
 
     own = after(tuple(own), dm)
     down_grad, inner_grad = lax.psum(own, "dp")
-    dh1, da, sums = call_middle_rest(h1, after(dn1, own), dm, row(gain_one), sums, slopes[1:], wis[1:], wds[1:])
+    dh1, da, sums = call_middle_rest(h1, after(dn1, own), dm, vec, sums, slopes[1:], wis[1:], wds[1:])
 
     def backward(j, *done):
         qkv, context, logs, pack = saved[j]

time: 359 us -> 353 us (0.983)
  waiting for transfers between devices: 35.2 us -> 23.2 us
  local copies, waits for them, and re-layouts: 36.8 us -> 41.4 us
    ppermute x53, waiting for transfers between devices: 28.5 us -> 14.6 us  [swap(): return lax.ppermute(value, 'dp', [(i, i ^ mask) for i in range(size)])]
    unnamed x147 -> x151, local copies, waits for them, and re-layouts: 31.4 us -> 38.4 us
    pallas_call x4, Pallas kernels: 63 us -> 56.3 us  [call_feed_forward(): pl.pallas_call(functools.partial(feed_forward, remote), grid=(count // bl...]
    pallas_call x0 -> x1, Pallas kernels: none -> 6 us  [call_first_norm(): pl.pallas_call(functools.partial(first_norm, groups), grid=(count // bloc...]
  transfers between devices with their start and end apart: 60 -> 60, of which waited for: 17 -> 16; matrix products, arithmetic and copies ran while one was open for 3% -> 2% of each run, Pallas kernels for 50% -> 51%
where the time goes in v5:
time: 353 us; the launch traced here: 348 us
  Pallas kernels  214 us (61%)
  starting transfers between devices  46.6 us (13%)
  local copies, waits for them, and re-layouts  41.4 us (12%)
  waiting for transfers between devices  23.2 us (7%)
  between operations  15.6 us (4%)
    pallas_call x4, Pallas kernels, call_feed_forward(): pl.pallas_call(functools.partial(feed_forward, remote), grid=(count // bl...  56.3 us
    pallas_call x4, Pallas kernels, call_attend_backward(): pl.pallas_call(functools.partial(attend_backward, width, own), grid=(seqs...  45.4 us
    pallas_call x4, Pallas kernels, call_attend_forward(): pl.pallas_call(functools.partial(attend_forward, remote, width), grid=(se...  42.3 us
    unnamed x151, local copies, waits for them, and re-layouts  38.4 us
    ppermute x53, starting transfers between devices, swap(): return lax.ppermute(value, 'dp', [(i, i ^ mask) for i in range(size)])  34.5 us
    pallas_call x1, Pallas kernels, call_middle_rest(): pl.pallas_call(functools.partial(middle_rest, groups), grid=(count // blo...  26 us
    pallas_call x1, Pallas kernels, call_middle_own(): pl.pallas_call(middle_own, grid=(count // block,), in_specs=[rows(block,...  23.5 us
    ppermute x53, waiting for transfers between devices, swap(): return lax.ppermute(value, 'dp', [(i, i ^ mask) for i in range(size)])  14.6 us
  transfers between devices with their start and end apart: 60, of which 16 were waited for; matrix products, arithmetic and copies ran while one was open for 2% of the time, Pallas kernels for 51%

profile of v5, /device:TPU:0, one launch (start us, length us, event | category | flops | bytes accessed | tf_op | source)
XLA Modules:
  0.0 347.6 jit_solution(4012349755012550525)
XLA Ops:
  9.5 5.0 %collective-permute-start = (f32[104,768]{1,0:T(8,128)}, f32[104,768]{1,0:T(8,128)S(1)}, u32[]{:S(2)}, u32[]{:S(2)}) collective-permute-start(f32[104,768]{1,0:T(8,128)} %select_maximum_fusion.1), channel_id=1, source_target_pairs={{1,0},{2,1},{3,2},{0,3},{5,4},{6,5},{7,6},{4,7},{9,8},{10,9},{11,1... | collective-permute-start | bytes 958472 | tf_op jit(solution)/shard_map/ppermute | solution.py:510
  14.6 1.6 copy.43
  18.6 3.1 collective-permute-done.rest_1_
  21.7 1.5 collective-permute-start.3
  23.2 1.5 collective-permute-start.4
  25.5 4.4 %collective-permute-start.1 = (f32[104,768]{1,0:T(8,128)}, f32[104,768]{1,0:T(8,128)S(1)}, u32[]{:S(2)}, u32[]{:S(2)}) collective-permute-start(f32[104,768]{1,0:T(8,128)} %select_maximum_fusion.1), channel_id=1, source_target_pairs={{2,0},{3,1},{0,2},{1,3},{6,4},{7,5},{4,6},{5,7},{10,8},{11,9},{8,1... | collective-permute-start | bytes 958472 | tf_op jit(solution)/shard_map/ppermute | solution.py:510
  31.2 1.9 copy-done.7
  33.0 9.9 %shard_map.305 = (bf16[2048,576]{1,0:T(8,128)(2,1)S(1)}, bf16[2048,192]{1,0:T(8,128)(2,1)S(1)}, f32[4,8,512]{2,1,0:T(8,128)S(1)}) custom-call(bf16[2048,768]{1,0:T(8,128)(2,1)S(1)} %copy-done.7, s32[2048,1]{1,0:T(8,128)S(1)} %copy-done.1, s32[4,1,512]{2,1,0:T(1,128)S(1)} %bitcast.26, f32[1,576]{1,0:T(1,128)S(1)} %reshape.61.rest_0_, ...), custom_call_target="tpu_custom_call" | custom-call | flops 15360000000 | bytes 16777216 | tf_op jit(solution)/shard_map/pallas_call | solution.py:164
  44.0 1.5 copy-done.34
  46.6 2.5 collective-permute-done.1.rest_1_
  49.1 1.6 collective-permute-start.10
  50.7 1.5 collective-permute-start.11
  52.7 10.2 %shard_map.306 = (bf16[2048,576]{1,0:T(8,128)(2,1)S(1)}, bf16[2048,192]{1,0:T(8,128)(2,1)S(1)}, f32[4,8,512]{2,1,0:T(8,128)S(1)}, bf16[768,768]{1,0:T(8,128)(2,1)S(1)}) custom-call(bf16[2048,768]{1,0:T(8,128)(2,1)S(1)} %copy-done.7, s32[2048,1]{1,0:T(8,128)S(1)} %copy-done.1, s32[4,1,512]{2,1,0:T(1,128)S(1)} %bitcast.27, s32[1]{0:T(128)} %bitcast.2.rest_0_.rest_1_.place_ref, ...), custom_call_target="tpu_custom_call" | custom-call | flops 15360000000 | bytes 16777216 | tf_op jit(solution)/shard_map/pallas_call | solution.py:164
  64.0 1.5 copy-done.28
  67.6 2.2 collective-permute-start.22
  70.0 1.6 collective-permute-start.19
  71.5 1.5 collective-permute-start.20
  73.5 10.2 %shard_map.307 = (bf16[2048,576]{1,0:T(8,128)(2,1)S(1)}, bf16[2048,192]{1,0:T(8,128)(2,1)S(1)}, f32[4,8,512]{2,1,0:T(8,128)S(1)}, bf16[768,768]{1,0:T(8,128)(2,1)S(1)}) custom-call(bf16[2048,768]{1,0:T(8,128)(2,1)S(1)} %copy-done.7, s32[2048,1]{1,0:T(8,128)S(1)} %copy-done.1, s32[4,1,512]{2,1,0:T(1,128)S(1)} %bitcast.28, s32[1]{0:T(128)} %bitcast.2.rest_0_.rest_1_.place_ref, ...), custom_call_target="tpu_custom_call" | custom-call | flops 15360000000 | bytes 16777216 | tf_op jit(solution)/shard_map/pallas_call | solution.py:164
  84.8 1.5 copy-done.30
  93.7 1.9 copy-done.8
  95.7 11.9 %shard_map.308 = (bf16[2048,576]{1,0:T(8,128)(2,1)S(1)}, bf16[2048,192]{1,0:T(8,128)(2,1)S(1)}, f32[4,8,512]{2,1,0:T(8,128)S(1)}, bf16[768,768]{1,0:T(8,128)(2,1)S(1)}) custom-call(bf16[2048,768]{1,0:T(8,128)(2,1)S(1)} %copy-done.8, s32[2048,1]{1,0:T(8,128)S(1)} %copy-done.2, s32[4,1,512]{2,1,0:T(1,128)S(1)} %bitcast.29, s32[1]{0:T(128)} %bitcast.2.rest_0_.rest_1_.place_ref, ...), custom_call_target="tpu_custom_call" | custom-call | flops 15360000000 | bytes 16777216 | tf_op jit(solution)/shard_map/pallas_call | solution.py:164
  107.6 1.5 copy-done.32
  110.7 6.0 %shard_map.309 = (f32[2048,768]{1,0:T(8,128)S(1)}, bf16[2048,768]{1,0:T(8,128)(2,1)S(1)}) custom-call(bf16[2048,768]{1,0:T(8,128)(2,1)S(1)} %copy-done.9, f32[8,768]{1,0:T(8,128)S(1)} %stack.29.vec_ref, bf16[2048,192]{1,0:T(8,128)(2,1)S(1)} %copy-done.14, bf16[2048,192]{1,0:T(8,128)(2,1)S(1)} %copy-done.37, ...), custom_call_target="tpu_custom_call" | custom-call | flops 15360000000 | bytes 16777216 | tf_op jit(solution)/shard_map/pallas_call | solution.py:335
  116.8 2.6 copy-done.16
  119.3 3.0 collective-permute-done.29.rest_2_
  124.5 11.2 %shard_map.310 = (bf16[2048,768]{1,0:T(8,128)(2,1)S(1)}, f32[2048,768]{1,0:T(8,128)}, bf16[2048,768]{1,0:T(8,128)(2,1)S(1)}) custom-call(bf16[2048,768]{1,0:T(8,128)(2,1)S(1)} %get-tuple-element.227.x_ref.n1_ref, f32[1,768]{1,0:T(1,128)S(1)} %reshape.62.rest_0_, bf16[768,768]{1,0:T(8,128)(2,1)S(1)} %bitcast.23, bf16[768,768]{1,0:T(8,128)(2,1)S(1)} %copy-done.5), custom_call_target="tpu_custom_call" | custom-call | flops 15360000000 | bytes 16777216 | tf_op jit(solution)/shard_map/pallas_call | solution.py:302
  135.7 1.7 copy-done.18
  137.5 1.6 copy-done.19
  144.2 15.1 %shard_map.311 = (bf16[2048,768]{1,0:T(8,128)(2,1)}, f32[2048,768]{1,0:T(8,128)}, bf16[768,768]{1,0:T(8,128)(2,1)}, bf16[768,768]{1,0:T(8,128)(2,1)}) custom-call(bf16[2048,768]{1,0:T(8,128)(2,1)} %copy-done.17, f32[2048,768]{1,0:T(8,128)} %get-tuple-element.228.rest_0_, s32[1]{0:T(128)} %bitcast.2.rest_0_.rest_1_.place_ref, ...), custom_call_target="tpu_custom_call", output_to_operand_aliasing={{1}: (1, {})} | custom-call | flops 15360000000 | bytes 16777216 | tf_op jit(solution)/shard_map/pallas_call | solution.py:302
  162.0 1.8 collective-permute-done.41.rest_7_
  163.7 14.9 %shard_map.312 = (bf16[2048,768]{1,0:T(8,128)(2,1)}, f32[2048,768]{1,0:T(8,128)}, bf16[768,768]{1,0:T(8,128)(2,1)}, bf16[768,768]{1,0:T(8,128)(2,1)}) custom-call(bf16[2048,768]{1,0:T(8,128)(2,1)} %copy-done.17, f32[2048,768]{1,0:T(8,128)} %get-tuple-element.244.rest_0_, s32[1]{0:T(128)} %bitcast.2.rest_0_.rest_1_.place_ref, ...), custom_call_target="tpu_custom_call", output_to_operand_aliasing={{1}: (1, {})} | custom-call | flops 15360000000 | bytes 16777216 | tf_op jit(solution)/shard_map/pallas_call | solution.py:302
  179.3 1.8 collective-permute-done.47.rest_9_
  181.8 15.0 %shard_map.313 = (bf16[2048,768]{1,0:T(8,128)(2,1)}, f32[2048,768]{1,0:T(8,128)}, bf16[768,768]{1,0:T(8,128)(2,1)}, bf16[768,768]{1,0:T(8,128)(2,1)}) custom-call(bf16[2048,768]{1,0:T(8,128)(2,1)} %copy-done.17, f32[2048,768]{1,0:T(8,128)} %get-tuple-element.259.rest_0_, s32[1]{0:T(128)} %bitcast.2.rest_0_.rest_1_.place_ref, ...), custom_call_target="tpu_custom_call", output_to_operand_aliasing={{1}: (1, {})} | custom-call | flops 15360000000 | bytes 16777216 | tf_op jit(solution)/shard_map/pallas_call | solution.py:302
  196.8 23.5 %shard_map.314 = (bf16[2048,768]{1,0:T(8,128)(2,1)}, bf16[2048,768]{1,0:T(8,128)(2,1)}, f32[2048,768]{1,0:T(8,128)}, f32[8,768]{1,0:T(8,128)}, f32[768,768]{1,0:T(8,128)}, /*index=5*/f32[768,768]{1,0:T(8,128)}) custom-call(f32[2048,768]{1,0:T(8,128)} %copy-done.16, f32[2048,768]{1,0:T(8,128)} %get-tuple-element.273.m_ref, ...), custom_call_target="tpu_custom_call", output_to_operand_aliasing={{2}: (1, {})} | custom-call | flops 15360000000 | bytes 16777216 | tf_op jit(solution)/shard_map/pallas_call | solution.py:425
  220.3 26.0 %shard_map.315 = (f32[2048,768]{1,0:T(8,128)}, bf16[2048,768]{1,0:T(8,128)(2,1)}, f32[8,768]{1,0:T(8,128)}) custom-call(f32[2048,768]{1,0:T(8,128)} %copy-done.16, f32[2048,768]{1,0:T(8,128)} %get-tuple-element.282.dn1_ref, bf16[2048,768]{1,0:T(8,128)(2,1)} %get-tuple-element.279.dm_ref, f32[8,768]{1,0:T(8,128)} %copy-done.4, ...), custom_call_target="tpu_custom_call", output_to_operand_aliasing={{0}: (1, {})} | custom-call | flops 15360000000 | bytes 16777216 | tf_op jit(solution)/shard_map/pallas_call | solution.py:450
  246.3 2.0 copy-done.11
  249.5 1.7 copy-done.35
  251.3 11.9 %shard_map.316 = (bf16[2048,576]{1,0:T(8,128)(2,1)S(1)}, f32[8,768]{1,0:T(8,128)S(1)}) custom-call(bf16[2048,576]{1,0:T(8,128)(2,1)S(1)} %copy-done.35, bf16[2048,192]{1,0:T(8,128)(2,1)S(1)} %copy-done.15, f32[4,8,512]{2,1,0:T(8,128)S(1)} %copy-done.45, s32[2048,1]{1,0:T(8,128)S(1)} %copy-done.3, s32[4,1,512]{2,1,0:T(1,128)S(1)} %bitcast.30, ...), custom_call_target="tpu_custom_call" | custom-call | flops 15360000000 | bytes 16777216 | tf_op jit(solution)/shard_map/pallas_call | solution.py:194
  263.2 2.1 convolution_dynamic-update-slice_fusion
  268.5 11.2 %shard_map.317.rest_1_ = bf16[2048,576]{1,0:T(8,128)(2,1)S(1)} custom-call(bf16[2048,576]{1,0:T(8,128)(2,1)S(1)} %copy-done.29, bf16[2048,192]{1,0:T(8,128)(2,1)S(1)} %copy-done.38, f32[4,8,512]{2,1,0:T(8,128)S(1)} %get-tuple-element.185.l_ref, s32[2048,1]{1,0:T(8,128)S(1)} %copy-done.3, s32[4,1,512]{2,1,0:T(1,128)S(1)} %bitcast.31, ...), custom_call_target="tpu_custom_call" | custom-call | flops 15360000000 | bytes 16777216 | tf_op jit(solution)/shard_map/pallas_call | solution.py:194
  281.3 2.3 collective-permute-start.51
  283.6 11.2 %shard_map.318.rest_2_ = bf16[2048,576]{1,0:T(8,128)(2,1)S(1)} custom-call(bf16[2048,576]{1,0:T(8,128)(2,1)S(1)} %copy-done.31, bf16[2048,192]{1,0:T(8,128)(2,1)S(1)} %copy-done.41, f32[4,8,512]{2,1,0:T(8,128)S(1)} %get-tuple-element.199.l_ref, s32[2048,1]{1,0:T(8,128)S(1)} %copy-done.3, s32[4,1,512]{2,1,0:T(1,128)S(1)} %bitcast.32, ...), custom_call_target="tpu_custom_call" | custom-call | flops 15360000000 | bytes 16777216 | tf_op jit(solution)/shard_map/pallas_call | solution.py:194
  294.8 11.2 %shard_map.319.rest_3_ = bf16[2048,576]{1,0:T(8,128)(2,1)S(1)} custom-call(bf16[2048,576]{1,0:T(8,128)(2,1)S(1)} %copy-done.33, bf16[2048,192]{1,0:T(8,128)(2,1)S(1)} %copy-done.43, f32[4,8,512]{2,1,0:T(8,128)S(1)} %get-tuple-element.212.l_ref, s32[2048,1]{1,0:T(8,128)S(1)} %copy-done.3, s32[4,1,512]{2,1,0:T(1,128)S(1)} %bitcast.33, ...), custom_call_target="tpu_custom_call" | custom-call | flops 15360000000 | bytes 16777216 | tf_op jit(solution)/shard_map/pallas_call | solution.py:194
  306.9 1.8 collective-permute-start.53
  310.1 13.5 %shard_map.320 = f32[2048,768]{1,0:T(8,128)} custom-call(f32[2048,768]{1,0:T(8,128)} %get-tuple-element.305.dh1_ref, bf16[2048,576]{1,0:T(8,128)(2,1)S(1)} %get-tuple-element.297.rest_0_, bf16[2048,576]{1,0:T(8,128)(2,1)S(1)} %shard_map.317.rest_1_, bf16[2048,576]{1,0:T(8,128)(2,1)S(1)} %shard_map.318.rest_2_, ...), custom_call_target="tpu_custom_call", output_to_operand_aliasing={{}: (0, {})} | custom-call | flops 15360000000 | bytes 16777216 | tf_op jit(solution)/shard_map/pallas_call | solution.py:218
  323.6 6.0 %collective-permute-done.53.rest_2_ = f32[104,768]{1,0:T(8,128)S(1)} collective-permute-done((f32[104,768]{1,0:T(8,128)S(1)}, f32[104,768]{1,0:T(8,128)S(1)}, u32[]{:S(2)}, u32[]{:S(2)}) %collective-permute-start.53) | collective-permute-done | bytes 319520 | tf_op jit(solution)/shard_map/ppermute | solution.py:506
  332.6 1.6 shard_map.321
  335.4 3.4 copy.65
  (269 shorter events, 48.1 us)
Async XLA Ops:
  7.2 328.2 %all-reduce.5.cloned.1.call-start = ((), (), s32[]{:S(2)}) async-start(), calls=%async_computation | async-start | bytes 9437184 | tf_op jit(solution)/shard_map/psum | solution.py:702
  9.5 12.2 %collective-permute-start = (f32[104,768]{1,0:T(8,128)}, f32[104,768]{1,0:T(8,128)S(1)}, u32[]{:S(2)}, u32[]{:S(2)}) collective-permute-start(f32[104,768]{1,0:T(8,128)} %select_maximum_fusion.1), channel_id=1, source_target_pairs={{1,0},{2,1},{3,2},{0,3},{5,4},{6,5},{7,6},{4,7},{9,8},{10,9},{11,1... | collective-permute-start | bytes 958472 | tf_op jit(solution)/shard_map/ppermute | solution.py:510
  21.7 23.8 %collective-permute-start.3 = (f32[104,768]{1,0:T(8,128)S(1)}, f32[104,768]{1,0:T(8,128)S(1)}, u32[]{:S(2)}, u32[]{:S(2)}) collective-permute-start(f32[104,768]{1,0:T(8,128)S(1)} %collective-permute-done.rest_1_), channel_id=1, source_target_pairs={{0,8},{4,12},{8,0},{12,4},{16,24},{20,28},{24,16},{28,20},{1,9},{5... | collective-permute-start | bytes 958472 | tf_op jit(solution)/shard_map/ppermute | solution.py:506
  23.2 22.3 %collective-permute-start.4 = (f32[104,768]{1,0:T(8,128)S(1)}, f32[104,768]{1,0:T(8,128)S(1)}, u32[]{:S(2)}, u32[]{:S(2)}) collective-permute-start(f32[104,768]{1,0:T(8,128)S(1)} %collective-permute-done.rest_1_), channel_id=1, source_target_pairs={{0,16},{4,20},{8,24},{12,28},{16,0},{20,4},{24,8},{28,12},{1,17},{... | collective-permute-start | bytes 958472 | tf_op jit(solution)/shard_map/ppermute | solution.py:506
  24.7 20.8 %collective-permute-start.5 = (f32[104,768]{1,0:T(8,128)S(1)}, f32[104,768]{1,0:T(8,128)S(1)}, u32[]{:S(2)}, u32[]{:S(2)}) collective-permute-start(f32[104,768]{1,0:T(8,128)S(1)} %collective-permute-done.rest_1_), channel_id=1, source_target_pairs={{0,24},{4,28},{8,16},{12,20},{16,8},{20,12},{24,0},{28,4},{1,25},{... | collective-permute-start | bytes 958472 | tf_op jit(solution)/shard_map/ppermute | solution.py:506
  25.2 20.3 %collective-permute-start.2 = (f32[104,768]{1,0:T(8,128)}, f32[104,768]{1,0:T(8,128)S(1)}, u32[]{:S(2)}, u32[]{:S(2)}) collective-permute-start(f32[104,768]{1,0:T(8,128)} %select_maximum_fusion.1), channel_id=1, source_target_pairs={{3,0},{0,1},{1,2},{2,3},{7,4},{4,5},{5,6},{6,7},{11,8},{8,9},{9,10... | collective-permute-start | bytes 958472 | tf_op jit(solution)/shard_map/ppermute | solution.py:510
  25.5 23.5 %collective-permute-start.1 = (f32[104,768]{1,0:T(8,128)}, f32[104,768]{1,0:T(8,128)S(1)}, u32[]{:S(2)}, u32[]{:S(2)}) collective-permute-start(f32[104,768]{1,0:T(8,128)} %select_maximum_fusion.1), channel_id=1, source_target_pairs={{2,0},{3,1},{0,2},{1,3},{6,4},{7,5},{4,6},{5,7},{10,8},{11,9},{8,1... | collective-permute-start | bytes 958472 | tf_op jit(solution)/shard_map/ppermute | solution.py:510
  45.5 3.6 %collective-permute-start.9 = (f32[104,768]{1,0:T(8,128)S(1)}, f32[104,768]{1,0:T(8,128)S(1)}, u32[]{:S(2)}, u32[]{:S(2)}) collective-permute-start(f32[104,768]{1,0:T(8,128)S(1)} %collective-permute-done.5.rest_7_), channel_id=1, source_target_pairs={{0,4},{4,0},{8,12},{12,8},{16,20},{20,16},{24,28},{28,24},{1,5},{5... | collective-permute-start | bytes 958472 | tf_op jit(solution)/shard_map/ppermute | solution.py:506
  45.6 3.5 %collective-permute-start.8 = (f32[104,768]{1,0:T(8,128)S(1)}, f32[104,768]{1,0:T(8,128)S(1)}, u32[]{:S(2)}, u32[]{:S(2)}) collective-permute-start(f32[104,768]{1,0:T(8,128)S(1)} %collective-permute-done.4.rest_5_), channel_id=1, source_target_pairs={{0,4},{4,0},{8,12},{12,8},{16,20},{20,16},{24,28},{28,24},{1,5},{5... | collective-permute-start | bytes 958472 | tf_op jit(solution)/shard_map/ppermute | solution.py:506
  46.1 3.0 collective-permute-start.7
  46.2 2.9 collective-permute-start.6
  49.1 17.3 %collective-permute-start.10 = (f32[104,768]{1,0:T(8,128)S(1)}, f32[104,768]{1,0:T(8,128)S(1)}, u32[]{:S(2)}, u32[]{:S(2)}) collective-permute-start(f32[104,768]{1,0:T(8,128)S(1)} %collective-permute-done.2.rest_1_), channel_id=1, source_target_pairs={{0,8},{4,12},{8,0},{12,4},{16,24},{20,28},{24,16},{28,20},{1,9},{5... | collective-permute-start | bytes 958472 | tf_op jit(solution)/shard_map/ppermute | solution.py:506
  50.7 16.0 %collective-permute-start.11 = (f32[104,768]{1,0:T(8,128)S(1)}, f32[104,768]{1,0:T(8,128)S(1)}, u32[]{:S(2)}, u32[]{:S(2)}) collective-permute-start(f32[104,768]{1,0:T(8,128)S(1)} %collective-permute-done.2.rest_1_), channel_id=1, source_target_pairs={{0,16},{4,20},{8,24},{12,28},{16,0},{20,4},{24,8},{28,12},{1,17},{... | collective-permute-start | bytes 958472 | tf_op jit(solution)/shard_map/ppermute | solution.py:506
  52.2 14.5 %collective-permute-start.12 = (f32[104,768]{1,0:T(8,128)S(1)}, f32[104,768]{1,0:T(8,128)S(1)}, u32[]{:S(2)}, u32[]{:S(2)}) collective-permute-start(f32[104,768]{1,0:T(8,128)S(1)} %collective-permute-done.2.rest_1_), channel_id=1, source_target_pairs={{0,24},{4,28},{8,16},{12,20},{16,8},{20,12},{24,0},{28,4},{1,25},{... | collective-permute-start | bytes 958472 | tf_op jit(solution)/shard_map/ppermute | solution.py:506
  52.7 14.0 %collective-permute-start.13 = (f32[104,768]{1,0:T(8,128)S(1)}, f32[104,768]{1,0:T(8,128)S(1)}, u32[]{:S(2)}, u32[]{:S(2)}) collective-permute-start(f32[104,768]{1,0:T(8,128)S(1)} %collective-permute-done.2.rest_1_), channel_id=1, source_target_pairs={{0,4},{4,0},{8,12},{12,8},{16,20},{20,16},{24,28},{28,24},{1,5},{5... | collective-permute-start | bytes 958472 | tf_op jit(solution)/shard_map/ppermute | solution.py:506
  52.7 17.2 %collective-permute-start.17 = (f32[200,768]{1,0:T(8,128)S(1)}, f32[200,768]{1,0:T(8,128)S(1)}, u32[]{:S(2)}, u32[]{:S(2)}) collective-permute-start(f32[200,768]{1,0:T(8,128)S(1)} %select_maximum_fusion), channel_id=1, source_target_pairs={{1,0},{2,1},{3,2},{0,3},{5,4},{6,5},{7,6},{4,7},{9,8},{10,9},{11,1... | collective-permute-start | bytes 1843208 | tf_op jit(solution)/shard_map/ppermute | solution.py:510
  66.8 3.1 collective-permute-start.16
  67.6 19.7 %collective-permute-start.22 = (f32[200,768]{1,0:T(8,128)S(1)}, f32[200,768]{1,0:T(8,128)S(1)}, u32[]{:S(2)}, u32[]{:S(2)}) collective-permute-start(f32[200,768]{1,0:T(8,128)S(1)} %select_maximum_fusion), channel_id=1, source_target_pairs={{3,0},{0,1},{1,2},{2,3},{7,4},{4,5},{5,6},{6,7},{11,8},{8,9},{9,10... | collective-permute-start | bytes 1843208 | tf_op jit(solution)/shard_map/ppermute | solution.py:510
  69.9 17.4 %collective-permute-start.18 = (f32[104,768]{1,0:T(8,128)S(1)}, f32[104,768]{1,0:T(8,128)S(1)}, u32[]{:S(2)}, u32[]{:S(2)}) collective-permute-start(f32[104,768]{1,0:T(8,128)S(1)} %collective-permute-done.1.rest_1_), channel_id=1, source_target_pairs={{0,4},{4,0},{8,12},{12,8},{16,20},{20,16},{24,28},{28,24},{1,5},{5... | collective-permute-start | bytes 958472 | tf_op jit(solution)/shard_map/ppermute | solution.py:506
  70.0 17.3 %collective-permute-start.19 = (f32[104,768]{1,0:T(8,128)S(1)}, f32[104,768]{1,0:T(8,128)}, u32[]{:S(2)}, u32[]{:S(2)}) collective-permute-start(f32[104,768]{1,0:T(8,128)S(1)} %collective-permute-done.1.rest_1_), channel_id=1, source_target_pairs={{0,8},{4,12},{8,0},{12,4},{16,24},{20,28},{24,16},{28,20},{1,9},{5... | collective-permute-start | bytes 958472 | tf_op jit(solution)/shard_map/ppermute | solution.py:506
  71.5 16.6 %collective-permute-start.20 = (f32[104,768]{1,0:T(8,128)S(1)}, f32[104,768]{1,0:T(8,128)}, u32[]{:S(2)}, u32[]{:S(2)}) collective-permute-start(f32[104,768]{1,0:T(8,128)S(1)} %collective-permute-done.1.rest_1_), channel_id=1, source_target_pairs={{0,16},{4,20},{8,24},{12,28},{16,0},{20,4},{24,8},{28,12},{1,17},{... | collective-permute-start | bytes 958472 | tf_op jit(solution)/shard_map/ppermute | solution.py:506
  73.1 15.0 %collective-permute-start.21 = (f32[104,768]{1,0:T(8,128)S(1)}, f32[104,768]{1,0:T(8,128)}, u32[]{:S(2)}, u32[]{:S(2)}) collective-permute-start(f32[104,768]{1,0:T(8,128)S(1)} %collective-permute-done.1.rest_1_), channel_id=1, source_target_pairs={{0,24},{4,28},{8,16},{12,20},{16,8},{20,12},{24,0},{28,4},{1,25},{... | collective-permute-start | bytes 958472 | tf_op jit(solution)/shard_map/ppermute | solution.py:506
  88.1 3.2 collective-permute-start.25
  88.1 3.2 collective-permute-start.24
  88.8 20.2 %collective-permute-start.26 = (f32[200,768]{1,0:T(8,128)}, f32[200,768]{1,0:T(8,128)S(1)}, u32[]{:S(2)}, u32[]{:S(2)}) collective-permute-start(f32[200,768]{1,0:T(8,128)} %copy-done.62), channel_id=1, source_target_pairs={{0,8},{4,12},{8,0},{12,4},{16,24},{20,28},{24,16},{28,20},{1,9},{5... | collective-permute-start | bytes 1843208 | tf_op jit(solution)/shard_map/ppermute | solution.py:506
  90.1 19.0 %collective-permute-start.27 = (f32[200,768]{1,0:T(8,128)}, f32[200,768]{1,0:T(8,128)S(1)}, u32[]{:S(2)}, u32[]{:S(2)}) collective-permute-start(f32[200,768]{1,0:T(8,128)} %copy-done.62), channel_id=1, source_target_pairs={{0,16},{4,20},{8,24},{12,28},{16,0},{20,4},{24,8},{28,12},{1,17},{... | collective-permute-start | bytes 1843208 | tf_op jit(solution)/shard_map/ppermute | solution.py:506
  91.3 28.0 %collective-permute-start.30 = (f32[200,768]{1,0:T(8,128)}, f32[200,768]{1,0:T(8,128)}, u32[]{:S(2)}, u32[]{:S(2)}) collective-permute-start(f32[200,768]{1,0:T(8,128)} %copy-done.58), channel_id=1, source_target_pairs={{0,8},{4,12},{8,0},{12,4},{16,24},{20,28},{24,16},{28,20},{1,9},{5... | collective-permute-start | bytes 1843208 | tf_op jit(solution)/shard_map/ppermute | solution.py:506
  92.5 29.8 %collective-permute-start.29 = (f32[200,768]{1,0:T(8,128)}, f32[200,768]{1,0:T(8,128)}, u32[]{:S(2)}, u32[]{:S(2)}) collective-permute-start(f32[200,768]{1,0:T(8,128)} %copy-done.47), channel_id=1, source_target_pairs={{2,0},{3,1},{0,2},{1,3},{6,4},{7,5},{4,6},{5,7},{10,8},{11,9},{8,1... | collective-permute-start | bytes 1843208 | tf_op jit(solution)/shard_map/ppermute | solution.py:510
  92.5 16.6 %collective-permute-start.28 = (f32[200,768]{1,0:T(8,128)}, f32[200,768]{1,0:T(8,128)S(1)}, u32[]{:S(2)}, u32[]{:S(2)}) collective-permute-start(f32[200,768]{1,0:T(8,128)} %copy-done.62), channel_id=1, source_target_pairs={{0,4},{4,0},{8,12},{12,8},{16,20},{20,16},{24,28},{28,24},{1,5},{5... | collective-permute-start | bytes 1843208 | tf_op jit(solution)/shard_map/ppermute | solution.py:506
  109.1 30.9 %collective-permute-start.31 = (f32[200,768]{1,0:T(8,128)S(1)}, f32[200,768]{1,0:T(8,128)S(1)}, u32[]{:S(2)}, u32[]{:S(2)}) collective-permute-start(f32[200,768]{1,0:T(8,128)S(1)} %collective-permute-done.26.rest_4_), channel_id=1, source_target_pairs={{0,4},{4,0},{8,12},{12,8},{16,20},{20,16},{24,28},{28,24},{1,5},{5... | collective-permute-start | bytes 1843208 | tf_op jit(solution)/shard_map/ppermute | solution.py:506
  109.7 30.3 %collective-permute-start.32 = (f32[200,768]{1,0:T(8,128)S(1)}, f32[200,768]{1,0:T(8,128)S(1)}, u32[]{:S(2)}, u32[]{:S(2)}) collective-permute-start(f32[200,768]{1,0:T(8,128)S(1)} %collective-permute-done.26.rest_4_), channel_id=1, source_target_pairs={{0,16},{4,20},{8,24},{12,28},{16,0},{20,4},{24,8},{28,12},{1,17},{... | collective-permute-start | bytes 1843208 | tf_op jit(solution)/shard_map/ppermute | solution.py:506
  122.3 16.8 %collective-permute-start.35 = (f32[200,768]{1,0:T(8,128)S(1)}, f32[200,768]{1,0:T(8,128)S(1)}, u32[]{:S(2)}, u32[]{:S(2)}) collective-permute-start(f32[200,768]{1,0:T(8,128)S(1)} %copy-done.59), channel_id=1, source_target_pairs={{0,4},{4,0},{8,12},{12,8},{16,20},{20,16},{24,28},{28,24},{1,5},{5... | collective-permute-start | bytes 1843208 | tf_op jit(solution)/shard_map/ppermute | solution.py:506
  122.3 16.8 %collective-permute-start.34 = (f32[200,768]{1,0:T(8,128)}, f32[200,768]{1,0:T(8,128)S(1)}, u32[]{:S(2)}, u32[]{:S(2)}) collective-permute-start(f32[200,768]{1,0:T(8,128)} %collective-permute-done.29.rest_2_), channel_id=1, source_target_pairs={{0,8},{4,12},{8,0},{12,4},{16,24},{20,28},{24,16},{28,20},{1,9},{5... | collective-permute-start | bytes 1843208 | tf_op jit(solution)/shard_map/ppermute | solution.py:506
  123.1 16.1 %collective-permute-start.33 = (f32[200,768]{1,0:T(8,128)S(1)}, f32[200,768]{1,0:T(8,128)}, u32[]{:S(2)}, u32[]{:S(2)}) collective-permute-start(f32[200,768]{1,0:T(8,128)S(1)} %copy-done.59), channel_id=1, source_target_pairs={{0,16},{4,20},{8,24},{12,28},{16,0},{20,4},{24,8},{28,12},{1,17},{... | collective-permute-start | bytes 1843208 | tf_op jit(solution)/shard_map/ppermute | solution.py:506
  140.6 18.7 %collective-permute-start.40 = (f32[200,768]{1,0:T(8,128)}, f32[200,768]{1,0:T(8,128)}, u32[]{:S(2)}, u32[]{:S(2)}) collective-permute-start(f32[200,768]{1,0:T(8,128)} %collective-permute-done.33.rest_6_), channel_id=1, source_target_pairs={{0,8},{4,12},{8,0},{12,4},{16,24},{20,28},{24,16},{28,20},{1,9},{5... | collective-permute-start | bytes 1843208 | tf_op jit(solution)/shard_map/ppermute | solution.py:506
  141.4 18.0 %collective-permute-start.39 = (f32[200,768]{1,0:T(8,128)}, f32[200,768]{1,0:T(8,128)S(1)}, u32[]{:S(2)}, u32[]{:S(2)}) collective-permute-start(f32[200,768]{1,0:T(8,128)} %collective-permute-done.29.rest_2_), channel_id=1, source_target_pairs={{0,16},{4,20},{8,24},{12,28},{16,0},{20,4},{24,8},{28,12},{1,17},{... | collective-permute-start | bytes 1843208 | tf_op jit(solution)/shard_map/ppermute | solution.py:506
  142.5 16.9 %collective-permute-start.38 = (f32[200,768]{1,0:T(8,128)}, f32[200,768]{1,0:T(8,128)}, u32[]{:S(2)}, u32[]{:S(2)}) collective-permute-start(f32[200,768]{1,0:T(8,128)} %collective-permute-done.30.rest_4_), channel_id=1, source_target_pairs={{0,4},{4,0},{8,12},{12,8},{16,20},{20,16},{24,28},{28,24},{1,5},{5... | collective-permute-start | bytes 1843208 | tf_op jit(solution)/shard_map/ppermute | solution.py:506
  159.9 3.8 %collective-permute-start.41 = (f32[200,768]{1,0:T(8,128)}, f32[200,768]{1,0:T(8,128)}, u32[]{:S(2)}, u32[]{:S(2)}) collective-permute-start(f32[200,768]{1,0:T(8,128)} %collective-permute-done.33.rest_6_), channel_id=1, source_target_pairs={{0,4},{4,0},{8,12},{12,8},{16,20},{20,16},{24,28},{28,24},{1,5},{5... | collective-permute-start | bytes 1843208 | tf_op jit(solution)/shard_map/ppermute | solution.py:506
  160.0 18.6 %collective-permute-start.44 = (f32[200,768]{1,0:T(8,128)S(1)}, f32[200,768]{1,0:T(8,128)}, u32[]{:S(2)}, u32[]{:S(2)}) collective-permute-start(f32[200,768]{1,0:T(8,128)S(1)} %copy-done.61), channel_id=1, source_target_pairs={{0,4},{4,0},{8,12},{12,8},{16,20},{20,16},{24,28},{28,24},{1,5},{5... | collective-permute-start | bytes 1843208 | tf_op jit(solution)/shard_map/ppermute | solution.py:506
  160.5 18.2 %collective-permute-start.45 = (f32[200,768]{1,0:T(8,128)S(1)}, f32[200,768]{1,0:T(8,128)}, u32[]{:S(2)}, u32[]{:S(2)}) collective-permute-start(f32[200,768]{1,0:T(8,128)S(1)} %copy-done.61), channel_id=1, source_target_pairs={{0,16},{4,20},{8,24},{12,28},{16,0},{20,4},{24,8},{28,12},{1,17},{... | collective-permute-start | bytes 1843208 | tf_op jit(solution)/shard_map/ppermute | solution.py:506
  161.4 17.3 %collective-permute-start.43 = (f32[200,768]{1,0:T(8,128)}, f32[200,768]{1,0:T(8,128)}, u32[]{:S(2)}, u32[]{:S(2)}) collective-permute-start(f32[200,768]{1,0:T(8,128)} %collective-permute-done.29.rest_2_), channel_id=1, source_target_pairs={{0,4},{4,0},{8,12},{12,8},{16,20},{20,16},{24,28},{28,24},{1,5},{5... | collective-permute-start | bytes 1843208 | tf_op jit(solution)/shard_map/ppermute | solution.py:506
  266.3 13.4 %collective-permute-start.48 = (f32[416,768]{1,0:T(8,128)S(1)}, f32[416,768]{1,0:T(8,128)S(1)}, u32[]{:S(2)}, u32[]{:S(2)}) collective-permute-start(f32[416,768]{1,0:T(8,128)S(1)} %constant_dynamic-slice_fusion.4), channel_id=1, source_target_pairs={{0,4},{4,0},{8,12},{12,8},{16,20},{20,16},{24,28},{28,24},{1,5},{5... | collective-permute-start | bytes 3833864 | tf_op jit(solution)/shard_map/ppermute | solution.py:506
  280.0 26.0 %collective-permute-start.49 = (f32[104,768]{1,0:T(8,128)S(1)}, f32[104,768]{1,0:T(8,128)S(1)}, u32[]{:S(2)}, u32[]{:S(2)}) collective-permute-start(f32[104,768]{1,0:T(8,128)S(1)} %get-tuple-element.330), channel_id=1, source_target_pairs={{0,8},{4,12},{8,0},{12,4},{16,24},{20,28},{24,16},{28,20},{1,9},{5... | collective-permute-start | bytes 958472 | tf_op jit(solution)/shard_map/ppermute | solution.py:506
  280.1 25.9 %collective-permute-start.50 = (f32[104,768]{1,0:T(8,128)S(1)}, f32[104,768]{1,0:T(8,128)S(1)}, u32[]{:S(2)}, u32[]{:S(2)}) collective-permute-start(f32[104,768]{1,0:T(8,128)S(1)} %get-tuple-element.329), channel_id=1, source_target_pairs={{0,16},{4,20},{8,24},{12,28},{16,0},{20,4},{24,8},{28,12},{1,17},{... | collective-permute-start | bytes 958472 | tf_op jit(solution)/shard_map/ppermute | solution.py:506
  281.3 24.7 %collective-permute-start.51 = (f32[104,768]{1,0:T(8,128)S(1)}, f32[104,768]{1,0:T(8,128)S(1)}, u32[]{:S(2)}, u32[]{:S(2)}) collective-permute-start(f32[104,768]{1,0:T(8,128)S(1)} %get-tuple-element.328), channel_id=1, source_target_pairs={{0,24},{4,28},{8,16},{12,20},{16,8},{20,12},{24,0},{28,4},{1,25},{... | collective-permute-start | bytes 958472 | tf_op jit(solution)/shard_map/ppermute | solution.py:506
  306.1 17.4 %collective-permute-start.52 = (f32[104,768]{1,0:T(8,128)S(1)}, f32[104,768]{1,0:T(8,128)S(1)}, u32[]{:S(2)}, u32[]{:S(2)}) collective-permute-start(f32[104,768]{1,0:T(8,128)S(1)} %add_add_fusion.rest_0_), channel_id=1, source_target_pairs={{0,8},{4,12},{8,0},{12,4},{16,24},{20,28},{24,16},{28,20},{1,9},{5... | collective-permute-start | bytes 958472 | tf_op jit(solution)/shard_map/ppermute | solution.py:506
  306.9 22.7 %collective-permute-start.53 = (f32[104,768]{1,0:T(8,128)S(1)}, f32[104,768]{1,0:T(8,128)S(1)}, u32[]{:S(2)}, u32[]{:S(2)}) collective-permute-start(f32[104,768]{1,0:T(8,128)S(1)} %add_add_fusion.rest_0_), channel_id=1, source_target_pairs={{0,16},{4,20},{8,24},{12,28},{16,0},{20,4},{24,8},{28,12},{1,17},{... | collective-permute-start | bytes 958472 | tf_op jit(solution)/shard_map/ppermute | solution.py:506
  308.7 20.9 %collective-permute-start.54 = (f32[104,768]{1,0:T(8,128)S(1)}, f32[104,768]{1,0:T(8,128)S(1)}, u32[]{:S(2)}, u32[]{:S(2)}) collective-permute-start(f32[104,768]{1,0:T(8,128)S(1)} %add_add_fusion.rest_0_), channel_id=1, source_target_pairs={{0,24},{4,28},{8,16},{12,20},{16,8},{20,12},{24,0},{28,4},{1,25},{... | collective-permute-start | bytes 958472 | tf_op jit(solution)/shard_map/ppermute | solution.py:506
  (85 other events, 784.4 us)
Sparse Core Ops, SparseCore 0:
  220.4 109.2 all-reduce.4

commit v6 on v5

--- a/solution.py
+++ b/solution.py
@@ -197,7 +197,7 @@
         in_specs=in_specs,
         out_specs=out_specs,
         out_shape=out_shape,
-        compiler_params=params(),
+        compiler_params=params((61 if own else 26) * 1024 * 1024),
         cost_estimate=cost(count),
     )(qkv, context, logs, scol, srow, da, weight)
 
@@ -559,11 +559,12 @@
             total = total + swap(total, mask, self.size)
             mask *= 2
         self.got = [total] + [swap(total, 2 * m, self.size) for m in (1, 2, 3)]
-        return self.got
+        self.other = [swap(total, 1, self.size)]
+        return self.got + self.other
 
     def share(self, *done):
         self.got = list(after(self.got, *done))
-        self.other = [swap(part, 1, self.size) for part in self.got]
+        self.other += [swap(part, 1, self.size) for part in self.got[1:]]
         return self.other
 
     def pieces(self):

time: 353 us -> 349 us (0.989)
  local copies, waits for them, and re-layouts: 41.4 us -> 35.6 us
    unnamed x151 -> x157, local copies, waits for them, and re-layouts: 38.4 us -> 32.6 us
  transfers between devices with their start and end apart: 60 -> 60, of which waited for: 16 -> 14; matrix products, arithmetic and copies ran while one was open for 2% -> 3% of each run, Pallas kernels for 51% -> 51%
where the time goes in v6:
time: 349 us; the launch traced here: 344 us
  Pallas kernels  215 us (62%)
  starting transfers between devices  45.9 us (13%)
  local copies, waits for them, and re-layouts  35.6 us (10%)
  waiting for transfers between devices  23 us (7%)
  between operations  15.7 us (4%)
  matrix products  5.79 us (2%)
    pallas_call x4, Pallas kernels, call_feed_forward(): pl.pallas_call(functools.partial(feed_forward, remote), grid=(count // bl...  56.2 us
    pallas_call x4, Pallas kernels, call_attend_backward(): pl.pallas_call(functools.partial(attend_backward, width, own), grid=(seqs...  47.9 us
    pallas_call x4, Pallas kernels, call_attend_forward(): pl.pallas_call(functools.partial(attend_forward, remote, width), grid=(se...  42.1 us
    ppermute x53, starting transfers between devices, swap(): return lax.ppermute(value, 'dp', [(i, i ^ mask) for i in range(size)])  33.5 us
    unnamed x157, local copies, waits for them, and re-layouts  32.6 us
    pallas_call x1, Pallas kernels, call_middle_rest(): pl.pallas_call(functools.partial(middle_rest, groups), grid=(count // blo...  25.1 us
    pallas_call x1, Pallas kernels, call_middle_own(): pl.pallas_call(middle_own, grid=(count // block,), in_specs=[rows(block,...  23.5 us
    ppermute x53, waiting for transfers between devices, swap(): return lax.ppermute(value, 'dp', [(i, i ^ mask) for i in range(size)])  14.6 us
  transfers between devices with their start and end apart: 60, of which 14 were waited for; matrix products, arithmetic and copies ran while one was open for 3% of the time, Pallas kernels for 51%

profile of v6, /device:TPU:0, one launch (start us, length us, event | category | flops | bytes accessed | tf_op | source)
XLA Modules:
  0.0 344.0 jit_solution(17700241996430660550)
XLA Ops:
  8.8 5.1 %collective-permute-start = (f32[104,768]{1,0:T(8,128)S(1)}, f32[104,768]{1,0:T(8,128)S(1)}, u32[]{:S(2)}, u32[]{:S(2)}) collective-permute-start(f32[104,768]{1,0:T(8,128)S(1)} %select_maximum_fusion.1), channel_id=1, source_target_pairs={{1,0},{2,1},{3,2},{0,3},{5,4},{6,5},{7,6},{4,7},{9,8},{10,9},{11,1... | collective-permute-start | bytes 958472 | tf_op jit(solution)/shard_map/ppermute | solution.py:510
  13.9 1.6 copy.43
  15.6 1.4 copy.47.scol_ref
  18.0 2.8 collective-permute-done.rest_1_
  20.7 1.5 collective-permute-start.3
  22.2 1.5 collective-permute-start.4
  24.7 4.4 %collective-permute-start.1 = (f32[104,768]{1,0:T(8,128)S(1)}, f32[104,768]{1,0:T(8,128)S(1)}, u32[]{:S(2)}, u32[]{:S(2)}) collective-permute-start(f32[104,768]{1,0:T(8,128)S(1)} %select_maximum_fusion.1), channel_id=1, source_target_pairs={{2,0},{3,1},{0,2},{1,3},{6,4},{7,5},{4,6},{5,7},{10,8},{11,9},{8,1... | collective-permute-start | bytes 958472 | tf_op jit(solution)/shard_map/ppermute | solution.py:510
  30.3 1.9 copy-done.10
  32.2 9.9 %shard_map.305 = (bf16[2048,576]{1,0:T(8,128)(2,1)S(1)}, bf16[2048,192]{1,0:T(8,128)(2,1)S(1)}, f32[4,8,512]{2,1,0:T(8,128)S(1)}) custom-call(bf16[2048,768]{1,0:T(8,128)(2,1)S(1)} %copy-done.10, s32[2048,1]{1,0:T(8,128)S(1)} %copy-done.3, s32[4,1,512]{2,1,0:T(1,128)S(1)} %bitcast.27, f32[1,576]{1,0:T(1,128)S(1)} %reshape.61.rest_0_, ...), custom_call_target="tpu_custom_call" | custom-call | flops 15360000000 | bytes 16777216 | tf_op jit(solution)/shard_map/pallas_call | solution.py:164
  43.1 1.5 copy-done.36
  45.7 2.3 collective-permute-done.1.rest_1_
  48.0 1.6 collective-permute-start.10
  49.6 1.5 collective-permute-start.11
  51.6 10.2 %shard_map.306 = (bf16[2048,576]{1,0:T(8,128)(2,1)S(1)}, bf16[2048,192]{1,0:T(8,128)(2,1)S(1)}, f32[4,8,512]{2,1,0:T(8,128)S(1)}, bf16[768,768]{1,0:T(8,128)(2,1)S(1)}) custom-call(bf16[2048,768]{1,0:T(8,128)(2,1)S(1)} %copy-done.10, s32[2048,1]{1,0:T(8,128)S(1)} %copy-done.3, s32[4,1,512]{2,1,0:T(1,128)S(1)} %bitcast.28, ...), custom_call_target="tpu_custom_call" | custom-call | flops 15360000000 | bytes 16777216 | tf_op jit(solution)/shard_map/pallas_call | solution.py:164
  62.9 1.5 copy-done.30
  66.5 2.2 collective-permute-start.22
  68.9 1.6 collective-permute-start.19
  70.4 1.5 collective-permute-start.20
  72.4 10.2 %shard_map.307 = (bf16[2048,576]{1,0:T(8,128)(2,1)S(1)}, bf16[2048,192]{1,0:T(8,128)(2,1)S(1)}, f32[4,8,512]{2,1,0:T(8,128)S(1)}, bf16[768,768]{1,0:T(8,128)(2,1)S(1)}) custom-call(bf16[2048,768]{1,0:T(8,128)(2,1)S(1)} %copy-done.10, s32[2048,1]{1,0:T(8,128)S(1)} %copy-done.3, s32[4,1,512]{2,1,0:T(1,128)S(1)} %bitcast.29, ...), custom_call_target="tpu_custom_call" | custom-call | flops 15360000000 | bytes 16777216 | tf_op jit(solution)/shard_map/pallas_call | solution.py:164
  83.7 1.5 copy-done.32
  92.8 1.9 copy-done.11
  94.7 11.8 %shard_map.308 = (bf16[2048,576]{1,0:T(8,128)(2,1)S(1)}, bf16[2048,192]{1,0:T(8,128)(2,1)S(1)}, f32[4,8,512]{2,1,0:T(8,128)S(1)}, bf16[768,768]{1,0:T(8,128)(2,1)S(1)}) custom-call(bf16[2048,768]{1,0:T(8,128)(2,1)S(1)} %copy-done.11, s32[2048,1]{1,0:T(8,128)S(1)} %copy-done.4, s32[4,1,512]{2,1,0:T(1,128)S(1)} %bitcast.30, ...), custom_call_target="tpu_custom_call" | custom-call | flops 15360000000 | bytes 16777216 | tf_op jit(solution)/shard_map/pallas_call | solution.py:164
  106.5 1.5 copy-done.34
  109.4 5.7 %shard_map.309 = (f32[2048,768]{1,0:T(8,128)S(1)}, bf16[2048,768]{1,0:T(8,128)(2,1)S(1)}) custom-call(bf16[2048,768]{1,0:T(8,128)(2,1)S(1)} %copy-done.12, f32[8,768]{1,0:T(8,128)S(1)} %stack.29.vec_ref, bf16[2048,192]{1,0:T(8,128)(2,1)S(1)} %copy-done.15, bf16[2048,192]{1,0:T(8,128)(2,1)S(1)} %copy-done.38, ...), custom_call_target="tpu_custom_call" | custom-call | flops 15360000000 | bytes 16777216 | tf_op jit(solution)/shard_map/pallas_call | solution.py:335
  115.2 2.6 copy-done.18
  117.8 3.4 collective-permute-done.29.rest_2_
  123.3 11.1 %shard_map.310 = (bf16[2048,768]{1,0:T(8,128)(2,1)S(1)}, f32[2048,768]{1,0:T(8,128)}, bf16[2048,768]{1,0:T(8,128)(2,1)S(1)}) custom-call(bf16[2048,768]{1,0:T(8,128)(2,1)S(1)} %get-tuple-element.227.x_ref.n1_ref, f32[1,768]{1,0:T(1,128)S(1)} %reshape.62.rest_0_, bf16[768,768]{1,0:T(8,128)(2,1)S(1)} %bitcast.23, bf16[768,768]{1,0:T(8,128)(2,1)S(1)} %copy-done.7), custom_call_target="tpu_custom_call" | custom-call | flops 15360000000 | bytes 16777216 | tf_op jit(solution)/shard_map/pallas_call | solution.py:302
  134.4 1.7 copy-done.20
  136.1 1.6 copy-done.21
  141.9 15.1 %shard_map.311 = (bf16[2048,768]{1,0:T(8,128)(2,1)}, f32[2048,768]{1,0:T(8,128)}, bf16[768,768]{1,0:T(8,128)(2,1)}, bf16[768,768]{1,0:T(8,128)(2,1)}) custom-call(bf16[2048,768]{1,0:T(8,128)(2,1)} %copy-done.19, f32[2048,768]{1,0:T(8,128)} %get-tuple-element.228.rest_0_, s32[1]{0:T(128)} %bitcast.2.rest_0_.rest_1_.place_ref, ...), custom_call_target="tpu_custom_call", output_to_operand_aliasing={{1}: (1, {})} | custom-call | flops 15360000000 | bytes 16777216 | tf_op jit(solution)/shard_map/pallas_call | solution.py:302
  160.5 15.0 %shard_map.312 = (bf16[2048,768]{1,0:T(8,128)(2,1)}, f32[2048,768]{1,0:T(8,128)}, bf16[768,768]{1,0:T(8,128)(2,1)}, bf16[768,768]{1,0:T(8,128)(2,1)}) custom-call(bf16[2048,768]{1,0:T(8,128)(2,1)} %copy-done.19, f32[2048,768]{1,0:T(8,128)} %get-tuple-element.244.rest_0_, s32[1]{0:T(128)} %bitcast.2.rest_0_.rest_1_.place_ref, ...), custom_call_target="tpu_custom_call", output_to_operand_aliasing={{1}: (1, {})} | custom-call | flops 15360000000 | bytes 16777216 | tf_op jit(solution)/shard_map/pallas_call | solution.py:302
  176.1 1.5 collective-permute-done.47.rest_9_
  178.6 15.0 %shard_map.313 = (bf16[2048,768]{1,0:T(8,128)(2,1)}, f32[2048,768]{1,0:T(8,128)}, bf16[768,768]{1,0:T(8,128)(2,1)}, bf16[768,768]{1,0:T(8,128)(2,1)}) custom-call(bf16[2048,768]{1,0:T(8,128)(2,1)} %copy-done.19, f32[2048,768]{1,0:T(8,128)} %get-tuple-element.259.rest_0_, s32[1]{0:T(128)} %bitcast.2.rest_0_.rest_1_.place_ref, ...), custom_call_target="tpu_custom_call", output_to_operand_aliasing={{1}: (1, {})} | custom-call | flops 15360000000 | bytes 16777216 | tf_op jit(solution)/shard_map/pallas_call | solution.py:302
  193.6 23.5 %shard_map.314 = (bf16[2048,768]{1,0:T(8,128)(2,1)}, bf16[2048,768]{1,0:T(8,128)(2,1)}, f32[2048,768]{1,0:T(8,128)}, f32[8,768]{1,0:T(8,128)}, f32[768,768]{1,0:T(8,128)}, /*index=5*/f32[768,768]{1,0:T(8,128)}) custom-call(f32[2048,768]{1,0:T(8,128)} %copy-done.18, f32[2048,768]{1,0:T(8,128)} %get-tuple-element.273.m_ref, ...), custom_call_target="tpu_custom_call", output_to_operand_aliasing={{2}: (1, {})} | custom-call | flops 15360000000 | bytes 16777216 | tf_op jit(solution)/shard_map/pallas_call | solution.py:425
  217.1 25.1 %shard_map.315 = (f32[2048,768]{1,0:T(8,128)}, bf16[2048,768]{1,0:T(8,128)(2,1)}, f32[8,768]{1,0:T(8,128)}) custom-call(f32[2048,768]{1,0:T(8,128)} %copy-done.18, f32[2048,768]{1,0:T(8,128)} %get-tuple-element.282.dn1_ref, bf16[2048,768]{1,0:T(8,128)(2,1)} %get-tuple-element.279.dm_ref, f32[8,768]{1,0:T(8,128)} %copy-done.6, ...), custom_call_target="tpu_custom_call", output_to_operand_aliasing={{0}: (1, {})} | custom-call | flops 15360000000 | bytes 16777216 | tf_op jit(solution)/shard_map/pallas_call | solution.py:450
  242.2 14.4 %shard_map.316 = (bf16[2048,576]{1,0:T(8,128)(2,1)}, f32[8,768]{1,0:T(8,128)}) custom-call(bf16[2048,576]{1,0:T(8,128)(2,1)} %copy-done.36, bf16[2048,192]{1,0:T(8,128)(2,1)} %copy-done.14, f32[4,8,512]{2,1,0:T(8,128)} %copy-done.45, s32[2048,1]{1,0:T(8,128)} %copy.47.scol_ref, s32[4,1,512]{2,1,0:T(1,128)} %bitcast.25, ...), custom_call_target="tpu_custom_call" | custom-call | flops 15360000000 | bytes 16777216 | tf_op jit(solution)/shard_map/pallas_call | solution.py:194
  256.6 5.0 %convolution_dynamic-update-slice_fusion = f32[832,768]{1,0:T(8,128)S(1)} fusion(bf16[2048,576]{1,0:T(8,128)(2,1)} %get-tuple-element.297.rest_0_, bf16[2048,768]{1,0:T(8,128)(2,1)} %x_ref.7), kind=kOutput, calls=%fused_computation | convolution fusion | flops 1811939328 | bytes 7274496 | tf_op jit(solution)/shard_map/dot_general | solution.py:470
  264.5 11.2 %shard_map.317.rest_1_ = bf16[2048,576]{1,0:T(8,128)(2,1)S(1)} custom-call(bf16[2048,576]{1,0:T(8,128)(2,1)S(1)} %copy-done.31, bf16[2048,192]{1,0:T(8,128)(2,1)S(1)} %copy-done.39, f32[4,8,512]{2,1,0:T(8,128)S(1)} %get-tuple-element.185.l_ref, s32[2048,1]{1,0:T(8,128)S(1)} %copy-done.5, s32[4,1,512]{2,1,0:T(1,128)S(1)} %bitcast.31, ...), custom_call_target="tpu_custom_call" | custom-call | flops 15360000000 | bytes 16777216 | tf_op jit(solution)/shard_map/pallas_call | solution.py:194
  276.0 1.3 collective-permute-start.49
  278.1 1.5 collective-permute-start.51
  279.6 11.2 %shard_map.318.rest_2_ = bf16[2048,576]{1,0:T(8,128)(2,1)S(1)} custom-call(bf16[2048,576]{1,0:T(8,128)(2,1)S(1)} %copy-done.33, bf16[2048,192]{1,0:T(8,128)(2,1)S(1)} %copy-done.42, f32[4,8,512]{2,1,0:T(8,128)S(1)} %get-tuple-element.199.l_ref, s32[2048,1]{1,0:T(8,128)S(1)} %copy-done.5, s32[4,1,512]{2,1,0:T(1,128)S(1)} %bitcast.32, ...), custom_call_target="tpu_custom_call" | custom-call | flops 15360000000 | bytes 16777216 | tf_op jit(solution)/shard_map/pallas_call | solution.py:194
  290.9 11.2 %shard_map.319.rest_3_ = bf16[2048,576]{1,0:T(8,128)(2,1)S(1)} custom-call(bf16[2048,576]{1,0:T(8,128)(2,1)S(1)} %copy-done.35, bf16[2048,192]{1,0:T(8,128)(2,1)S(1)} %copy-done.44, f32[4,8,512]{2,1,0:T(8,128)S(1)} %get-tuple-element.212.l_ref, s32[2048,1]{1,0:T(8,128)S(1)} %copy-done.5, s32[4,1,512]{2,1,0:T(1,128)S(1)} %bitcast.33, ...), custom_call_target="tpu_custom_call" | custom-call | flops 15360000000 | bytes 16777216 | tf_op jit(solution)/shard_map/pallas_call | solution.py:194
  302.1 1.4 collective-permute-start.52
  305.7 13.4 %shard_map.320 = f32[2048,768]{1,0:T(8,128)} custom-call(f32[2048,768]{1,0:T(8,128)} %get-tuple-element.305.dh1_ref, bf16[2048,576]{1,0:T(8,128)(2,1)S(1)} %copy-done.17, bf16[2048,576]{1,0:T(8,128)(2,1)S(1)} %shard_map.317.rest_1_, bf16[2048,576]{1,0:T(8,128)(2,1)S(1)} %shard_map.318.rest_2_, ...), custom_call_target="tpu_custom_call", output_to_operand_aliasing={{}: (0, {})} | custom-call | flops 15360000000 | bytes 16777216 | tf_op jit(solution)/shard_map/pallas_call | solution.py:218
  319.1 7.4 %collective-permute-done.53.rest_2_ = f32[104,768]{1,0:T(8,128)S(1)} collective-permute-done((f32[104,768]{1,0:T(8,128)S(1)}, f32[104,768]{1,0:T(8,128)S(1)}, u32[]{:S(2)}, u32[]{:S(2)}) %collective-permute-start.53) | collective-permute-done | bytes 319520 | tf_op jit(solution)/shard_map/ppermute | solution.py:506
  329.1 1.6 shard_map.321
  331.9 3.4 copy.65
  335.3 1.4 copy.66
  (275 shorter events, 42.2 us)
Async XLA Ops:
  7.2 324.7 %all-reduce.5.cloned.1.call-start = ((), (), s32[]{:S(2)}) async-start(), calls=%async_computation | async-start | bytes 9437184 | tf_op jit(solution)/shard_map/psum | solution.py:703
  8.8 11.9 %collective-permute-start = (f32[104,768]{1,0:T(8,128)S(1)}, f32[104,768]{1,0:T(8,128)S(1)}, u32[]{:S(2)}, u32[]{:S(2)}) collective-permute-start(f32[104,768]{1,0:T(8,128)S(1)} %select_maximum_fusion.1), channel_id=1, source_target_pairs={{1,0},{2,1},{3,2},{0,3},{5,4},{6,5},{7,6},{4,7},{9,8},{10,9},{11,1... | collective-permute-start | bytes 958472 | tf_op jit(solution)/shard_map/ppermute | solution.py:510
  20.7 23.9 %collective-permute-start.3 = (f32[104,768]{1,0:T(8,128)S(1)}, f32[104,768]{1,0:T(8,128)S(1)}, u32[]{:S(2)}, u32[]{:S(2)}) collective-permute-start(f32[104,768]{1,0:T(8,128)S(1)} %collective-permute-done.rest_1_), channel_id=1, source_target_pairs={{0,8},{4,12},{8,0},{12,4},{16,24},{20,28},{24,16},{28,20},{1,9},{5... | collective-permute-start | bytes 958472 | tf_op jit(solution)/shard_map/ppermute | solution.py:506
  22.2 22.4 %collective-permute-start.4 = (f32[104,768]{1,0:T(8,128)S(1)}, f32[104,768]{1,0:T(8,128)S(1)}, u32[]{:S(2)}, u32[]{:S(2)}) collective-permute-start(f32[104,768]{1,0:T(8,128)S(1)} %collective-permute-done.rest_1_), channel_id=1, source_target_pairs={{0,16},{4,20},{8,24},{12,28},{16,0},{20,4},{24,8},{28,12},{1,17},{... | collective-permute-start | bytes 958472 | tf_op jit(solution)/shard_map/ppermute | solution.py:506
  23.7 20.9 %collective-permute-start.5 = (f32[104,768]{1,0:T(8,128)S(1)}, f32[104,768]{1,0:T(8,128)S(1)}, u32[]{:S(2)}, u32[]{:S(2)}) collective-permute-start(f32[104,768]{1,0:T(8,128)S(1)} %collective-permute-done.rest_1_), channel_id=1, source_target_pairs={{0,24},{4,28},{8,16},{12,20},{16,8},{20,12},{24,0},{28,4},{1,25},{... | collective-permute-start | bytes 958472 | tf_op jit(solution)/shard_map/ppermute | solution.py:506
  24.2 20.4 %collective-permute-start.2 = (f32[104,768]{1,0:T(8,128)S(1)}, f32[104,768]{1,0:T(8,128)S(1)}, u32[]{:S(2)}, u32[]{:S(2)}) collective-permute-start(f32[104,768]{1,0:T(8,128)S(1)} %select_maximum_fusion.1), channel_id=1, source_target_pairs={{3,0},{0,1},{1,2},{2,3},{7,4},{4,5},{5,6},{6,7},{11,8},{8,9},{9,10... | collective-permute-start | bytes 958472 | tf_op jit(solution)/shard_map/ppermute | solution.py:510
  24.7 23.3 %collective-permute-start.1 = (f32[104,768]{1,0:T(8,128)S(1)}, f32[104,768]{1,0:T(8,128)S(1)}, u32[]{:S(2)}, u32[]{:S(2)}) collective-permute-start(f32[104,768]{1,0:T(8,128)S(1)} %select_maximum_fusion.1), channel_id=1, source_target_pairs={{2,0},{3,1},{0,2},{1,3},{6,4},{7,5},{4,6},{5,7},{10,8},{11,9},{8,1... | collective-permute-start | bytes 958472 | tf_op jit(solution)/shard_map/ppermute | solution.py:510
  44.6 3.4 collective-permute-start.9
  44.7 3.3 collective-permute-start.8
  45.2 2.8 collective-permute-start.7
  48.0 17.3 %collective-permute-start.10 = (f32[104,768]{1,0:T(8,128)S(1)}, f32[104,768]{1,0:T(8,128)S(1)}, u32[]{:S(2)}, u32[]{:S(2)}) collective-permute-start(f32[104,768]{1,0:T(8,128)S(1)} %collective-permute-done.2.rest_1_), channel_id=1, source_target_pairs={{0,8},{4,12},{8,0},{12,4},{16,24},{20,28},{24,16},{28,20},{1,9},{5... | collective-permute-start | bytes 958472 | tf_op jit(solution)/shard_map/ppermute | solution.py:506
  49.6 16.0 %collective-permute-start.11 = (f32[104,768]{1,0:T(8,128)S(1)}, f32[104,768]{1,0:T(8,128)S(1)}, u32[]{:S(2)}, u32[]{:S(2)}) collective-permute-start(f32[104,768]{1,0:T(8,128)S(1)} %collective-permute-done.2.rest_1_), channel_id=1, source_target_pairs={{0,16},{4,20},{8,24},{12,28},{16,0},{20,4},{24,8},{28,12},{1,17},{... | collective-permute-start | bytes 958472 | tf_op jit(solution)/shard_map/ppermute | solution.py:506
  51.1 14.5 %collective-permute-start.12 = (f32[104,768]{1,0:T(8,128)S(1)}, f32[104,768]{1,0:T(8,128)S(1)}, u32[]{:S(2)}, u32[]{:S(2)}) collective-permute-start(f32[104,768]{1,0:T(8,128)S(1)} %collective-permute-done.2.rest_1_), channel_id=1, source_target_pairs={{0,24},{4,28},{8,16},{12,20},{16,8},{20,12},{24,0},{28,4},{1,25},{... | collective-permute-start | bytes 958472 | tf_op jit(solution)/shard_map/ppermute | solution.py:506
  51.6 14.0 %collective-permute-start.13 = (f32[104,768]{1,0:T(8,128)S(1)}, f32[104,768]{1,0:T(8,128)S(1)}, u32[]{:S(2)}, u32[]{:S(2)}) collective-permute-start(f32[104,768]{1,0:T(8,128)S(1)} %collective-permute-done.2.rest_1_), channel_id=1, source_target_pairs={{0,4},{4,0},{8,12},{12,8},{16,20},{20,16},{24,28},{28,24},{1,5},{5... | collective-permute-start | bytes 958472 | tf_op jit(solution)/shard_map/ppermute | solution.py:506
  51.6 17.2 %collective-permute-start.17 = (f32[200,768]{1,0:T(8,128)S(1)}, f32[200,768]{1,0:T(8,128)S(1)}, u32[]{:S(2)}, u32[]{:S(2)}) collective-permute-start(f32[200,768]{1,0:T(8,128)S(1)} %select_maximum_fusion), channel_id=1, source_target_pairs={{1,0},{2,1},{3,2},{0,3},{5,4},{6,5},{7,6},{4,7},{9,8},{10,9},{11,1... | collective-permute-start | bytes 1843208 | tf_op jit(solution)/shard_map/ppermute | solution.py:510
  65.7 3.1 collective-permute-start.16
  66.5 19.7 %collective-permute-start.22 = (f32[200,768]{1,0:T(8,128)S(1)}, f32[200,768]{1,0:T(8,128)S(1)}, u32[]{:S(2)}, u32[]{:S(2)}) collective-permute-start(f32[200,768]{1,0:T(8,128)S(1)} %select_maximum_fusion), channel_id=1, source_target_pairs={{3,0},{0,1},{1,2},{2,3},{7,4},{4,5},{5,6},{6,7},{11,8},{8,9},{9,10... | collective-permute-start | bytes 1843208 | tf_op jit(solution)/shard_map/ppermute | solution.py:510
  68.8 17.4 %collective-permute-start.18 = (f32[104,768]{1,0:T(8,128)S(1)}, f32[104,768]{1,0:T(8,128)S(1)}, u32[]{:S(2)}, u32[]{:S(2)}) collective-permute-start(f32[104,768]{1,0:T(8,128)S(1)} %collective-permute-done.1.rest_1_), channel_id=1, source_target_pairs={{0,4},{4,0},{8,12},{12,8},{16,20},{20,16},{24,28},{28,24},{1,5},{5... | collective-permute-start | bytes 958472 | tf_op jit(solution)/shard_map/ppermute | solution.py:506
  68.9 17.3 %collective-permute-start.19 = (f32[104,768]{1,0:T(8,128)S(1)}, f32[104,768]{1,0:T(8,128)S(1)}, u32[]{:S(2)}, u32[]{:S(2)}) collective-permute-start(f32[104,768]{1,0:T(8,128)S(1)} %collective-permute-done.1.rest_1_), channel_id=1, source_target_pairs={{0,8},{4,12},{8,0},{12,4},{16,24},{20,28},{24,16},{28,20},{1,9},{5... | collective-permute-start | bytes 958472 | tf_op jit(solution)/shard_map/ppermute | solution.py:506
  70.4 16.6 %collective-permute-start.20 = (f32[104,768]{1,0:T(8,128)S(1)}, f32[104,768]{1,0:T(8,128)}, u32[]{:S(2)}, u32[]{:S(2)}) collective-permute-start(f32[104,768]{1,0:T(8,128)S(1)} %collective-permute-done.1.rest_1_), channel_id=1, source_target_pairs={{0,16},{4,20},{8,24},{12,28},{16,0},{20,4},{24,8},{28,12},{1,17},{... | collective-permute-start | bytes 958472 | tf_op jit(solution)/shard_map/ppermute | solution.py:506
  71.9 15.0 %collective-permute-start.21 = (f32[104,768]{1,0:T(8,128)S(1)}, f32[104,768]{1,0:T(8,128)}, u32[]{:S(2)}, u32[]{:S(2)}) collective-permute-start(f32[104,768]{1,0:T(8,128)S(1)} %collective-permute-done.1.rest_1_), channel_id=1, source_target_pairs={{0,24},{4,28},{8,16},{12,20},{16,8},{20,12},{24,0},{28,4},{1,25},{... | collective-permute-start | bytes 958472 | tf_op jit(solution)/shard_map/ppermute | solution.py:506
  87.0 3.2 collective-permute-start.25
  87.0 3.2 collective-permute-start.24
  87.7 20.3 %collective-permute-start.26 = (f32[200,768]{1,0:T(8,128)}, f32[200,768]{1,0:T(8,128)S(1)}, u32[]{:S(2)}, u32[]{:S(2)}) collective-permute-start(f32[200,768]{1,0:T(8,128)} %copy-done.62), channel_id=1, source_target_pairs={{0,8},{4,12},{8,0},{12,4},{16,24},{20,28},{24,16},{28,20},{1,9},{5... | collective-permute-start | bytes 1843208 | tf_op jit(solution)/shard_map/ppermute | solution.py:506
  89.0 19.0 %collective-permute-start.27 = (f32[200,768]{1,0:T(8,128)}, f32[200,768]{1,0:T(8,128)S(1)}, u32[]{:S(2)}, u32[]{:S(2)}) collective-permute-start(f32[200,768]{1,0:T(8,128)} %copy-done.62), channel_id=1, source_target_pairs={{0,16},{4,20},{8,24},{12,28},{16,0},{20,4},{24,8},{28,12},{1,17},{... | collective-permute-start | bytes 1843208 | tf_op jit(solution)/shard_map/ppermute | solution.py:506
  90.2 27.6 %collective-permute-start.30 = (f32[200,768]{1,0:T(8,128)}, f32[200,768]{1,0:T(8,128)}, u32[]{:S(2)}, u32[]{:S(2)}) collective-permute-start(f32[200,768]{1,0:T(8,128)} %copy-done.59), channel_id=1, source_target_pairs={{0,8},{4,12},{8,0},{12,4},{16,24},{20,28},{24,16},{28,20},{1,9},{5... | collective-permute-start | bytes 1843208 | tf_op jit(solution)/shard_map/ppermute | solution.py:506
  91.4 29.8 %collective-permute-start.29 = (f32[200,768]{1,0:T(8,128)}, f32[200,768]{1,0:T(8,128)}, u32[]{:S(2)}, u32[]{:S(2)}) collective-permute-start(f32[200,768]{1,0:T(8,128)} %copy-done.47), channel_id=1, source_target_pairs={{2,0},{3,1},{0,2},{1,3},{6,4},{7,5},{4,6},{5,7},{10,8},{11,9},{8,1... | collective-permute-start | bytes 1843208 | tf_op jit(solution)/shard_map/ppermute | solution.py:510
  91.6 16.4 %collective-permute-start.28 = (f32[200,768]{1,0:T(8,128)}, f32[200,768]{1,0:T(8,128)S(1)}, u32[]{:S(2)}, u32[]{:S(2)}) collective-permute-start(f32[200,768]{1,0:T(8,128)} %copy-done.62), channel_id=1, source_target_pairs={{0,4},{4,0},{8,12},{12,8},{16,20},{20,16},{24,28},{28,24},{1,5},{5... | collective-permute-start | bytes 1843208 | tf_op jit(solution)/shard_map/ppermute | solution.py:506
  108.0 30.0 %collective-permute-start.31 = (f32[200,768]{1,0:T(8,128)S(1)}, f32[200,768]{1,0:T(8,128)S(1)}, u32[]{:S(2)}, u32[]{:S(2)}) collective-permute-start(f32[200,768]{1,0:T(8,128)S(1)} %collective-permute-done.26.rest_4_), channel_id=1, source_target_pairs={{0,4},{4,0},{8,12},{12,8},{16,20},{20,16},{24,28},{28,24},{1,5},{5... | collective-permute-start | bytes 1843208 | tf_op jit(solution)/shard_map/ppermute | solution.py:506
  108.6 29.5 %collective-permute-start.32 = (f32[200,768]{1,0:T(8,128)S(1)}, f32[200,768]{1,0:T(8,128)S(1)}, u32[]{:S(2)}, u32[]{:S(2)}) collective-permute-start(f32[200,768]{1,0:T(8,128)S(1)} %collective-permute-done.26.rest_4_), channel_id=1, source_target_pairs={{0,16},{4,20},{8,24},{12,28},{16,0},{20,4},{24,8},{28,12},{1,17},{... | collective-permute-start | bytes 1843208 | tf_op jit(solution)/shard_map/ppermute | solution.py:506
  121.2 16.5 %collective-permute-start.35 = (f32[200,768]{1,0:T(8,128)S(1)}, f32[200,768]{1,0:T(8,128)S(1)}, u32[]{:S(2)}, u32[]{:S(2)}) collective-permute-start(f32[200,768]{1,0:T(8,128)S(1)} %copy-done.60), channel_id=1, source_target_pairs={{0,4},{4,0},{8,12},{12,8},{16,20},{20,16},{24,28},{28,24},{1,5},{5... | collective-permute-start | bytes 1843208 | tf_op jit(solution)/shard_map/ppermute | solution.py:506
  121.2 16.5 %collective-permute-start.34 = (f32[200,768]{1,0:T(8,128)}, f32[200,768]{1,0:T(8,128)S(1)}, u32[]{:S(2)}, u32[]{:S(2)}) collective-permute-start(f32[200,768]{1,0:T(8,128)} %collective-permute-done.29.rest_2_), channel_id=1, source_target_pairs={{0,8},{4,12},{8,0},{12,4},{16,24},{20,28},{24,16},{28,20},{1,9},{5... | collective-permute-start | bytes 1843208 | tf_op jit(solution)/shard_map/ppermute | solution.py:506
  122.0 16.1 %collective-permute-start.33 = (f32[200,768]{1,0:T(8,128)S(1)}, f32[200,768]{1,0:T(8,128)}, u32[]{:S(2)}, u32[]{:S(2)}) collective-permute-start(f32[200,768]{1,0:T(8,128)S(1)} %copy-done.60), channel_id=1, source_target_pairs={{0,16},{4,20},{8,24},{12,28},{16,0},{20,4},{24,8},{28,12},{1,17},{... | collective-permute-start | bytes 1843208 | tf_op jit(solution)/shard_map/ppermute | solution.py:506
  138.2 2.9 collective-permute-start.36
  138.7 18.4 %collective-permute-start.40 = (f32[200,768]{1,0:T(8,128)}, f32[200,768]{1,0:T(8,128)}, u32[]{:S(2)}, u32[]{:S(2)}) collective-permute-start(f32[200,768]{1,0:T(8,128)} %collective-permute-done.33.rest_6_), channel_id=1, source_target_pairs={{0,8},{4,12},{8,0},{12,4},{16,24},{20,28},{24,16},{28,20},{1,9},{5... | collective-permute-start | bytes 1843208 | tf_op jit(solution)/shard_map/ppermute | solution.py:506
  139.9 17.2 %collective-permute-start.39 = (f32[200,768]{1,0:T(8,128)}, f32[200,768]{1,0:T(8,128)S(1)}, u32[]{:S(2)}, u32[]{:S(2)}) collective-permute-start(f32[200,768]{1,0:T(8,128)} %collective-permute-done.29.rest_2_), channel_id=1, source_target_pairs={{0,16},{4,20},{8,24},{12,28},{16,0},{20,4},{24,8},{28,12},{1,17},{... | collective-permute-start | bytes 1843208 | tf_op jit(solution)/shard_map/ppermute | solution.py:506
  140.7 16.4 %collective-permute-start.38 = (f32[200,768]{1,0:T(8,128)}, f32[200,768]{1,0:T(8,128)S(1)}, u32[]{:S(2)}, u32[]{:S(2)}) collective-permute-start(f32[200,768]{1,0:T(8,128)} %collective-permute-done.30.rest_4_), channel_id=1, source_target_pairs={{0,4},{4,0},{8,12},{12,8},{16,20},{20,16},{24,28},{28,24},{1,5},{5... | collective-permute-start | bytes 1843208 | tf_op jit(solution)/shard_map/ppermute | solution.py:506
  158.3 17.1 %collective-permute-start.44 = (f32[200,768]{1,0:T(8,128)S(1)}, f32[200,768]{1,0:T(8,128)S(1)}, u32[]{:S(2)}, u32[]{:S(2)}) collective-permute-start(f32[200,768]{1,0:T(8,128)S(1)} %collective-permute-done.34.rest_4_), channel_id=1, source_target_pairs={{0,4},{4,0},{8,12},{12,8},{16,20},{20,16},{24,28},{28,24},{1,5},{5... | collective-permute-start | bytes 1843208 | tf_op jit(solution)/shard_map/ppermute | solution.py:506
  158.5 16.9 %collective-permute-start.45 = (f32[200,768]{1,0:T(8,128)S(1)}, f32[200,768]{1,0:T(8,128)S(1)}, u32[]{:S(2)}, u32[]{:S(2)}) collective-permute-start(f32[200,768]{1,0:T(8,128)S(1)} %collective-permute-done.34.rest_4_), channel_id=1, source_target_pairs={{0,16},{4,20},{8,24},{12,28},{16,0},{20,4},{24,8},{28,12},{1,17},{... | collective-permute-start | bytes 1843208 | tf_op jit(solution)/shard_map/ppermute | solution.py:506
  159.8 15.7 %collective-permute-start.43 = (f32[200,768]{1,0:T(8,128)}, f32[200,768]{1,0:T(8,128)}, u32[]{:S(2)}, u32[]{:S(2)}) collective-permute-start(f32[200,768]{1,0:T(8,128)} %collective-permute-done.29.rest_2_), channel_id=1, source_target_pairs={{0,4},{4,0},{8,12},{12,8},{16,20},{20,16},{24,28},{28,24},{1,5},{5... | collective-permute-start | bytes 1843208 | tf_op jit(solution)/shard_map/ppermute | solution.py:506
  262.6 13.1 %collective-permute-start.48 = (f32[416,768]{1,0:T(8,128)S(1)}, f32[416,768]{1,0:T(8,128)S(1)}, u32[]{:S(2)}, u32[]{:S(2)}) collective-permute-start(f32[416,768]{1,0:T(8,128)S(1)} %constant_dynamic-slice_fusion.4), channel_id=1, source_target_pairs={{0,4},{4,0},{8,12},{12,8},{16,20},{20,16},{24,28},{28,24},{1,5},{5... | collective-permute-start | bytes 3833864 | tf_op jit(solution)/shard_map/ppermute | solution.py:506
  276.0 26.0 %collective-permute-start.49 = (f32[104,768]{1,0:T(8,128)S(1)}, f32[104,768]{1,0:T(8,128)S(1)}, u32[]{:S(2)}, u32[]{:S(2)}) collective-permute-start(f32[104,768]{1,0:T(8,128)S(1)} %get-tuple-element.330), channel_id=1, source_target_pairs={{0,8},{4,12},{8,0},{12,4},{16,24},{20,28},{24,16},{28,20},{1,9},{5... | collective-permute-start | bytes 958472 | tf_op jit(solution)/shard_map/ppermute | solution.py:506
  277.4 24.7 %collective-permute-start.50 = (f32[104,768]{1,0:T(8,128)S(1)}, f32[104,768]{1,0:T(8,128)S(1)}, u32[]{:S(2)}, u32[]{:S(2)}) collective-permute-start(f32[104,768]{1,0:T(8,128)S(1)} %get-tuple-element.329), channel_id=1, source_target_pairs={{0,16},{4,20},{8,24},{12,28},{16,0},{20,4},{24,8},{28,12},{1,17},{... | collective-permute-start | bytes 958472 | tf_op jit(solution)/shard_map/ppermute | solution.py:506
  278.1 23.9 %collective-permute-start.51 = (f32[104,768]{1,0:T(8,128)S(1)}, f32[104,768]{1,0:T(8,128)S(1)}, u32[]{:S(2)}, u32[]{:S(2)}) collective-permute-start(f32[104,768]{1,0:T(8,128)S(1)} %get-tuple-element.328), channel_id=1, source_target_pairs={{0,24},{4,28},{8,16},{12,20},{16,8},{20,12},{24,0},{28,4},{1,25},{... | collective-permute-start | bytes 958472 | tf_op jit(solution)/shard_map/ppermute | solution.py:506
  302.1 17.0 %collective-permute-start.52 = (f32[104,768]{1,0:T(8,128)S(1)}, f32[104,768]{1,0:T(8,128)S(1)}, u32[]{:S(2)}, u32[]{:S(2)}) collective-permute-start(f32[104,768]{1,0:T(8,128)S(1)} %add_add_fusion.rest_0_), channel_id=1, source_target_pairs={{0,8},{4,12},{8,0},{12,4},{16,24},{20,28},{24,16},{28,20},{1,9},{5... | collective-permute-start | bytes 958472 | tf_op jit(solution)/shard_map/ppermute | solution.py:506
  303.5 23.0 %collective-permute-start.53 = (f32[104,768]{1,0:T(8,128)S(1)}, f32[104,768]{1,0:T(8,128)S(1)}, u32[]{:S(2)}, u32[]{:S(2)}) collective-permute-start(f32[104,768]{1,0:T(8,128)S(1)} %add_add_fusion.rest_0_), channel_id=1, source_target_pairs={{0,16},{4,20},{8,24},{12,28},{16,0},{20,4},{24,8},{28,12},{1,17},{... | collective-permute-start | bytes 958472 | tf_op jit(solution)/shard_map/ppermute | solution.py:506
  304.7 21.9 %collective-permute-start.54 = (f32[104,768]{1,0:T(8,128)S(1)}, f32[104,768]{1,0:T(8,128)S(1)}, u32[]{:S(2)}, u32[]{:S(2)}) collective-permute-start(f32[104,768]{1,0:T(8,128)S(1)} %add_add_fusion.rest_0_), channel_id=1, source_target_pairs={{0,24},{4,28},{8,16},{12,20},{16,8},{20,12},{24,0},{28,4},{1,25},{... | collective-permute-start | bytes 958472 | tf_op jit(solution)/shard_map/ppermute | solution.py:506
  305.7 21.4 %collective-permute-start.55 = (f32[104,768]{1,0:T(8,128)S(1)}, f32[104,768]{1,0:T(8,128)S(1)}, u32[]{:S(2)}, u32[]{:S(2)}) collective-permute-start(f32[104,768]{1,0:T(8,128)S(1)} %add_add_fusion.rest_0_), channel_id=1, source_target_pairs={{0,4},{4,0},{8,12},{12,8},{16,20},{20,16},{24,28},{28,24},{1,5},{5... | collective-permute-start | bytes 958472 | tf_op jit(solution)/shard_map/ppermute | solution.py:506
  (88 other events, 856.4 us)
Sparse Core Ops, SparseCore 0:
  217.2 109.5 all-reduce.4
